TPU v7x, 1024 devices: a whole 8x8x8 slice. The times are simulated.
1024 devices in a mesh: row: 16 (over x, core), col: 16 (over y, z_lo), depth: 4 (over z_hi).
Axes of the slice: x: 8, y: 8, z: 8 (z_hi: 4, z_lo: 2; z = z_hi * 2 + z_lo), core: 2. Of those that a mesh axis runs over, the one named last changes fastest.
Arguments:
- density: bfloat16 [8192, 8192], P('row', 'col'), may hold values from -1.5 to 1.5
- pattern: int32 [128, 16], P('row'), may hold values from 0 to 127, all different within a row
- orbital_counts: int32 [16, 128], P('row'), may hold values from 1 to 9, 512 in all within a row
- branch_flag: int32 [128], P('row'), may hold values from 0 to 1
Outputs:
- updated: bfloat16 [8192, 8192], P('row', ('col', 'depth'))
- populations: float32 [2048], P('row')
Inputs may be any that keep to these rules, and one draw needn't show every extreme that they name: `pattern`: each row names distinct block columns. `orbital_counts`: each row sums to 512.
All inputs are finite; a program needn't handle non-finite values.
Results may differ from a plain program's by a relative error of at most 0.007.
Values may be sent and summed in bfloat16 or wider, within the bound.
No kernel may reach another device: no remote copies, remote signals or barrier semaphores. Data moves between devices by JAX's collectives and lax.ppermute only.
A program may use at most 32 MiB of HBM per device.

v0:
```python
import jax
import jax.numpy as jnp
from jax import lax
from jax.sharding import PartitionSpec as P

BLOCK = 64


def local_keep(pattern, row_index, col_global):
    block_rows = pattern.shape[0]
    col_blocks = col_global // BLOCK
    block_hit = jnp.any(pattern[:, :, None] == col_blocks[None, None, :], axis=1)
    row_blocks = row_index * block_rows + jnp.arange(block_rows, dtype=jnp.int32)
    block_hit = block_hit | (row_blocks[:, None] == col_blocks[None, :])
    count_cols = col_global.shape[0]
    spread = jnp.broadcast_to(block_hit[:, None, :], (block_rows, BLOCK, count_cols))
    return spread.reshape(block_rows * BLOCK, count_cols)


def per_device(density, pattern, orbital_counts, branch_flag):
    tile_size = density.shape[0]
    strip_width = tile_size // lax.axis_size("depth")
    row_index = lax.axis_index("row")
    col_index = lax.axis_index("col")
    depth_index = lax.axis_index("depth")
    col_global = col_index * tile_size + jnp.arange(tile_size, dtype=jnp.int32)
    mask_in = local_keep(pattern, row_index, col_global)
    masked = jnp.where(mask_in, density, jnp.zeros_like(density))
    a_slice = lax.dynamic_slice_in_dim(masked, depth_index * strip_width, strip_width, 1)
    b_slice = lax.dynamic_slice_in_dim(masked, depth_index * strip_width, strip_width, 0)
    b_full = lax.all_gather(b_slice, "row", axis=0, tiled=True)
    partial_sum = jnp.dot(
        lax.all_gather(a_slice, "col", axis=1, tiled=True),
        b_full,
        preferred_element_type=jnp.float32,
    )
    total_sum = lax.psum(partial_sum, "depth")
    squared = lax.dynamic_slice_in_dim(total_sum, depth_index * strip_width, strip_width, 1)
    own_share = a_slice.astype(jnp.float32)
    row_flags = jnp.repeat(branch_flag, BLOCK)
    chosen = jnp.where(row_flags[:, None] == 1, squared, 2.0 * own_share - squared)
    strip_global = (
        col_index * tile_size + depth_index * strip_width + jnp.arange(strip_width, dtype=jnp.int32)
    )
    mask_out = local_keep(pattern, row_index, strip_global)
    updated = jnp.where(mask_out, chosen, jnp.zeros_like(chosen)).astype(jnp.bfloat16)
    row_global = row_index * tile_size + jnp.arange(tile_size, dtype=jnp.int32)
    on_diagonal = row_global[:, None] == strip_global[None, :]
    diagonal_vals = jnp.sum(jnp.where(on_diagonal, updated.astype(jnp.float32), 0.0), axis=1)
    atom_ends = jnp.cumsum(orbital_counts[0])
    atom_starts = atom_ends - orbital_counts[0]
    positions = jnp.arange(tile_size, dtype=jnp.int32)
    membership = (
        (positions[None, :] >= atom_starts[:, None]) & (positions[None, :] < atom_ends[:, None])
    ).astype(jnp.float32)
    local_terms = jnp.dot(membership, diagonal_vals, precision=lax.Precision.HIGHEST)
    populations = lax.psum(local_terms, ("col", "depth"))
    return (updated, populations)


def solution(mesh):
    in_specs = (P("row", "col"), P("row", None), P("row", None), P("row"))
    out_specs = (P("row", ("col", "depth")), P("row"))
    return jax.shard_map(
        per_device, mesh=mesh, in_specs=in_specs, out_specs=out_specs, check_vma=False
    )
```

profile of v0, /device:TPU:6, one launch (start us, length us, event | category | flops | bytes accessed | tf_op | source)
XLA Modules:
  0.0 393.0 jit_solution(12419604504548955187)
XLA Ops:
  7.2 0.0 all-gather.5.cloned.1.call-start
  7.2 0.8 compare_reduce_fusion
  8.1 0.1 compare_or_fusion
  8.1 1.1 bitcast_select_fusion
  9.2 0.7 constant_dynamic-slice_fusion
  9.9 0.0 all-gather.5.cloned.1.call-update
  9.9 0.0 all-gather.3.cloned.1.call-start
  10.0 0.7 constant_dynamic-slice_fusion.1
  10.7 0.0 all-gather.3.cloned.1.call-update
  10.7 0.0 copy-start.2
  10.7 0.0 copy-start.1
  10.7 0.0 copy-start
  10.7 0.0 all-reduce.2.cloned.1.call-start
  10.8 55.5 %all-gather.5.cloned.1.call-done = bf16[2048,512]{1,0:T(8,128)(2,1)} async-done(((bf16[128,512]{1,0:T(8,128)(2,1)}), bf16[2048,512]{1,0:T(8,128)(2,1)}) %all-gather.5.cloned.1.call-update) | async-done | bytes 2097168 | tf_op jit(solution)/shard_map/all_gather | solution.py:31
  66.2 90.6 %all-gather.3.cloned.1.call-done = bf16[512,2048]{1,0:T(8,128)(2,1)} async-done(((bf16[512,128]{1,0:T(8,128)(2,1)}), bf16[512,2048]{1,0:T(8,128)(2,1)}) %all-gather.3.cloned.1.call-update) | async-done | bytes 2097168 | tf_op jit(solution)/shard_map/all_gather | solution.py:33
  156.8 4.4 %fusion.10 = f32[512,512]{1,0:T(8,128)} fusion(bf16[512,2048]{1,0:T(8,128)(2,1)} %all-gather.3.cloned.1.call-done, bf16[2048,512]{1,0:T(8,128)(2,1)} %all-gather.5.cloned.1.call-done), kind=kOutput, calls=%fused_computation.35 | convolution fusion | flops 1073741824 | bytes 5242880 | tf_op jit(solution)/shard_map/dot_general | solution.py:32
  161.2 0.0 all-reduce.2.cloned.1.call-update
  161.3 0.0 copy-done.2
  161.3 0.1 broadcast_in_dim.20
  161.4 0.1 eq.98
  161.5 0.0 copy-done.1
  161.5 0.1 copy.8
  161.6 0.2 reduce-window.7
  161.7 0.1 reduce
  161.9 0.0 copy-done
  161.9 0.1 compare_reduce_fusion.1
  162.0 0.1 compare_or_fusion.1
  162.1 80.2 %all-reduce.2.cloned.1.call-done = f32[512,512]{1,0:T(8,128)} async-done(((f32[512,512]{1,0:T(8,128)}), f32[512,512]{1,0:T(8,128)}) %all-reduce.2.cloned.1.call-update) | async-done | bytes 1048592 | tf_op jit(solution)/shard_map/psum | solution.py:37
  242.3 1.8 select_reduce_fusion
  244.1 0.3 convolution_bitcast_fusion
  244.3 142.1 %psum.15 = f32[128]{0:T(128)} all-reduce(f32[128]{0:T(128)S(1)} %convolution_bitcast_fusion), channel_id=1, replica_groups=mesh['row'=16,'col'=16,'depth'=4] {'col','depth'}, use_global_device_ids=true, to_apply=%region_5.6 | all-reduce | flops 128 | bytes 1024 | tf_op jit(solution)/shard_map/psum | solution.py:57
  (6 shorter events, 0.0 us)
Async XLA Ops:
  7.2 59.1 %all-gather.5.cloned.1.call-start = ((), (), s32[]{:S(2)}) async-start(), calls=%async_computation.1 | async-start | bytes 2228224 | tf_op jit(solution)/shard_map/all_gather | solution.py:31
  9.9 146.9 %all-gather.3.cloned.1.call-start = ((), (), s32[]{:S(2)}) async-start(), calls=%async_computation | async-start | bytes 2228224 | tf_op jit(solution)/shard_map/all_gather | solution.py:33
  10.7 150.6 %copy-start.2 = (s32[8]{0:T(128)S(1)}, s32[8]{0:T(128)}, u32[]{:S(2)}) copy-start(s32[8]{0:T(128)} %param.7) | copy-start | bytes 100
  10.7 150.8 %copy-start.1 = (s32[1,128]{1,0:T(1,128)S(1)}, s32[1,128]{1,0:T(1,128)}, u32[]{:S(2)}) copy-start(s32[1,128]{1,0:T(1,128)} %param.6) | copy-start | bytes 1540
  10.7 151.2 %copy-start = (s32[8,16]{1,0:T(8,128)S(1)}, s32[8,16]{1,0:T(8,128)}, u32[]{:S(2)}) copy-start(s32[8,16]{1,0:T(8,128)} %param.5) | copy-start | bytes 1540
  10.7 231.5 %all-reduce.2.cloned.1.call-start = ((), (), s32[]{:S(2)}) async-start(), calls=%async_computation.2 | async-start | bytes 2097152 | tf_op jit(solution)/shard_map/psum | solution.py:37
Sparse Core Ops, SparseCore 0:
  10.7 55.4 all-gather.4
  69.4 87.3 all-gather.2
  161.4 80.8 all-reduce.1
where the time goes:
time: 393 us
  waiting for transfers between devices  226 us (58%)
  blocking collectives  142 us (36%)
  between operations  13.9 us (4%)
  matrix products  4.7 us (1%)
  other arithmetic  4.28 us (1%)
    psum x1, blocking collectives, per_device(): populations = lax.psum(local_terms, ('col', 'depth'))  142 us
    all_gather x1, waiting for transfers between devices, per_device(): lax.all_gather(a_slice, 'col', axis=1, tiled=True)  90.6 us
    psum x1, waiting for transfers between devices, per_device(): total_sum = lax.psum(partial_sum, 'depth')  80.2 us
    all_gather x1, waiting for transfers between devices, per_device(): b_full = lax.all_gather(b_slice, 'row', axis=0, tiled=True)  55.5 us
  transfers between devices with their start and end apart: 3, of which 3 were waited for; matrix products, arithmetic and copies ran while one was open for 0% of the time, Pallas kernels for 0%

commit v1 on v0

v1 whole, which is shorter than its diff:
```python
import functools

import jax
import jax.numpy as jnp
from jax import lax
from jax.experimental import pallas as pl
from jax.experimental.pallas import tpu as pltpu
from jax.sharding import PartitionSpec as P

BLOCK = 64
VMEM = pl.BlockSpec(memory_space=pltpu.VMEM)
SMEM = pl.BlockSpec(memory_space=pltpu.SMEM)
F32 = jnp.float32
BF16 = jnp.bfloat16


def lanes(rows, count):
    return lax.broadcasted_iota(jnp.int32, (rows, count), 1)


def block_bits(pat_ref, block_row, own_block, first_col, count):
    bits = jnp.int32(0)
    for slot in range(pat_ref.shape[1] + 1):
        listed = own_block if slot == pat_ref.shape[1] else pat_ref[block_row, slot]
        local = listed - first_col
        inside = (local >= 0) & (local < count)
        bits = bits | jnp.where(inside, jnp.int32(1) << jnp.clip(local, 0, count - 1), 0)
    return bits


def pack_kernel(ids_ref, pat_ref, dens_ref, strip_ref, rows_ref, slots_ref, blocks):
    row, col, depth = ids_ref[0], ids_ref[1], ids_ref[2]
    n_rows, names = pat_ref.shape
    tile = dens_ref.shape[1]
    n_cols = tile // BLOCK
    width = strip_ref.shape[1]
    part = rows_ref.shape[0]
    first_col = col * n_cols
    start = pl.multiple_of(depth * width, width)
    which = lanes(BLOCK, width) // BLOCK
    for i in range(n_rows):
        bits = block_bits(pat_ref, i, row * n_rows + i, first_col, n_cols)
        keep = (lax.shift_right_logical(bits, depth * (width // BLOCK)) >> which) & 1
        here = pl.ds(i * BLOCK, BLOCK)
        value = dens_ref[here, pl.ds(start, width)].astype(F32)
        strip_ref[here, :] = jnp.where(keep == 1, value, 0.0).astype(BF16)
    first_row = depth * (part // BLOCK)
    begin = pl.multiple_of(depth * part, part)
    which = lanes(BLOCK, tile) // BLOCK
    blocks[n_cols] = jnp.zeros_like(blocks[n_cols])
    for u in range(part // BLOCK):
        i = first_row + u
        bits = block_bits(pat_ref, i, row * n_rows + i, first_col, n_cols)
        value = dens_ref[pl.ds(pl.multiple_of(begin + u * BLOCK, BLOCK), BLOCK), :].astype(F32)
        value = jnp.where(((bits >> which) & 1) == 1, value, 0.0)
        here = pl.ds(u * BLOCK, BLOCK)
        rows_ref[here, :] = value.astype(BF16)
        for j in range(n_cols):
            one = value[:, j * BLOCK : (j + 1) * BLOCK]
            blocks[j, here, :] = jnp.concatenate([one, one], axis=1)
    left = lanes(BLOCK, 2 * BLOCK) < BLOCK
    for u in range(part // BLOCK):
        i = first_row + u
        own_block = row * n_rows + i
        here = pl.ds(u * BLOCK, BLOCK)
        places = []
        repeated = jnp.int32(0)
        for slot in range(names):
            listed = pat_ref[i, slot]
            local = listed - first_col
            places.append(jnp.where((local >= 0) & (local < n_cols), local, n_cols))
            repeated = repeated | jnp.where(listed == own_block, 1, 0)
        local = own_block - first_col
        inside = (local >= 0) & (local < n_cols) & (repeated == 0)
        places.append(jnp.where(inside, local, n_cols))
        places.append(jnp.int32(n_cols))
        for pair in range(len(places) // 2):
            value = jnp.where(
                left, blocks[places[2 * pair], here, :], blocks[places[2 * pair + 1], here, :]
            )
            slots_ref[here, pair * 2 * BLOCK : (pair + 1) * 2 * BLOCK] = value.astype(BF16)


def share_kernel(ids_ref, flag_ref, rows_ref, trans_ref, parts_ref, out_ref):
    row, col, depth = ids_ref[0], ids_ref[1], ids_ref[2]
    part, tile = rows_ref.shape
    total = parts_ref[0].astype(F32)
    for source in range(1, parts_ref.shape[0]):
        total = total + parts_ref[source].astype(F32)
    product = jnp.dot(rows_ref[...], trans_ref[...], preferred_element_type=F32)
    eye = lax.broadcasted_iota(jnp.int32, (part, part), 0) == lanes(part, part)
    share = jnp.sum(jnp.where(eye, product, 0.0), axis=0, keepdims=True)
    on_diag = lax.broadcasted_iota(jnp.int32, (part, part), 0) == lanes(part, part)
    own = rows_ref[:, pl.ds(pl.multiple_of(depth * part, part), part)].astype(F32)
    own = jnp.sum(jnp.where(on_diag, own, 0.0), axis=0, keepdims=True)
    twice = jnp.where(row == col, 2.0, 0.0) * own
    first = depth * (part // BLOCK)
    flags = jnp.where(lanes(1, part) < BLOCK, flag_ref[first], flag_ref[first + 1])
    share = jnp.where(flags == 1, share, twice - share)
    rows8 = lax.broadcasted_iota(jnp.int32, (8, part), 0)
    full = jnp.broadcast_to(share, (8, part))
    base = jnp.where(rows8 % 2 == 0, pltpu.roll(full, BLOCK, 1), full)
    high = base.astype(BF16).astype(F32)
    middle = (base - high).astype(BF16).astype(F32)
    low = (base - high - middle).astype(BF16).astype(F32)
    terms = jnp.where(rows8 < 2, high, jnp.where(rows8 < 4, middle, jnp.where(rows8 < 6, low, 0.0)))
    wide = total.shape[1]
    last = jnp.where(lanes(8, part) < BLOCK, total[:, wide - part :], terms)
    send = jnp.concatenate([total[:, : wide - part], last], axis=1).astype(BF16)
    for target in range(out_ref.shape[0]):
        out_ref[target] = send


def product_kernel(
    ids_ref, pat_ref, flag_ref, count_ref, strip_ref, slots_ref, full_ref, out_ref, pop_ref, chosen
):
    row, col, depth = ids_ref[0], ids_ref[1], ids_ref[2]
    n_rows, names = pat_ref.shape
    width = strip_ref.shape[1]
    first_col = col * n_rows
    which = lanes(BLOCK, width) // BLOCK
    used = (names + 1) * BLOCK
    for i in range(n_rows):
        bits = block_bits(pat_ref, i, row * n_rows + i, first_col, n_rows)
        keep = (lax.shift_right_logical(bits, depth * (width // BLOCK)) >> which) & 1
        chosen[i, used:, :] = jnp.zeros_like(chosen[i, used:, :])
        for slot in range(names + 1):
            listed = row * n_rows + i if slot == names else pat_ref[i, slot]
            source = pl.ds(pl.multiple_of(listed * BLOCK, BLOCK), BLOCK)
            chosen[i, slot * BLOCK : (slot + 1) * BLOCK, :] = full_ref[source, :]
        here = pl.ds(i * BLOCK, BLOCK)
        squared = jnp.dot(slots_ref[here, :], chosen[i], preferred_element_type=F32)
        own = strip_ref[here, :].astype(F32)
        flag = jnp.broadcast_to(flag_ref[i], squared.shape)
        value = jnp.where(flag == 1, squared, 2.0 * own - squared)
        out_ref[here, :] = jnp.where(keep == 1, value, 0.0).astype(BF16)
    atoms = count_ref.shape[1]
    span = 2 * BLOCK
    wide = slots_ref.shape[1]
    low = lax.broadcasted_iota(jnp.int32, (atoms, atoms), 0)
    counts = jnp.broadcast_to(count_ref[...].astype(F32), (atoms, atoms))
    ends = jnp.sum(jnp.where(lanes(atoms, atoms) <= low, counts, 0.0), axis=1, keepdims=True)
    starts = jnp.sum(jnp.where(lanes(atoms, atoms) < low, counts, 0.0), axis=1, keepdims=True)
    at = lanes(atoms, span)
    total = jnp.zeros((atoms, span), F32)
    per_depth = 2 * BLOCK
    for d in range(n_rows // 2):
        terms = slots_ref[d * per_depth : (d + 1) * per_depth, wide - span :].astype(F32)
        terms = jnp.sum(terms.reshape(per_depth // 8, 8, span), axis=0)
        diag = terms[0:2] + terms[2:4] + terms[4:6]
        diag = diag.astype(BF16).astype(F32)
        for u in range(2):
            place = (at + ((2 * d + u) * BLOCK - BLOCK)).astype(F32)
            inside = (place >= starts) & (place < ends) & (at >= BLOCK)
            total = total + jnp.where(inside, jnp.broadcast_to(diag[u : u + 1], (atoms, span)), 0.0)
    ones = jnp.ones((8, span), F32)
    sums = lax.dot_general(
        ones, total, (((1,), (1,)), ((), ())), precision=lax.Precision.HIGHEST, preferred_element_type=F32
    )
    pop_ref[...] = sums[0:1]


def per_device(density, pattern, orbital_counts, branch_flag):
    tile = density.shape[0]
    n_row, n_col, n_depth = (lax.axis_size(name) for name in ("row", "col", "depth"))
    width = tile // n_depth
    n_rows, names = pattern.shape
    slots_wide = (names + 2) * BLOCK
    ids = jnp.stack([lax.axis_index("row"), lax.axis_index("col"), lax.axis_index("depth")]).astype(jnp.int32)
    limit = pltpu.CompilerParams(vmem_limit_bytes=48 << 20)
    strip, rows, slots = pl.pallas_call(
        pack_kernel,
        out_shape=(
            jax.ShapeDtypeStruct((tile, width), BF16),
            jax.ShapeDtypeStruct((width, tile), BF16),
            jax.ShapeDtypeStruct((width, slots_wide), BF16),
        ),
        in_specs=[SMEM, SMEM, VMEM],
        out_specs=(VMEM, VMEM, VMEM),
        scratch_shapes=[pltpu.VMEM((tile // BLOCK + 1, width, 2 * BLOCK), F32)],
        compiler_params=limit,
        name="pack",
    )(ids, pattern, density)
    full = lax.all_gather(strip, "row", axis=0, tiled=True)
    swap = [(r * n_col + c, c * n_col + r) for r in range(n_row) for c in range(n_col)]
    trans = lax.ppermute(strip, ("row", "col"), swap)
    chunk = width // n_col
    parts = lax.all_to_all(slots.reshape(n_col, chunk, slots_wide), "col", 0, 0)
    send = pl.pallas_call(
        share_kernel,
        out_shape=jax.ShapeDtypeStruct((n_depth * n_col, chunk, slots_wide), BF16),
        in_specs=[SMEM, SMEM, VMEM, VMEM, VMEM],
        out_specs=VMEM,
        compiler_params=limit,
        name="share",
    )(ids, branch_flag, rows, trans, parts)
    stripe = lax.all_to_all(send, ("depth", "col"), 0, 0).reshape(tile, slots_wide)
    updated, populations = pl.pallas_call(
        product_kernel,
        out_shape=(
            jax.ShapeDtypeStruct((tile, width), BF16),
            jax.ShapeDtypeStruct((1, orbital_counts.shape[1]), F32),
        ),
        in_specs=[SMEM, SMEM, SMEM, VMEM, VMEM, VMEM, VMEM],
        out_specs=(VMEM, VMEM),
        scratch_shapes=[pltpu.VMEM((n_rows, slots_wide, width), BF16)],
        compiler_params=limit,
        name="product",
    )(ids, pattern, branch_flag, orbital_counts, strip, stripe, full)
    return (updated, populations.reshape(-1))


def solution(mesh):
    in_specs = (P("row", "col"), P("row", None), P("row", None), P("row"))
    out_specs = (P("row", ("col", "depth")), P("row"))
    return jax.shard_map(
        per_device, mesh=mesh, in_specs=in_specs, out_specs=out_specs, check_vma=False
    )
```

time: 393 us -> 109 us (0.28)
  waiting for transfers between devices: 226 us -> 10.9 us
  blocking collectives: 142 us -> 52.7 us
  starting transfers between devices: 0.12 us -> 21.7 us
  Pallas kernels: 0 us -> 5.46 us
  matrix products: 4.7 us -> 0 us
  other arithmetic: 4.28 us -> 0.08 us
    all_gather x2 -> x1, waiting for transfers between devices: 146 us -> 0.01 us  [per_device(): full = lax.all_gather(strip, 'row', axis=0, tiled=True)]
    psum x1 -> x0, blocking collectives: 142 us -> none  [per_device(): populations = lax.psum(local_terms, ('col', 'depth'))]
    psum x1 -> x0, waiting for transfers between devices: 80.2 us -> none  [per_device(): total_sum = lax.psum(partial_sum, 'depth')]
    all_to_all x0 -> x1, blocking collectives: none -> 52.7 us  [per_device(): lax.all_to_all(send, ('depth', 'col'), 0, 0).reshape(tile, slots_wide)]
    ppermute x0 -> x1, starting transfers between devices: none -> 11.3 us  [per_device(): trans = lax.ppermute(strip, ('row', 'col'), swap)]
    all_to_all x0 -> x1, starting transfers between devices: none -> 10.4 us  [per_device(): parts = lax.all_to_all(slots.reshape(n_col, chunk, slots_wide), 'col', 0, 0)]
    all_to_all x0 -> x1, waiting for transfers between devices: none -> 6.17 us  [per_device(): parts = lax.all_to_all(slots.reshape(n_col, chunk, slots_wide), 'col', 0, 0)]
    pallas_call x0 -> x3, Pallas kernels: none -> 5.46 us  [the longest x1 2.5 us: per_device(): pl.pallas_call(product_kernel, out_shape=(jax.ShapeDtypeStruct((tile, wid...]
  transfers between devices with their start and end apart: 3 -> 3, of which waited for: 3 -> 2; matrix products, arithmetic and copies ran while one was open for 0% -> 0% of each run, Pallas kernels for 0% -> 1%
where the time goes in v1:
time: 109 us; the launch traced here: 108 us
  blocking collectives  52.7 us (48%)
  starting transfers between devices  21.7 us (20%)
  between operations  14.1 us (13%)
  waiting for transfers between devices  10.9 us (10%)
  Pallas kernels  5.46 us (5%)
  local copies, waits for them, and re-layouts  3.34 us (3%)
    all_to_all x1, blocking collectives, per_device(): lax.all_to_all(send, ('depth', 'col'), 0, 0).reshape(tile, slots_wide)  52.7 us
    ppermute x1, starting transfers between devices, per_device(): trans = lax.ppermute(strip, ('row', 'col'), swap)  11.3 us
    all_to_all x1, starting transfers between devices, per_device(): parts = lax.all_to_all(slots.reshape(n_col, chunk, slots_wide), 'col', 0, 0)  10.4 us
    all_to_all x1, waiting for transfers between devices, per_device(): parts = lax.all_to_all(slots.reshape(n_col, chunk, slots_wide), 'col', 0, 0)  6.17 us
    ppermute x1, waiting for transfers between devices, per_device(): trans = lax.ppermute(strip, ('row', 'col'), swap)  4.67 us
    unnamed x12, local copies, waits for them, and re-layouts  3.34 us
    pallas_call x1, Pallas kernels, per_device(): pl.pallas_call(product_kernel, out_shape=(jax.ShapeDtypeStruct((tile, wid...  2.5 us
  transfers between devices with their start and end apart: 3, of which 2 were waited for; matrix products, arithmetic and copies ran while one was open for 0% of the time, Pallas kernels for 1%

profile of v1, /device:TPU:6, one launch (start us, length us, event | category | flops | bytes accessed | tf_op | source)
XLA Modules:
  0.0 108.3 jit_solution(2613493395761884096)
XLA Ops:
  7.2 0.0 copy-start.4
  7.2 0.0 all-gather.2.cloned.1.call-start
  7.2 0.1 pad_add_fusion.ids_ref
  7.3 0.0 copy-start.1
  7.3 1.0 copy-done.1
  8.3 0.0 copy-start.2
  8.3 0.7 copy-done.2
  9.0 2.1 %pack.1 = (bf16[512,128]{1,0:T(8,128)(2,1)}, bf16[128,512]{1,0:T(8,128)(2,1)S(1)}, bf16[128,1152]{1,0:T(8,128)(2,1)}) custom-call(s32[3]{0:T(128)S(1)} %pad_add_fusion.ids_ref, s32[8,16]{1,0:T(8,128)S(1)} %copy-done.2, bf16[512,512]{1,0:T(8,128)(2,1)S(1)} %copy-done.1), custom_call_target="tpu_custom_call" | custom-call | tf_op jit(solution)/shard_map/pack/pallas_call | solution.py:171
  11.2 0.0 all-gather.2.cloned.1.call-update
  11.2 10.4 %all-to-all-start = ((bf16[16,8,1152]{2,1,0:T(8,128)(2,1)}), bf16[16,8,1152]{2,1,0:T(8,128)(2,1)S(1)}, u32[]{:S(2)}, u32[]{:S(2)}) async-start(bf16[16,8,1152]{2,1,0:T(8,128)(2,1)} %bitcast.3), calls=%async_computation | async-start | bytes 589824 | tf_op jit(solution)/shard_map/all_to_all | solution.py:188
  21.6 11.3 %collective-permute-start = (bf16[512,128]{1,0:T(8,128)(2,1)}, bf16[512,128]{1,0:T(8,128)(2,1)S(1)}, u32[]{:S(2)}, u32[]{:S(2)}) collective-permute-start(bf16[512,128]{1,0:T(8,128)(2,1)} %get-tuple-element.7.strip_ref), channel_id=1, source_target_pairs={{0,0},{4,64},{8,128},{12,192},{16,256},{20,320},{24,384},{28,448},... | collective-permute-start | bytes 393224 | tf_op jit(solution)/shard_map/ppermute | solution.py:186
  32.9 4.7 %collective-permute-done.trans_ref = bf16[512,128]{1,0:T(8,128)(2,1)S(1)} collective-permute-done((bf16[512,128]{1,0:T(8,128)(2,1)}, bf16[512,128]{1,0:T(8,128)(2,1)S(1)}, u32[]{:S(2)}, u32[]{:S(2)}) %collective-permute-start) | collective-permute-done | bytes 131104 | tf_op jit(solution)/shard_map/ppermute | solution.py:186
  37.5 6.2 %all-to-all-done.parts_ref = bf16[16,8,1152]{2,1,0:T(8,128)(2,1)S(1)} async-done(((bf16[16,8,1152]{2,1,0:T(8,128)(2,1)}), bf16[16,8,1152]{2,1,0:T(8,128)(2,1)S(1)}, u32[]{:S(2)}, u32[]{:S(2)}) %all-to-all-start) | async-done | bytes 294944 | tf_op jit(solution)/shard_map/all_to_all | solution.py:188
  43.7 0.0 copy-done.4
  43.7 0.8 share.1
  44.5 0.0 copy-start.3
  44.5 0.0 copy-start.5
  44.6 52.7 %all_to_all.10 = bf16[64,8,1152]{2,1,0:T(8,128)(2,1)S(1)} all-to-all(bf16[64,8,1152]{2,1,0:T(8,128)(2,1)S(1)} %share.1), channel_id=1, replica_groups=mesh['row'=16,'col'=16,'depth'=4] {'depth','col'}, dimensions={0} | all-to-all | bytes 2359296 | tf_op jit(solution)/shard_map/all_to_all | solution.py:197
  97.3 0.0 all-gather.2.cloned.1.call-done.full_ref
  97.3 0.0 copy-done.3
  97.3 0.0 copy-done.5
  97.3 0.0 copy-start
  97.3 1.6 %copy-done = bf16[8192,128]{1,0:T(8,128)(2,1)S(1)} copy-done((bf16[8192,128]{1,0:T(8,128)(2,1)S(1)}, bf16[8192,128]{1,0:T(8,128)(2,1)}, u32[]{:S(2)}) %copy-start) | copy-done | bytes 2097176
  98.9 2.5 %product.1 = (bf16[512,128]{1,0:T(8,128)(2,1)}, f32[1,128]{1,0:T(1,128)}) custom-call(s32[3]{0:T(128)S(1)} %pad_add_fusion.ids_ref, s32[8,16]{1,0:T(8,128)S(1)} %copy-done.3, s32[8]{0:T(128)S(1)} %copy-done.4, s32[1,128]{1,0:T(1,128)S(1)} %copy-done.5, bf16[512,128]{1,0:T(8,128)(2,1)} %get-tuple-element.7.strip_ref, bf16[512,1152]{1,0:T(8,128)(2,1)S(1)} %bitcast.6, ...), custom_call_target="tpu_custom_call" | custom-call | tf_op jit(solution)/shard_map/product/pallas_call | solution.py:198
Async XLA Ops:
  7.2 36.5 %copy-start.4 = (s32[8]{0:T(128)S(1)}, s32[8]{0:T(128)}, u32[]{:S(2)}) copy-start(s32[8]{0:T(128)} %flag_ref.3) | copy-start | bytes 100
  7.2 90.1 %all-gather.2.cloned.1.call-start = ((), (), s32[]{:S(2)}) async-start(), calls=%async_computation.2 | async-start | bytes 2228224 | tf_op jit(solution)/shard_map/all_gather | solution.py:184
  7.3 1.0 copy-start.1
  8.3 0.7 copy-start.2
  11.2 32.5 %all-to-all-start = ((bf16[16,8,1152]{2,1,0:T(8,128)(2,1)}), bf16[16,8,1152]{2,1,0:T(8,128)(2,1)S(1)}, u32[]{:S(2)}, u32[]{:S(2)}) async-start(bf16[16,8,1152]{2,1,0:T(8,128)(2,1)} %bitcast.3), calls=%async_computation | async-start | bytes 589824 | tf_op jit(solution)/shard_map/all_to_all | solution.py:188
  21.6 15.9 %collective-permute-start = (bf16[512,128]{1,0:T(8,128)(2,1)}, bf16[512,128]{1,0:T(8,128)(2,1)S(1)}, u32[]{:S(2)}, u32[]{:S(2)}) collective-permute-start(bf16[512,128]{1,0:T(8,128)(2,1)} %get-tuple-element.7.strip_ref), channel_id=1, source_target_pairs={{0,0},{4,64},{8,128},{12,192},{16,256},{20,320},{24,384},{28,448},... | collective-permute-start | bytes 393224 | tf_op jit(solution)/shard_map/ppermute | solution.py:186
  44.5 52.8 %copy-start.3 = (s32[8,16]{1,0:T(8,128)S(1)}, s32[8,16]{1,0:T(8,128)}, u32[]{:S(2)}) copy-start(s32[8,16]{1,0:T(8,128)} %pat_ref.3) | copy-start | bytes 1540
  44.5 52.8 %copy-start.5 = (s32[1,128]{1,0:T(1,128)S(1)}, s32[1,128]{1,0:T(1,128)}, u32[]{:S(2)}) copy-start(s32[1,128]{1,0:T(1,128)} %count_ref.1) | copy-start | bytes 1540
  97.3 1.6 %copy-start = (bf16[8192,128]{1,0:T(8,128)(2,1)S(1)}, bf16[8192,128]{1,0:T(8,128)(2,1)}, u32[]{:S(2)}) copy-start(bf16[8192,128]{1,0:T(8,128)(2,1)} %all-gather.2.cloned.1.call-done.full_ref) | copy-start | bytes 6291460
Sparse Core Ops, SparseCore 0:
  11.3 56.6 all-gather.1

commit v2 on v1

--- a/solution.py
+++ b/solution.py
@@ -28,22 +28,28 @@
     return bits
 
 
-def pack_kernel(ids_ref, pat_ref, dens_ref, strip_ref, rows_ref, slots_ref, blocks):
-    row, col, depth = ids_ref[0], ids_ref[1], ids_ref[2]
-    n_rows, names = pat_ref.shape
-    tile = dens_ref.shape[1]
-    n_cols = tile // BLOCK
+def strip_kernel(ids_ref, pat_ref, dens_ref, strip_ref):
+    row, col, depth = ids_ref[0], ids_ref[1], ids_ref[2]
+    n_rows = pat_ref.shape[0]
     width = strip_ref.shape[1]
-    part = rows_ref.shape[0]
-    first_col = col * n_cols
+    first_col = col * n_rows
     start = pl.multiple_of(depth * width, width)
     which = lanes(BLOCK, width) // BLOCK
     for i in range(n_rows):
-        bits = block_bits(pat_ref, i, row * n_rows + i, first_col, n_cols)
+        bits = block_bits(pat_ref, i, row * n_rows + i, first_col, n_rows)
         keep = (lax.shift_right_logical(bits, depth * (width // BLOCK)) >> which) & 1
         here = pl.ds(i * BLOCK, BLOCK)
         value = dens_ref[here, pl.ds(start, width)].astype(F32)
         strip_ref[here, :] = jnp.where(keep == 1, value, 0.0).astype(BF16)
+
+
+def pack_kernel(ids_ref, pat_ref, dens_ref, rows_ref, slots_ref, blocks):
+    row, col, depth = ids_ref[0], ids_ref[1], ids_ref[2]
+    n_rows, names = pat_ref.shape
+    tile = dens_ref.shape[1]
+    n_cols = tile // BLOCK
+    part = rows_ref.shape[0]
+    first_col = col * n_cols
     first_row = depth * (part // BLOCK)
     begin = pl.multiple_of(depth * part, part)
     which = lanes(BLOCK, tile) // BLOCK
@@ -168,22 +174,29 @@
     slots_wide = (names + 2) * BLOCK
     ids = jnp.stack([lax.axis_index("row"), lax.axis_index("col"), lax.axis_index("depth")]).astype(jnp.int32)
     limit = pltpu.CompilerParams(vmem_limit_bytes=48 << 20)
-    strip, rows, slots = pl.pallas_call(
+    strip = pl.pallas_call(
+        strip_kernel,
+        out_shape=jax.ShapeDtypeStruct((tile, width), BF16),
+        in_specs=[SMEM, SMEM, VMEM],
+        out_specs=VMEM,
+        compiler_params=limit,
+        name="strip",
+    )(ids, pattern, density)
+    full = lax.all_gather(strip, "row", axis=0, tiled=True)
+    swap = [(r * n_col + c, c * n_col + r) for r in range(n_row) for c in range(n_col)]
+    trans = lax.ppermute(strip, ("row", "col"), swap)
+    rows, slots = pl.pallas_call(
         pack_kernel,
         out_shape=(
-            jax.ShapeDtypeStruct((tile, width), BF16),
             jax.ShapeDtypeStruct((width, tile), BF16),
             jax.ShapeDtypeStruct((width, slots_wide), BF16),
         ),
         in_specs=[SMEM, SMEM, VMEM],
-        out_specs=(VMEM, VMEM, VMEM),
+        out_specs=(VMEM, VMEM),
         scratch_shapes=[pltpu.VMEM((tile // BLOCK + 1, width, 2 * BLOCK), F32)],
         compiler_params=limit,
         name="pack",
     )(ids, pattern, density)
-    full = lax.all_gather(strip, "row", axis=0, tiled=True)
-    swap = [(r * n_col + c, c * n_col + r) for r in range(n_row) for c in range(n_col)]
-    trans = lax.ppermute(strip, ("row", "col"), swap)
     chunk = width // n_col
     parts = lax.all_to_all(slots.reshape(n_col, chunk, slots_wide), "col", 0, 0)
     send = pl.pallas_call(

time: 109 us -> 112 us (1.028)
  local copies, waits for them, and re-layouts: 3.34 us -> 5.06 us
  Pallas kernels: 5.46 us -> 6.64 us
    unnamed x12 -> x16, local copies, waits for them, and re-layouts: 3.34 us -> 5.06 us
    pallas_call x1 -> x2, Pallas kernels: 2.13 us -> 3.32 us  [the longest x1 1.69 us: per_device(): pl.pallas_call(strip_kernel, out_shape=jax.ShapeDtypeStruct((tile, width)...]
  transfers between devices with their start and end apart: 3 -> 3, of which waited for: 2 -> 2; matrix products, arithmetic and copies ran while one was open for 0% -> 0% of each run, Pallas kernels for 1% -> 2%
where the time goes in v2:
time: 112 us; the launch traced here: 111 us
  blocking collectives  53.8 us (48%)
  starting transfers between devices  21.7 us (19%)
  between operations  14.1 us (13%)
  waiting for transfers between devices  10.1 us (9%)
  Pallas kernels  6.64 us (6%)
  local copies, waits for them, and re-layouts  5.06 us (5%)
    all_to_all x1, blocking collectives, per_device(): lax.all_to_all(send, ('depth', 'col'), 0, 0).reshape(tile, slots_wide)  53.8 us
    ppermute x1, starting transfers between devices, per_device(): trans = lax.ppermute(strip, ('row', 'col'), swap)  11.3 us
    all_to_all x1, starting transfers between devices, per_device(): parts = lax.all_to_all(slots.reshape(n_col, chunk, slots_wide), 'col', 0, 0)  10.4 us
    all_to_all x1, waiting for transfers between devices, per_device(): parts = lax.all_to_all(slots.reshape(n_col, chunk, slots_wide), 'col', 0, 0)  5.37 us
    unnamed x16, local copies, waits for them, and re-layouts  5.06 us
    ppermute x1, waiting for transfers between devices, per_device(): trans = lax.ppermute(strip, ('row', 'col'), swap)  4.71 us
    pallas_call x1, Pallas kernels, per_device(): pl.pallas_call(product_kernel, out_shape=(jax.ShapeDtypeStruct((tile, wid...  2.51 us
  transfers between devices with their start and end apart: 3, of which 2 were waited for; matrix products, arithmetic and copies ran while one was open for 0% of the time, Pallas kernels for 2%

profile of v2, /device:TPU:6, one launch (start us, length us, event | category | flops | bytes accessed | tf_op | source)
XLA Modules:
  0.0 111.5 jit_solution(5347624110496706403)
XLA Ops:
  7.2 0.0 copy-start.6
  7.2 0.0 all-gather.2.cloned.1.call-start
  7.2 0.1 pad_add_fusion.ids_ref
  7.3 0.0 copy-start.1
  7.3 1.0 copy-done.1
  8.3 0.0 copy-start.3
  8.3 0.7 copy-done.3
  9.0 1.7 %strip.1.strip_ref = bf16[512,128]{1,0:T(8,128)(2,1)} custom-call(s32[3]{0:T(128)S(1)} %pad_add_fusion.ids_ref, s32[8,16]{1,0:T(8,128)S(1)} %copy-done.3, bf16[512,512]{1,0:T(8,128)(2,1)S(1)} %copy-done.1), custom_call_target="tpu_custom_call" | custom-call | tf_op jit(solution)/shard_map/strip/pallas_call | solution.py:177
  10.7 0.0 all-gather.2.cloned.1.call-update
  10.7 0.0 copy-start.2
  10.8 1.0 copy-done.2
  11.8 0.0 copy-start.4
  11.8 0.7 copy-done.4
  12.5 1.6 %pack.1 = (bf16[128,512]{1,0:T(8,128)(2,1)S(1)}, bf16[128,1152]{1,0:T(8,128)(2,1)}) custom-call(s32[3]{0:T(128)S(1)} %pad_add_fusion.ids_ref, s32[8,16]{1,0:T(8,128)S(1)} %copy-done.4, bf16[512,512]{1,0:T(8,128)(2,1)S(1)} %copy-done.2), custom_call_target="tpu_custom_call" | custom-call | tf_op jit(solution)/shard_map/pack/pallas_call | solution.py:188
  14.1 10.4 %all-to-all-start = ((bf16[16,8,1152]{2,1,0:T(8,128)(2,1)}), bf16[16,8,1152]{2,1,0:T(8,128)(2,1)S(1)}, u32[]{:S(2)}, u32[]{:S(2)}) async-start(bf16[16,8,1152]{2,1,0:T(8,128)(2,1)} %bitcast.3), calls=%async_computation | async-start | bytes 589824 | tf_op jit(solution)/shard_map/all_to_all | solution.py:201
  24.5 11.3 %collective-permute-start = (bf16[512,128]{1,0:T(8,128)(2,1)}, bf16[512,128]{1,0:T(8,128)(2,1)S(1)}, u32[]{:S(2)}, u32[]{:S(2)}) collective-permute-start(bf16[512,128]{1,0:T(8,128)(2,1)} %strip.1.strip_ref), channel_id=1, source_target_pairs={{0,0},{4,64},{8,128},{12,192},{16,256},{20,320},{24,384},{28,448},... | collective-permute-start | bytes 393224 | tf_op jit(solution)/shard_map/ppermute | solution.py:187
  35.8 4.7 %collective-permute-done.trans_ref = bf16[512,128]{1,0:T(8,128)(2,1)S(1)} collective-permute-done((bf16[512,128]{1,0:T(8,128)(2,1)}, bf16[512,128]{1,0:T(8,128)(2,1)S(1)}, u32[]{:S(2)}, u32[]{:S(2)}) %collective-permute-start) | collective-permute-done | bytes 131104 | tf_op jit(solution)/shard_map/ppermute | solution.py:187
  40.5 5.4 %all-to-all-done.parts_ref = bf16[16,8,1152]{2,1,0:T(8,128)(2,1)S(1)} async-done(((bf16[16,8,1152]{2,1,0:T(8,128)(2,1)}), bf16[16,8,1152]{2,1,0:T(8,128)(2,1)S(1)}, u32[]{:S(2)}, u32[]{:S(2)}) %all-to-all-start) | async-done | bytes 294944 | tf_op jit(solution)/shard_map/all_to_all | solution.py:201
  45.8 0.0 copy-done.6
  45.8 0.8 share.1
  46.7 0.0 copy-start.5
  46.7 0.0 copy-start.7
  46.7 53.8 %all_to_all.10 = bf16[64,8,1152]{2,1,0:T(8,128)(2,1)S(1)} all-to-all(bf16[64,8,1152]{2,1,0:T(8,128)(2,1)S(1)} %share.1), channel_id=1, replica_groups=mesh['row'=16,'col'=16,'depth'=4] {'depth','col'}, dimensions={0} | all-to-all | bytes 2359296 | tf_op jit(solution)/shard_map/all_to_all | solution.py:210
  100.5 0.0 all-gather.2.cloned.1.call-done.full_ref
  100.5 0.0 copy-done.5
  100.5 0.0 copy-done.7
  100.5 0.0 copy-start
  100.5 1.6 %copy-done = bf16[8192,128]{1,0:T(8,128)(2,1)S(1)} copy-done((bf16[8192,128]{1,0:T(8,128)(2,1)S(1)}, bf16[8192,128]{1,0:T(8,128)(2,1)}, u32[]{:S(2)}) %copy-start) | copy-done | bytes 2097176
  102.1 2.5 %product.1 = (bf16[512,128]{1,0:T(8,128)(2,1)}, f32[1,128]{1,0:T(1,128)}) custom-call(s32[3]{0:T(128)S(1)} %pad_add_fusion.ids_ref, s32[8,16]{1,0:T(8,128)S(1)} %copy-done.5, s32[8]{0:T(128)S(1)} %copy-done.6, s32[1,128]{1,0:T(1,128)S(1)} %copy-done.7, bf16[512,128]{1,0:T(8,128)(2,1)} %strip.1.strip_ref, bf16[512,1152]{1,0:T(8,128)(2,1)S(1)} %bitcast.6, ...), custom_call_target="tpu_custom_call" | custom-call | tf_op jit(solution)/shard_map/product/pallas_call | solution.py:211
Async XLA Ops:
  7.2 38.7 %copy-start.6 = (s32[8]{0:T(128)S(1)}, s32[8]{0:T(128)}, u32[]{:S(2)}) copy-start(s32[8]{0:T(128)} %flag_ref.3) | copy-start | bytes 100
  7.2 93.3 %all-gather.2.cloned.1.call-start = ((), (), s32[]{:S(2)}) async-start(), calls=%async_computation.2 | async-start | bytes 2228224 | tf_op jit(solution)/shard_map/all_gather | solution.py:185
  7.3 1.0 copy-start.1
  8.3 0.7 copy-start.3
  10.7 1.0 copy-start.2
  11.8 0.7 copy-start.4
  14.1 31.7 %all-to-all-start = ((bf16[16,8,1152]{2,1,0:T(8,128)(2,1)}), bf16[16,8,1152]{2,1,0:T(8,128)(2,1)S(1)}, u32[]{:S(2)}, u32[]{:S(2)}) async-start(bf16[16,8,1152]{2,1,0:T(8,128)(2,1)} %bitcast.3), calls=%async_computation | async-start | bytes 589824 | tf_op jit(solution)/shard_map/all_to_all | solution.py:201
  24.5 16.0 %collective-permute-start = (bf16[512,128]{1,0:T(8,128)(2,1)}, bf16[512,128]{1,0:T(8,128)(2,1)S(1)}, u32[]{:S(2)}, u32[]{:S(2)}) collective-permute-start(bf16[512,128]{1,0:T(8,128)(2,1)} %strip.1.strip_ref), channel_id=1, source_target_pairs={{0,0},{4,64},{8,128},{12,192},{16,256},{20,320},{24,384},{28,448},... | collective-permute-start | bytes 393224 | tf_op jit(solution)/shard_map/ppermute | solution.py:187
  46.7 53.8 %copy-start.5 = (s32[8,16]{1,0:T(8,128)S(1)}, s32[8,16]{1,0:T(8,128)}, u32[]{:S(2)}) copy-start(s32[8,16]{1,0:T(8,128)} %pat_ref.5) | copy-start | bytes 1540
  46.7 53.8 %copy-start.7 = (s32[1,128]{1,0:T(1,128)S(1)}, s32[1,128]{1,0:T(1,128)}, u32[]{:S(2)}) copy-start(s32[1,128]{1,0:T(1,128)} %count_ref.1) | copy-start | bytes 1540
  100.5 1.6 %copy-start = (bf16[8192,128]{1,0:T(8,128)(2,1)S(1)}, bf16[8192,128]{1,0:T(8,128)(2,1)}, u32[]{:S(2)}) copy-start(bf16[8192,128]{1,0:T(8,128)(2,1)} %all-gather.2.cloned.1.call-done.full_ref) | copy-start | bytes 6291460
Sparse Core Ops, SparseCore 0:
  10.9 59.8 all-gather.1

commit v3 on v1

--- a/solution.py
+++ b/solution.py
@@ -12,6 +12,7 @@
 SMEM = pl.BlockSpec(memory_space=pltpu.SMEM)
 F32 = jnp.float32
 BF16 = jnp.bfloat16
+ORDER = (3, 2, 1, 0)
 
 
 def lanes(rows, count):
@@ -111,8 +112,27 @@
         out_ref[target] = send
 
 
+def held_at(block_row, row, n_rows):
+    differs = (block_row // n_rows) ^ row
+    place = jnp.int32(0)
+    for bit, axis_bit in enumerate(ORDER):
+        place = place | (((differs >> axis_bit) & 1) << bit)
+    return place * n_rows + block_row % n_rows
+
+
+def gather_strip(strip):
+    held = strip
+    n_row = lax.axis_size("row")
+    for axis_bit in ORDER:
+        pairs = [(r, r ^ (1 << axis_bit)) for r in range(n_row)]
+        other = lax.ppermute(held, "row", pairs)
+        if axis_bit == ORDER[-1]:
+            return held, other
+        held = jnp.concatenate([held, other], axis=0)
+
+
 def product_kernel(
-    ids_ref, pat_ref, flag_ref, count_ref, strip_ref, slots_ref, full_ref, out_ref, pop_ref, chosen
+    ids_ref, pat_ref, flag_ref, count_ref, strip_ref, slots_ref, even_ref, odd_ref, out_ref, pop_ref, full, chosen
 ):
     row, col, depth = ids_ref[0], ids_ref[1], ids_ref[2]
     n_rows, names = pat_ref.shape
@@ -120,14 +140,17 @@
     first_col = col * n_rows
     which = lanes(BLOCK, width) // BLOCK
     used = (names + 1) * BLOCK
+    half = even_ref.shape[0]
+    full[0:half, :] = even_ref[...]
+    full[half : 2 * half, :] = odd_ref[...]
     for i in range(n_rows):
         bits = block_bits(pat_ref, i, row * n_rows + i, first_col, n_rows)
         keep = (lax.shift_right_logical(bits, depth * (width // BLOCK)) >> which) & 1
         chosen[i, used:, :] = jnp.zeros_like(chosen[i, used:, :])
         for slot in range(names + 1):
             listed = row * n_rows + i if slot == names else pat_ref[i, slot]
-            source = pl.ds(pl.multiple_of(listed * BLOCK, BLOCK), BLOCK)
-            chosen[i, slot * BLOCK : (slot + 1) * BLOCK, :] = full_ref[source, :]
+            source = pl.ds(pl.multiple_of(held_at(listed, row, n_rows) * BLOCK, BLOCK), BLOCK)
+            chosen[i, slot * BLOCK : (slot + 1) * BLOCK, :] = full[source, :]
         here = pl.ds(i * BLOCK, BLOCK)
         squared = jnp.dot(slots_ref[here, :], chosen[i], preferred_element_type=F32)
         own = strip_ref[here, :].astype(F32)
@@ -181,7 +204,7 @@
         compiler_params=limit,
         name="pack",
     )(ids, pattern, density)
-    full = lax.all_gather(strip, "row", axis=0, tiled=True)
+    held, other = gather_strip(strip)
     swap = [(r * n_col + c, c * n_col + r) for r in range(n_row) for c in range(n_col)]
     trans = lax.ppermute(strip, ("row", "col"), swap)
     chunk = width // n_col
@@ -201,12 +224,15 @@
             jax.ShapeDtypeStruct((tile, width), BF16),
             jax.ShapeDtypeStruct((1, orbital_counts.shape[1]), F32),
         ),
-        in_specs=[SMEM, SMEM, SMEM, VMEM, VMEM, VMEM, VMEM],
+        in_specs=[SMEM, SMEM, SMEM, VMEM, VMEM, VMEM, VMEM, VMEM],
         out_specs=(VMEM, VMEM),
-        scratch_shapes=[pltpu.VMEM((n_rows, slots_wide, width), BF16)],
+        scratch_shapes=[
+            pltpu.VMEM((n_row * tile, width), BF16),
+            pltpu.VMEM((n_rows, slots_wide, width), BF16),
+        ],
         compiler_params=limit,
         name="product",
-    )(ids, pattern, branch_flag, orbital_counts, strip, stripe, full)
+    )(ids, pattern, branch_flag, orbital_counts, strip, stripe, held, other)
     return (updated, populations.reshape(-1))
 
 

time: 109 us -> 102 us (0.936)
  the two profiles are of different devices: /device:TPU:6 before, /device:TPU:15 now
where the time goes in v3:
time: 102 us
  starting transfers between devices  52.7 us (52%)
  waiting for transfers between devices  38.2 us (37%)
  Pallas kernels  7.3 us (7%)
  local copies, waits for them, and re-layouts  2.54 us (2%)
    ppermute x4, waiting for transfers between devices, gather_strip(): other = lax.ppermute(held, 'row', pairs)  26.6 us
    ppermute x4, starting transfers between devices, gather_strip(): other = lax.ppermute(held, 'row', pairs)  17 us
    all_to_all x1, starting transfers between devices, per_device(): lax.all_to_all(send, ('depth', 'col'), 0, 0).reshape(tile, slots_wide)  13.6 us
    ppermute x1, starting transfers between devices, per_device(): trans = lax.ppermute(strip, ('row', 'col'), swap)  12.1 us
    ppermute x1, waiting for transfers between devices, per_device(): trans = lax.ppermute(strip, ('row', 'col'), swap)  11.6 us
    all_to_all x1, starting transfers between devices, per_device(): parts = lax.all_to_all(slots.reshape(n_col, chunk, slots_wide), 'col', 0, 0)  10.1 us
    pallas_call x1, Pallas kernels, per_device(): pl.pallas_call(product_kernel, out_shape=(jax.ShapeDtypeStruct((tile, wid...  3.31 us
    unnamed x15, local copies, waits for them, and re-layouts  2.47 us
  transfers between devices with their start and end apart: 7, of which 4 were waited for; matrix products, arithmetic and copies ran while one was open for 0% of the time, Pallas kernels for 2%

profile of v3, /device:TPU:15, one launch (start us, length us, event | category | flops | bytes accessed | tf_op | source)
XLA Modules:
  0.0 101.7 jit_solution(14802913078759980451)
XLA Ops:
  0.6 0.1 pad_add_fusion.ids_ref
  0.7 0.0 copy-start
  0.7 1.0 %copy-done = bf16[512,512]{1,0:T(8,128)(2,1)S(1)} copy-done((bf16[512,512]{1,0:T(8,128)(2,1)S(1)}, bf16[512,512]{1,0:T(8,128)(2,1)}, u32[]{:S(2)}) %copy-start) | copy-done | bytes 524312
  1.8 0.0 copy-start.1
  1.8 0.7 copy-done.1
  2.4 2.1 %pack.1 = (bf16[512,128]{1,0:T(8,128)(2,1)S(1)}, bf16[128,512]{1,0:T(8,128)(2,1)S(1)}, bf16[128,1152]{1,0:T(8,128)(2,1)}) custom-call(s32[3]{0:T(128)S(1)} %pad_add_fusion.ids_ref, s32[8,16]{1,0:T(8,128)S(1)} %copy-done.1, bf16[512,512]{1,0:T(8,128)(2,1)S(1)} %copy-done), custom_call_target="tpu_custom_call" | custom-call | tf_op jit(solution)/shard_map/pack/pallas_call | solution.py:194
  4.6 10.1 %all-to-all-start = ((bf16[16,8,1152]{2,1,0:T(8,128)(2,1)}), bf16[16,8,1152]{2,1,0:T(8,128)(2,1)S(1)}, u32[]{:S(2)}, u32[]{:S(2)}) async-start(bf16[16,8,1152]{2,1,0:T(8,128)(2,1)} %bitcast.3), calls=%async_computation | async-start | bytes 589824 | tf_op jit(solution)/shard_map/all_to_all | solution.py:211
  14.7 12.1 %collective-permute-start = (bf16[512,128]{1,0:T(8,128)(2,1)S(1)}, bf16[512,128]{1,0:T(8,128)(2,1)S(1)}, u32[]{:S(2)}, u32[]{:S(2)}) collective-permute-start(bf16[512,128]{1,0:T(8,128)(2,1)S(1)} %get-tuple-element.7.strip_ref), channel_id=1, source_target_pairs={{0,0},{4,64},{8,128},{12,192},{16,256},{20,320},{24,384},{28,448},... | collective-permute-start | bytes 393224 | tf_op jit(solution)/shard_map/ppermute | solution.py:209
  26.8 5.4 %collective-permute-start.1 = (bf16[512,128]{1,0:T(8,128)(2,1)S(1)}, bf16[512,128]{1,0:T(8,128)(2,1)S(1)}, u32[]{:S(2)}, u32[]{:S(2)}) collective-permute-start(bf16[512,128]{1,0:T(8,128)(2,1)S(1)} %get-tuple-element.7.strip_ref), channel_id=1, source_target_pairs={{0,512},{64,576},{128,640},{192,704},{256,768},{320,832},{384,896}... | collective-permute-start | bytes 393224 | tf_op jit(solution)/shard_map/ppermute | solution.py:128
  32.2 11.6 %collective-permute-done.trans_ref = bf16[512,128]{1,0:T(8,128)(2,1)S(1)} collective-permute-done((bf16[512,128]{1,0:T(8,128)(2,1)S(1)}, bf16[512,128]{1,0:T(8,128)(2,1)S(1)}, u32[]{:S(2)}, u32[]{:S(2)}) %collective-permute-start) | collective-permute-done | bytes 131104 | tf_op jit(solution)/shard_map/ppermute | solution.py:209
  43.8 0.0 all-to-all-done.parts_ref
  43.8 0.0 copy-start.3
  43.8 0.7 copy-done.3
  44.4 1.9 %share.1 = bf16[64,8,1152]{2,1,0:T(8,128)(2,1)} custom-call(s32[3]{0:T(128)S(1)} %pad_add_fusion.ids_ref, s32[8]{0:T(128)S(1)} %copy-done.3, bf16[128,512]{1,0:T(8,128)(2,1)S(1)} %get-tuple-element.8.rows_ref, bf16[512,128]{1,0:T(8,128)(2,1)S(1)} %collective-permute-done.trans_ref, bf16[16,8,1152]{2,1,0:T(8,128)(2,1)S(1)} %all-to-all-done.parts_ref), custom_call_target="tpu_custom_call" | custom-call | tf_op jit(solution)/shard_map/share/pallas_call | solution.py:212
  46.3 13.6 %all-to-all-start.1 = ((bf16[64,8,1152]{2,1,0:T(8,128)(2,1)}), bf16[64,8,1152]{2,1,0:T(8,128)(2,1)S(1)}, u32[]{:S(2)}, u32[]{:S(2)}) async-start(bf16[64,8,1152]{2,1,0:T(8,128)(2,1)} %share.1), calls=%async_computation.1 | async-start | bytes 2359296 | tf_op jit(solution)/shard_map/all_to_all | solution.py:220
  59.9 0.0 collective-permute-done.1
  59.9 5.8 %collective-permute-start.2 = (bf16[1024,128]{1,0:T(8,128)(2,1)S(1)}, bf16[1024,128]{1,0:T(8,128)(2,1)S(1)}, u32[]{:S(2)}, u32[]{:S(2)}) collective-permute-start(bf16[1024,128]{1,0:T(8,128)(2,1)S(1)} %pad_maximum_fusion.1), channel_id=1, source_target_pairs={{0,256},{64,320},{128,384},{192,448},{256,0},{320,64},{384,128},{4... | collective-permute-start | bytes 786440 | tf_op jit(solution)/shard_map/ppermute | solution.py:128
  65.7 12.0 %collective-permute-done.2 = bf16[1024,128]{1,0:T(8,128)(2,1)S(1)} collective-permute-done((bf16[1024,128]{1,0:T(8,128)(2,1)S(1)}, bf16[1024,128]{1,0:T(8,128)(2,1)S(1)}, u32[]{:S(2)}, u32[]{:S(2)}) %collective-permute-start.2) | collective-permute-done | bytes 262176 | tf_op jit(solution)/shard_map/ppermute | solution.py:128
  77.7 0.0 copy-start.2
  77.7 0.0 copy-start.4
  77.7 0.0 copy-start.5
  77.8 2.1 %collective-permute-start.3 = (bf16[2048,128]{1,0:T(8,128)(2,1)S(1)}, bf16[2048,128]{1,0:T(8,128)(2,1)S(1)}, u32[]{:S(2)}, u32[]{:S(2)}) collective-permute-start(bf16[2048,128]{1,0:T(8,128)(2,1)S(1)} %pad_maximum_fusion), channel_id=1, source_target_pairs={{0,128},{64,192},{128,0},{192,64},{256,384},{320,448},{384,256},{4... | collective-permute-start | bytes 1572872 | tf_op jit(solution)/shard_map/ppermute | solution.py:128
  79.9 12.4 %collective-permute-done.3 = bf16[2048,128]{1,0:T(8,128)(2,1)S(1)} collective-permute-done((bf16[2048,128]{1,0:T(8,128)(2,1)S(1)}, bf16[2048,128]{1,0:T(8,128)(2,1)S(1)}, u32[]{:S(2)}, u32[]{:S(2)}) %collective-permute-start.3) | collective-permute-done | bytes 524320 | tf_op jit(solution)/shard_map/ppermute | solution.py:128
  92.3 0.1 constant_dynamic-update-slice_fusion.even_ref
  92.4 3.7 %collective-permute-start.4 = (bf16[4096,128]{1,0:T(8,128)(2,1)S(1)}, bf16[4096,128]{1,0:T(8,128)(2,1)S(1)}, u32[]{:S(2)}, u32[]{:S(2)}) collective-permute-start(bf16[4096,128]{1,0:T(8,128)(2,1)S(1)} %constant_dynamic-update-slice_fusion.even_ref), channel_id=1, source_target_pairs={{0,64},{64,0},{128,192},{192,128},{256,320},{320,256},{384,448},{4... | collective-permute-start | bytes 3145736 | tf_op jit(solution)/shard_map/ppermute | solution.py:128
  96.1 2.3 %collective-permute-done.4.odd_ref = bf16[4096,128]{1,0:T(8,128)(2,1)S(1)} collective-permute-done((bf16[4096,128]{1,0:T(8,128)(2,1)S(1)}, bf16[4096,128]{1,0:T(8,128)(2,1)S(1)}, u32[]{:S(2)}, u32[]{:S(2)}) %collective-permute-start.4) | collective-permute-done | bytes 1048608 | tf_op jit(solution)/shard_map/ppermute | solution.py:128
  98.4 0.0 all-to-all-done.1
  98.4 0.0 copy-done.2
  98.4 0.0 copy-done.4
  98.4 0.0 copy-done.5
  98.4 3.3 %product.1 = (bf16[512,128]{1,0:T(8,128)(2,1)}, f32[1,128]{1,0:T(1,128)}) custom-call(s32[3]{0:T(128)S(1)} %pad_add_fusion.ids_ref, s32[8,16]{1,0:T(8,128)S(1)} %copy-done.2, s32[8]{0:T(128)S(1)} %copy-done.4, s32[1,128]{1,0:T(1,128)S(1)} %copy-done.5, bf16[512,128]{1,0:T(8,128)(2,1)S(1)} %get-tuple-element.7.strip_ref, bf16[512,1152]{1,0:T(8,128)(2,1)S(1)} %bitcast.6, ...), custom_call_target="tpu_custom_call" | custom-call | tf_op jit(solution)/shard_map/product/pallas_call | solution.py:221
  (5 shorter events, 0.1 us)
Async XLA Ops:
  0.7 1.0 %copy-start = (bf16[512,512]{1,0:T(8,128)(2,1)S(1)}, bf16[512,512]{1,0:T(8,128)(2,1)}, u32[]{:S(2)}) copy-start(bf16[512,512]{1,0:T(8,128)(2,1)} %dens_ref.1) | copy-start | bytes 1572868
  1.8 0.7 copy-start.1
  4.6 39.2 %all-to-all-start = ((bf16[16,8,1152]{2,1,0:T(8,128)(2,1)}), bf16[16,8,1152]{2,1,0:T(8,128)(2,1)S(1)}, u32[]{:S(2)}, u32[]{:S(2)}) async-start(bf16[16,8,1152]{2,1,0:T(8,128)(2,1)} %bitcast.3), calls=%async_computation | async-start | bytes 589824 | tf_op jit(solution)/shard_map/all_to_all | solution.py:211
  14.7 29.1 %collective-permute-start = (bf16[512,128]{1,0:T(8,128)(2,1)S(1)}, bf16[512,128]{1,0:T(8,128)(2,1)S(1)}, u32[]{:S(2)}, u32[]{:S(2)}) collective-permute-start(bf16[512,128]{1,0:T(8,128)(2,1)S(1)} %get-tuple-element.7.strip_ref), channel_id=1, source_target_pairs={{0,0},{4,64},{8,128},{12,192},{16,256},{20,320},{24,384},{28,448},... | collective-permute-start | bytes 393224 | tf_op jit(solution)/shard_map/ppermute | solution.py:209
  26.8 33.1 %collective-permute-start.1 = (bf16[512,128]{1,0:T(8,128)(2,1)S(1)}, bf16[512,128]{1,0:T(8,128)(2,1)S(1)}, u32[]{:S(2)}, u32[]{:S(2)}) collective-permute-start(bf16[512,128]{1,0:T(8,128)(2,1)S(1)} %get-tuple-element.7.strip_ref), channel_id=1, source_target_pairs={{0,512},{64,576},{128,640},{192,704},{256,768},{320,832},{384,896}... | collective-permute-start | bytes 393224 | tf_op jit(solution)/shard_map/ppermute | solution.py:128
  43.8 0.7 copy-start.3
  46.3 52.1 %all-to-all-start.1 = ((bf16[64,8,1152]{2,1,0:T(8,128)(2,1)}), bf16[64,8,1152]{2,1,0:T(8,128)(2,1)S(1)}, u32[]{:S(2)}, u32[]{:S(2)}) async-start(bf16[64,8,1152]{2,1,0:T(8,128)(2,1)} %share.1), calls=%async_computation.1 | async-start | bytes 2359296 | tf_op jit(solution)/shard_map/all_to_all | solution.py:220
  59.9 17.8 %collective-permute-start.2 = (bf16[1024,128]{1,0:T(8,128)(2,1)S(1)}, bf16[1024,128]{1,0:T(8,128)(2,1)S(1)}, u32[]{:S(2)}, u32[]{:S(2)}) collective-permute-start(bf16[1024,128]{1,0:T(8,128)(2,1)S(1)} %pad_maximum_fusion.1), channel_id=1, source_target_pairs={{0,256},{64,320},{128,384},{192,448},{256,0},{320,64},{384,128},{4... | collective-permute-start | bytes 786440 | tf_op jit(solution)/shard_map/ppermute | solution.py:128
  77.7 20.7 %copy-start.2 = (s32[8,16]{1,0:T(8,128)S(1)}, s32[8,16]{1,0:T(8,128)}, u32[]{:S(2)}) copy-start(s32[8,16]{1,0:T(8,128)} %pat_ref.3) | copy-start | bytes 1540
  77.7 20.7 %copy-start.4 = (s32[8]{0:T(128)S(1)}, s32[8]{0:T(128)}, u32[]{:S(2)}) copy-start(s32[8]{0:T(128)} %flag_ref.3) | copy-start | bytes 100
  77.7 20.6 %copy-start.5 = (s32[1,128]{1,0:T(1,128)S(1)}, s32[1,128]{1,0:T(1,128)}, u32[]{:S(2)}) copy-start(s32[1,128]{1,0:T(1,128)} %count_ref.1) | copy-start | bytes 1540
  77.8 14.6 %collective-permute-start.3 = (bf16[2048,128]{1,0:T(8,128)(2,1)S(1)}, bf16[2048,128]{1,0:T(8,128)(2,1)S(1)}, u32[]{:S(2)}, u32[]{:S(2)}) collective-permute-start(bf16[2048,128]{1,0:T(8,128)(2,1)S(1)} %pad_maximum_fusion), channel_id=1, source_target_pairs={{0,128},{64,192},{128,0},{192,64},{256,384},{320,448},{384,256},{4... | collective-permute-start | bytes 1572872 | tf_op jit(solution)/shard_map/ppermute | solution.py:128
  92.4 6.0 %collective-permute-start.4 = (bf16[4096,128]{1,0:T(8,128)(2,1)S(1)}, bf16[4096,128]{1,0:T(8,128)(2,1)S(1)}, u32[]{:S(2)}, u32[]{:S(2)}) collective-permute-start(bf16[4096,128]{1,0:T(8,128)(2,1)S(1)} %constant_dynamic-update-slice_fusion.even_ref), channel_id=1, source_target_pairs={{0,64},{64,0},{128,192},{192,128},{256,320},{320,256},{384,448},{4... | collective-permute-start | bytes 3145736 | tf_op jit(solution)/shard_map/ppermute | solution.py:128

commit v4 on v3

--- a/solution.py
+++ b/solution.py
@@ -12,7 +12,7 @@
 SMEM = pl.BlockSpec(memory_space=pltpu.SMEM)
 F32 = jnp.float32
 BF16 = jnp.bfloat16
-ORDER = (3, 2, 1, 0)
+PLACES = 0x63517240
 
 
 def lanes(rows, count):
@@ -113,22 +113,25 @@
 
 
 def held_at(block_row, row, n_rows):
-    differs = (block_row // n_rows) ^ row
-    place = jnp.int32(0)
-    for bit, axis_bit in enumerate(ORDER):
-        place = place | (((differs >> axis_bit) & 1) << bit)
+    owner = block_row // n_rows
+    distance = (owner // 2 - row // 2) & 7
+    place = (jnp.int32(PLACES) >> (distance * 4)) & 7
+    place = place + ((owner ^ row) & 1) * 8
     return place * n_rows + block_row % n_rows
 
 
-def gather_strip(strip):
-    held = strip
+def from_chip(distance, value):
     n_row = lax.axis_size("row")
-    for axis_bit in ORDER:
-        pairs = [(r, r ^ (1 << axis_bit)) for r in range(n_row)]
-        other = lax.ppermute(held, "row", pairs)
-        if axis_bit == ORDER[-1]:
-            return held, other
-        held = jnp.concatenate([held, other], axis=0)
+    return lax.ppermute(value, "row", [(s, (s - 2 * distance) % n_row) for s in range(n_row)])
+
+
+def gather_strip(strip, across):
+    n_row = lax.axis_size("row")
+    pair = jnp.concatenate([strip, across], axis=0)
+    above, below = from_chip(1, pair), from_chip(-1, pair)
+    second, sixth = from_chip(2, strip), from_chip(-2, strip)
+    held = jnp.concatenate([pair, second, sixth, above, below], axis=0)
+    return held, lax.ppermute(held, "row", [(s, s ^ 1) for s in range(n_row)])
 
 
 def product_kernel(
@@ -190,7 +193,7 @@
     n_rows, names = pattern.shape
     slots_wide = (names + 2) * BLOCK
     ids = jnp.stack([lax.axis_index("row"), lax.axis_index("col"), lax.axis_index("depth")]).astype(jnp.int32)
-    limit = pltpu.CompilerParams(vmem_limit_bytes=48 << 20)
+    limit = pltpu.CompilerParams(vmem_limit_bytes=24 << 20)
     strip, rows, slots = pl.pallas_call(
         pack_kernel,
         out_shape=(
@@ -204,11 +207,13 @@
         compiler_params=limit,
         name="pack",
     )(ids, pattern, density)
-    held, other = gather_strip(strip)
+    across = from_chip(4, strip)
     swap = [(r * n_col + c, c * n_col + r) for r in range(n_row) for c in range(n_col)]
     trans = lax.ppermute(strip, ("row", "col"), swap)
     chunk = width // n_col
     parts = lax.all_to_all(slots.reshape(n_col, chunk, slots_wide), "col", 0, 0)
+    trans, parts, across = lax.optimization_barrier((trans, parts, across))
+    held, other = gather_strip(strip, across)
     send = pl.pallas_call(
         share_kernel,
         out_shape=jax.ShapeDtypeStruct((n_depth * n_col, chunk, slots_wide), BF16),

time: 102 us -> 100 us (0.980)
  the two profiles are of different devices: /device:TPU:15 before, /device:TPU:6 now
where the time goes in v4:
time: 100 us; the launch traced here: 99.4 us
  starting transfers between devices  64.8 us (65%)
  waiting for transfers between devices  23.5 us (24%)
  Pallas kernels  7.66 us (8%)
  local copies, waits for them, and re-layouts  2.58 us (3%)
    all_to_all x1, starting transfers between devices, per_device(): lax.all_to_all(send, ('depth', 'col'), 0, 0).reshape(tile, slots_wide)  23.3 us
    ppermute x5, starting transfers between devices, from_chip(): lax.ppermute(value, 'row', [(s, (s - 2 * distance) % n_row) for s in rang...  18 us
    ppermute x5, waiting for transfers between devices, from_chip(): lax.ppermute(value, 'row', [(s, (s - 2 * distance) % n_row) for s in rang...  15.4 us
    ppermute x1, starting transfers between devices, per_device(): trans = lax.ppermute(strip, ('row', 'col'), swap)  11.3 us
    all_to_all x1, starting transfers between devices, per_device(): parts = lax.all_to_all(slots.reshape(n_col, chunk, slots_wide), 'col', 0, 0)  10.4 us
    all_to_all x1, waiting for transfers between devices, per_device(): lax.all_to_all(send, ('depth', 'col'), 0, 0).reshape(tile, slots_wide)  4.95 us
    pallas_call x1, Pallas kernels, per_device(): pl.pallas_call(product_kernel, out_shape=(jax.ShapeDtypeStruct((tile, wid...  3.66 us
    ppermute x1, waiting for transfers between devices, gather_strip(): return (held, lax.ppermute(held, 'row', [(s, s ^ 1) for s in range(n_row)]))  2.63 us
  transfers between devices with their start and end apart: 9, of which 6 were waited for; matrix products, arithmetic and copies ran while one was open for 0% of the time, Pallas kernels for 0%

profile of v4, /device:TPU:6, one launch (start us, length us, event | category | flops | bytes accessed | tf_op | source)
XLA Modules:
  0.0 99.4 jit_solution(12114771693014632920)
XLA Ops:
  0.6 0.1 pad_add_fusion.ids_ref
  0.7 0.0 copy-start
  0.7 1.0 %copy-done = bf16[512,512]{1,0:T(8,128)(2,1)S(1)} copy-done((bf16[512,512]{1,0:T(8,128)(2,1)S(1)}, bf16[512,512]{1,0:T(8,128)(2,1)}, u32[]{:S(2)}) %copy-start) | copy-done | bytes 524312
  1.8 0.7 copy-done.1
  2.4 2.1 %pack.1 = (bf16[512,128]{1,0:T(8,128)(2,1)S(1)}, bf16[128,512]{1,0:T(8,128)(2,1)S(1)}, bf16[128,1152]{1,0:T(8,128)(2,1)}) custom-call(s32[3]{0:T(128)S(1)} %pad_add_fusion.ids_ref, s32[8,16]{1,0:T(8,128)S(1)} %copy-done.1, bf16[512,512]{1,0:T(8,128)(2,1)S(1)} %copy-done), custom_call_target="tpu_custom_call" | custom-call | tf_op jit(solution)/shard_map/pack/pallas_call | solution.py:197
  4.6 10.4 %all-to-all-start = ((bf16[16,8,1152]{2,1,0:T(8,128)(2,1)}), bf16[16,8,1152]{2,1,0:T(8,128)(2,1)S(1)}, u32[]{:S(2)}, u32[]{:S(2)}) async-start(bf16[16,8,1152]{2,1,0:T(8,128)(2,1)} %bitcast.3), calls=%async_computation | async-start | bytes 589824 | tf_op jit(solution)/shard_map/all_to_all | solution.py:214
  15.0 11.3 %collective-permute-start = (bf16[512,128]{1,0:T(8,128)(2,1)S(1)}, bf16[512,128]{1,0:T(8,128)(2,1)S(1)}, u32[]{:S(2)}, u32[]{:S(2)}) collective-permute-start(bf16[512,128]{1,0:T(8,128)(2,1)S(1)} %get-tuple-element.10.strip_ref), channel_id=1, source_target_pairs={{0,0},{4,64},{8,128},{12,192},{16,256},{20,320},{24,384},{28,448},... | collective-permute-start | bytes 393224 | tf_op jit(solution)/shard_map/ppermute | solution.py:212
  26.2 4.0 %collective-permute-start.1 = (bf16[512,128]{1,0:T(8,128)(2,1)S(1)}, bf16[512,128]{1,0:T(8,128)(2,1)S(1)}, u32[]{:S(2)}, u32[]{:S(2)}) collective-permute-start(bf16[512,128]{1,0:T(8,128)(2,1)S(1)} %get-tuple-element.10.strip_ref), channel_id=1, source_target_pairs={{0,512},{64,576},{128,640},{192,704},{256,768},{320,832},{384,896}... | collective-permute-start | bytes 393224 | tf_op jit(solution)/shard_map/ppermute | solution.py:125
  30.3 0.5 collective-permute-done.trans_ref
  30.8 7.6 %collective-permute-done.1 = bf16[512,128]{1,0:T(8,128)(2,1)S(1)} collective-permute-done((bf16[512,128]{1,0:T(8,128)(2,1)S(1)}, bf16[512,128]{1,0:T(8,128)(2,1)S(1)}, u32[]{:S(2)}, u32[]{:S(2)}) %collective-permute-start.1) | collective-permute-done | bytes 131104 | tf_op jit(solution)/shard_map/ppermute | solution.py:125
  38.4 0.0 all-to-all-done.parts_ref
  38.4 0.7 copy-done.3
  39.1 1.9 %share.1 = bf16[64,8,1152]{2,1,0:T(8,128)(2,1)} custom-call(s32[3]{0:T(128)S(1)} %pad_add_fusion.ids_ref, s32[8]{0:T(128)S(1)} %copy-done.3, bf16[128,512]{1,0:T(8,128)(2,1)S(1)} %get-tuple-element.11.rows_ref, bf16[512,128]{1,0:T(8,128)(2,1)S(1)} %collective-permute-done.trans_ref, bf16[16,8,1152]{2,1,0:T(8,128)(2,1)S(1)} %all-to-all-done.parts_ref), custom_call_target="tpu_custom_call" | custom-call | tf_op jit(solution)/shard_map/share/pallas_call | solution.py:217
  41.0 23.3 %all-to-all-start.1 = ((bf16[64,8,1152]{2,1,0:T(8,128)(2,1)}), bf16[64,8,1152]{2,1,0:T(8,128)(2,1)S(1)}, u32[]{:S(2)}, u32[]{:S(2)}) async-start(bf16[64,8,1152]{2,1,0:T(8,128)(2,1)} %share.1), calls=%async_computation.1 | async-start | bytes 2359296 | tf_op jit(solution)/shard_map/all_to_all | solution.py:225
  64.3 0.0 copy-start.2
  64.3 0.0 copy-start.4
  64.3 0.0 copy-start.5
  64.3 2.1 %collective-permute-start.2 = (bf16[512,128]{1,0:T(8,128)(2,1)S(1)}, bf16[512,128]{1,0:T(8,128)(2,1)S(1)}, u32[]{:S(2)}, u32[]{:S(2)}) collective-permute-start(bf16[512,128]{1,0:T(8,128)(2,1)S(1)} %get-tuple-element.10.strip_ref), channel_id=1, source_target_pairs={{0,768},{64,832},{128,896},{192,960},{256,0},{320,64},{384,128},{4... | collective-permute-start | bytes 393224 | tf_op jit(solution)/shard_map/ppermute | solution.py:125
  66.4 1.9 %collective-permute-start.4 = (bf16[1024,128]{1,0:T(8,128)(2,1)S(1)}, bf16[1024,128]{1,0:T(8,128)(2,1)S(1)}, u32[]{:S(2)}, u32[]{:S(2)}) collective-permute-start(bf16[1024,128]{1,0:T(8,128)(2,1)S(1)} %get-tuple-element.18), channel_id=1, source_target_pairs={{0,896},{64,960},{128,0},{192,64},{256,128},{320,192},{384,256},{4... | collective-permute-start | bytes 786440 | tf_op jit(solution)/shard_map/ppermute | solution.py:125
  68.4 6.0 %collective-permute-start.3 = (bf16[512,128]{1,0:T(8,128)(2,1)S(1)}, bf16[512,128]{1,0:T(8,128)(2,1)S(1)}, u32[]{:S(2)}, u32[]{:S(2)}) collective-permute-start(bf16[512,128]{1,0:T(8,128)(2,1)S(1)} %get-tuple-element.10.strip_ref), channel_id=1, source_target_pairs={{0,256},{64,320},{128,384},{192,448},{256,512},{320,576},{384,640}... | collective-permute-start | bytes 393224 | tf_op jit(solution)/shard_map/ppermute | solution.py:125
  74.4 3.9 %collective-permute-start.5 = (bf16[1024,128]{1,0:T(8,128)(2,1)S(1)}, bf16[1024,128]{1,0:T(8,128)(2,1)S(1)}, u32[]{:S(2)}, u32[]{:S(2)}) collective-permute-start(bf16[1024,128]{1,0:T(8,128)(2,1)S(1)} %get-tuple-element.18), channel_id=1, source_target_pairs={{0,128},{64,192},{128,256},{192,320},{256,384},{320,448},{384,512}... | collective-permute-start | bytes 786440 | tf_op jit(solution)/shard_map/ppermute | solution.py:125
  78.3 0.0 collective-permute-done.2
  78.4 1.0 collective-permute-done.3
  79.4 0.0 collective-permute-done.4
  79.4 6.8 %collective-permute-done.5 = bf16[1024,128]{1,0:T(8,128)(2,1)S(1)} collective-permute-done((bf16[1024,128]{1,0:T(8,128)(2,1)S(1)}, bf16[1024,128]{1,0:T(8,128)(2,1)S(1)}, u32[]{:S(2)}, u32[]{:S(2)}) %collective-permute-start.5) | collective-permute-done | bytes 262176 | tf_op jit(solution)/shard_map/ppermute | solution.py:125
  86.3 1.9 %collective-permute-start.6 = (bf16[4096,128]{1,0:T(8,128)(2,1)S(1)}, bf16[4096,128]{1,0:T(8,128)(2,1)S(1)}, u32[]{:S(2)}, u32[]{:S(2)}) collective-permute-start(bf16[4096,128]{1,0:T(8,128)(2,1)S(1)} %constant_dynamic-update-slice_fusion.2.even_ref), channel_id=1, source_target_pairs={{0,64},{64,0},{128,192},{192,128},{256,320},{320,256},{384,448},{4... | collective-permute-start | bytes 3145736 | tf_op jit(solution)/shard_map/ppermute | solution.py:134
  88.2 2.6 %collective-permute-done.6.odd_ref = bf16[4096,128]{1,0:T(8,128)(2,1)S(1)} collective-permute-done((bf16[4096,128]{1,0:T(8,128)(2,1)S(1)}, bf16[4096,128]{1,0:T(8,128)(2,1)S(1)}, u32[]{:S(2)}, u32[]{:S(2)}) %collective-permute-start.6) | collective-permute-done | bytes 1048608 | tf_op jit(solution)/shard_map/ppermute | solution.py:134
  90.8 4.9 %all-to-all-done.1 = bf16[64,8,1152]{2,1,0:T(8,128)(2,1)S(1)} async-done(((bf16[64,8,1152]{2,1,0:T(8,128)(2,1)}), bf16[64,8,1152]{2,1,0:T(8,128)(2,1)S(1)}, u32[]{:S(2)}, u32[]{:S(2)}) %all-to-all-start.1) | async-done | bytes 1179680 | tf_op jit(solution)/shard_map/all_to_all | solution.py:225
  95.8 0.0 copy-done.2
  95.8 0.0 copy-done.4
  95.8 0.0 copy-done.5
  95.8 3.7 %product.1 = (bf16[512,128]{1,0:T(8,128)(2,1)}, f32[1,128]{1,0:T(1,128)}) custom-call(s32[3]{0:T(128)S(1)} %pad_add_fusion.ids_ref, s32[8,16]{1,0:T(8,128)S(1)} %copy-done.2, s32[8]{0:T(128)S(1)} %copy-done.4, s32[1,128]{1,0:T(1,128)S(1)} %copy-done.5, bf16[512,128]{1,0:T(8,128)(2,1)S(1)} %get-tuple-element.10.strip_ref, bf16[512,1152]{1,0:T(8,128)(2,1)S(1)} %bitcast.6, ...), custom_call_target="tpu_custom_call" | custom-call | tf_op jit(solution)/shard_map/product/pallas_call | solution.py:226
  (8 shorter events, 0.2 us)
Async XLA Ops:
  0.7 1.0 %copy-start = (bf16[512,512]{1,0:T(8,128)(2,1)S(1)}, bf16[512,512]{1,0:T(8,128)(2,1)}, u32[]{:S(2)}) copy-start(bf16[512,512]{1,0:T(8,128)(2,1)} %dens_ref.1) | copy-start | bytes 1572868
  1.8 0.7 copy-start.1
  4.6 33.9 %all-to-all-start = ((bf16[16,8,1152]{2,1,0:T(8,128)(2,1)}), bf16[16,8,1152]{2,1,0:T(8,128)(2,1)S(1)}, u32[]{:S(2)}, u32[]{:S(2)}) async-start(bf16[16,8,1152]{2,1,0:T(8,128)(2,1)} %bitcast.3), calls=%async_computation | async-start | bytes 589824 | tf_op jit(solution)/shard_map/all_to_all | solution.py:214
  15.0 15.9 %collective-permute-start = (bf16[512,128]{1,0:T(8,128)(2,1)S(1)}, bf16[512,128]{1,0:T(8,128)(2,1)S(1)}, u32[]{:S(2)}, u32[]{:S(2)}) collective-permute-start(bf16[512,128]{1,0:T(8,128)(2,1)S(1)} %get-tuple-element.10.strip_ref), channel_id=1, source_target_pairs={{0,0},{4,64},{8,128},{12,192},{16,256},{20,320},{24,384},{28,448},... | collective-permute-start | bytes 393224 | tf_op jit(solution)/shard_map/ppermute | solution.py:212
  26.2 12.2 %collective-permute-start.1 = (bf16[512,128]{1,0:T(8,128)(2,1)S(1)}, bf16[512,128]{1,0:T(8,128)(2,1)S(1)}, u32[]{:S(2)}, u32[]{:S(2)}) collective-permute-start(bf16[512,128]{1,0:T(8,128)(2,1)S(1)} %get-tuple-element.10.strip_ref), channel_id=1, source_target_pairs={{0,512},{64,576},{128,640},{192,704},{256,768},{320,832},{384,896}... | collective-permute-start | bytes 393224 | tf_op jit(solution)/shard_map/ppermute | solution.py:125
  38.4 0.7 copy-start.3
  41.0 54.8 %all-to-all-start.1 = ((bf16[64,8,1152]{2,1,0:T(8,128)(2,1)}), bf16[64,8,1152]{2,1,0:T(8,128)(2,1)S(1)}, u32[]{:S(2)}, u32[]{:S(2)}) async-start(bf16[64,8,1152]{2,1,0:T(8,128)(2,1)} %share.1), calls=%async_computation.1 | async-start | bytes 2359296 | tf_op jit(solution)/shard_map/all_to_all | solution.py:225
  64.3 31.5 %copy-start.2 = (s32[8,16]{1,0:T(8,128)S(1)}, s32[8,16]{1,0:T(8,128)}, u32[]{:S(2)}) copy-start(s32[8,16]{1,0:T(8,128)} %pat_ref.3) | copy-start | bytes 1540
  64.3 31.5 %copy-start.4 = (s32[8]{0:T(128)S(1)}, s32[8]{0:T(128)}, u32[]{:S(2)}) copy-start(s32[8]{0:T(128)} %flag_ref.3) | copy-start | bytes 100
  64.3 31.5 %copy-start.5 = (s32[1,128]{1,0:T(1,128)S(1)}, s32[1,128]{1,0:T(1,128)}, u32[]{:S(2)}) copy-start(s32[1,128]{1,0:T(1,128)} %count_ref.1) | copy-start | bytes 1540
  64.3 14.0 %collective-permute-start.2 = (bf16[512,128]{1,0:T(8,128)(2,1)S(1)}, bf16[512,128]{1,0:T(8,128)(2,1)S(1)}, u32[]{:S(2)}, u32[]{:S(2)}) collective-permute-start(bf16[512,128]{1,0:T(8,128)(2,1)S(1)} %get-tuple-element.10.strip_ref), channel_id=1, source_target_pairs={{0,768},{64,832},{128,896},{192,960},{256,0},{320,64},{384,128},{4... | collective-permute-start | bytes 393224 | tf_op jit(solution)/shard_map/ppermute | solution.py:125
  66.4 12.9 %collective-permute-start.4 = (bf16[1024,128]{1,0:T(8,128)(2,1)S(1)}, bf16[1024,128]{1,0:T(8,128)(2,1)S(1)}, u32[]{:S(2)}, u32[]{:S(2)}) collective-permute-start(bf16[1024,128]{1,0:T(8,128)(2,1)S(1)} %get-tuple-element.18), channel_id=1, source_target_pairs={{0,896},{64,960},{128,0},{192,64},{256,128},{320,192},{384,256},{4... | collective-permute-start | bytes 786440 | tf_op jit(solution)/shard_map/ppermute | solution.py:125
  68.4 11.0 %collective-permute-start.3 = (bf16[512,128]{1,0:T(8,128)(2,1)S(1)}, bf16[512,128]{1,0:T(8,128)(2,1)S(1)}, u32[]{:S(2)}, u32[]{:S(2)}) collective-permute-start(bf16[512,128]{1,0:T(8,128)(2,1)S(1)} %get-tuple-element.10.strip_ref), channel_id=1, source_target_pairs={{0,256},{64,320},{128,384},{192,448},{256,512},{320,576},{384,640}... | collective-permute-start | bytes 393224 | tf_op jit(solution)/shard_map/ppermute | solution.py:125
  74.4 11.8 %collective-permute-start.5 = (bf16[1024,128]{1,0:T(8,128)(2,1)S(1)}, bf16[1024,128]{1,0:T(8,128)(2,1)S(1)}, u32[]{:S(2)}, u32[]{:S(2)}) collective-permute-start(bf16[1024,128]{1,0:T(8,128)(2,1)S(1)} %get-tuple-element.18), channel_id=1, source_target_pairs={{0,128},{64,192},{128,256},{192,320},{256,384},{320,448},{384,512}... | collective-permute-start | bytes 786440 | tf_op jit(solution)/shard_map/ppermute | solution.py:125
  86.3 4.6 %collective-permute-start.6 = (bf16[4096,128]{1,0:T(8,128)(2,1)S(1)}, bf16[4096,128]{1,0:T(8,128)(2,1)S(1)}, u32[]{:S(2)}, u32[]{:S(2)}) collective-permute-start(bf16[4096,128]{1,0:T(8,128)(2,1)S(1)} %constant_dynamic-update-slice_fusion.2.even_ref), channel_id=1, source_target_pairs={{0,64},{64,0},{128,192},{192,128},{256,320},{320,256},{384,448},{4... | collective-permute-start | bytes 3145736 | tf_op jit(solution)/shard_map/ppermute | solution.py:134

commit v5 on v4

--- a/solution.py
+++ b/solution.py
@@ -13,6 +13,7 @@
 F32 = jnp.float32
 BF16 = jnp.bfloat16
 PLACES = 0x63517240
+COST = 1 << 36
 
 
 def lanes(rows, count):
@@ -82,18 +83,14 @@
             slots_ref[here, pair * 2 * BLOCK : (pair + 1) * 2 * BLOCK] = value.astype(BF16)
 
 
-def share_kernel(ids_ref, flag_ref, rows_ref, trans_ref, parts_ref, out_ref):
+def diagonal_kernel(ids_ref, flag_ref, rows_ref, trans_ref, terms_ref):
     row, col, depth = ids_ref[0], ids_ref[1], ids_ref[2]
-    part, tile = rows_ref.shape
-    total = parts_ref[0].astype(F32)
-    for source in range(1, parts_ref.shape[0]):
-        total = total + parts_ref[source].astype(F32)
+    part = rows_ref.shape[0]
     product = jnp.dot(rows_ref[...], trans_ref[...], preferred_element_type=F32)
     eye = lax.broadcasted_iota(jnp.int32, (part, part), 0) == lanes(part, part)
     share = jnp.sum(jnp.where(eye, product, 0.0), axis=0, keepdims=True)
-    on_diag = lax.broadcasted_iota(jnp.int32, (part, part), 0) == lanes(part, part)
     own = rows_ref[:, pl.ds(pl.multiple_of(depth * part, part), part)].astype(F32)
-    own = jnp.sum(jnp.where(on_diag, own, 0.0), axis=0, keepdims=True)
+    own = jnp.sum(jnp.where(eye, own, 0.0), axis=0, keepdims=True)
     twice = jnp.where(row == col, 2.0, 0.0) * own
     first = depth * (part // BLOCK)
     flags = jnp.where(lanes(1, part) < BLOCK, flag_ref[first], flag_ref[first + 1])
@@ -104,9 +101,16 @@
     high = base.astype(BF16).astype(F32)
     middle = (base - high).astype(BF16).astype(F32)
     low = (base - high - middle).astype(BF16).astype(F32)
-    terms = jnp.where(rows8 < 2, high, jnp.where(rows8 < 4, middle, jnp.where(rows8 < 6, low, 0.0)))
+    terms_ref[...] = jnp.where(rows8 < 2, high, jnp.where(rows8 < 4, middle, jnp.where(rows8 < 6, low, 0.0)))
+
+
+def share_kernel(terms_ref, parts_ref, out_ref):
+    total = parts_ref[0].astype(F32)
+    for source in range(1, parts_ref.shape[0]):
+        total = total + parts_ref[source].astype(F32)
+    part = terms_ref.shape[1]
     wide = total.shape[1]
-    last = jnp.where(lanes(8, part) < BLOCK, total[:, wide - part :], terms)
+    last = jnp.where(lanes(8, part) < BLOCK, total[:, wide - part :], terms_ref[...])
     send = jnp.concatenate([total[:, : wide - part], last], axis=1).astype(BF16)
     for target in range(out_ref.shape[0]):
         out_ref[target] = send
@@ -212,16 +216,25 @@
     trans = lax.ppermute(strip, ("row", "col"), swap)
     chunk = width // n_col
     parts = lax.all_to_all(slots.reshape(n_col, chunk, slots_wide), "col", 0, 0)
-    trans, parts, across = lax.optimization_barrier((trans, parts, across))
+    parts, across = lax.optimization_barrier((parts, across))
     held, other = gather_strip(strip, across)
+    terms = pl.pallas_call(
+        diagonal_kernel,
+        out_shape=jax.ShapeDtypeStruct((8, width), F32),
+        in_specs=[SMEM, SMEM, VMEM, VMEM],
+        out_specs=VMEM,
+        compiler_params=limit,
+        cost_estimate=pl.CostEstimate(flops=COST, bytes_accessed=1 << 20, transcendentals=0),
+        name="diagonal",
+    )(ids, branch_flag, rows, trans)
     send = pl.pallas_call(
         share_kernel,
         out_shape=jax.ShapeDtypeStruct((n_depth * n_col, chunk, slots_wide), BF16),
-        in_specs=[SMEM, SMEM, VMEM, VMEM, VMEM],
+        in_specs=[VMEM, VMEM],
         out_specs=VMEM,
         compiler_params=limit,
         name="share",
-    )(ids, branch_flag, rows, trans, parts)
+    )(terms, parts)
     stripe = lax.all_to_all(send, ("depth", "col"), 0, 0).reshape(tile, slots_wide)
     updated, populations = pl.pallas_call(
         product_kernel,

time: 100 us -> 95.1 us (0.951)
  starting transfers between devices: 64.8 us -> 55.2 us
  waiting for transfers between devices: 23.5 us -> 28.2 us
    all_to_all x1, waiting for transfers between devices: 0.01 us -> 11.7 us  [per_device(): parts = lax.all_to_all(slots.reshape(n_col, chunk, slots_wide), 'col', 0, 0)]
    ppermute x5, waiting for transfers between devices: 15.4 us -> 7.78 us  [from_chip(): lax.ppermute(value, 'row', [(s, (s - 2 * distance) % n_row) for s in rang...]
    ppermute x1, starting transfers between devices: 11.3 us -> 5.75 us  [per_device(): trans = lax.ppermute(strip, ('row', 'col'), swap)]
    all_to_all x1, starting transfers between devices: 10.4 us -> 7.8 us  [per_device(): parts = lax.all_to_all(slots.reshape(n_col, chunk, slots_wide), 'col', 0, 0)]
    all_to_all x1, starting transfers between devices: 23.3 us -> 20.9 us  [per_device(): lax.all_to_all(send, ('depth', 'col'), 0, 0).reshape(tile, slots_wide)]
    all_to_all x1, waiting for transfers between devices: 4.95 us -> 6.05 us  [per_device(): lax.all_to_all(send, ('depth', 'col'), 0, 0).reshape(tile, slots_wide)]
  transfers between devices with their start and end apart: 9 -> 9, of which waited for: 6 -> 6; matrix products, arithmetic and copies ran while one was open for 0% -> 0% of each run, Pallas kernels for 0% -> 1%
where the time goes in v5:
time: 95.1 us; the launch traced here: 94.5 us
  starting transfers between devices  55.2 us (58%)
  waiting for transfers between devices  28.2 us (30%)
  Pallas kernels  7.73 us (8%)
  local copies, waits for them, and re-layouts  2.57 us (3%)
    all_to_all x1, starting transfers between devices, per_device(): lax.all_to_all(send, ('depth', 'col'), 0, 0).reshape(tile, slots_wide)  20.9 us
    ppermute x5, starting transfers between devices, from_chip(): lax.ppermute(value, 'row', [(s, (s - 2 * distance) % n_row) for s in rang...  18.8 us
    all_to_all x1, waiting for transfers between devices, per_device(): parts = lax.all_to_all(slots.reshape(n_col, chunk, slots_wide), 'col', 0, 0)  11.7 us
    all_to_all x1, starting transfers between devices, per_device(): parts = lax.all_to_all(slots.reshape(n_col, chunk, slots_wide), 'col', 0, 0)  7.8 us
    ppermute x5, waiting for transfers between devices, from_chip(): lax.ppermute(value, 'row', [(s, (s - 2 * distance) % n_row) for s in rang...  7.78 us
    all_to_all x1, waiting for transfers between devices, per_device(): lax.all_to_all(send, ('depth', 'col'), 0, 0).reshape(tile, slots_wide)  6.05 us
    ppermute x1, starting transfers between devices, per_device(): trans = lax.ppermute(strip, ('row', 'col'), swap)  5.75 us
    pallas_call x1, Pallas kernels, per_device(): pl.pallas_call(product_kernel, out_shape=(jax.ShapeDtypeStruct((tile, wid...  3.66 us
  transfers between devices with their start and end apart: 9, of which 6 were waited for; matrix products, arithmetic and copies ran while one was open for 0% of the time, Pallas kernels for 1%

profile of v5, /device:TPU:6, one launch (start us, length us, event | category | flops | bytes accessed | tf_op | source)
XLA Modules:
  0.0 94.5 jit_solution(3544819855353070545)
XLA Ops:
  0.6 0.1 pad_add_fusion.ids_ref
  0.7 1.0 %copy-done = bf16[512,512]{1,0:T(8,128)(2,1)S(1)} copy-done((bf16[512,512]{1,0:T(8,128)(2,1)S(1)}, bf16[512,512]{1,0:T(8,128)(2,1)}, u32[]{:S(2)}) %copy-start) | copy-done | bytes 524312
  1.8 0.7 copy-done.1
  2.4 2.1 %pack.1 = (bf16[512,128]{1,0:T(8,128)(2,1)S(1)}, bf16[128,512]{1,0:T(8,128)(2,1)S(1)}, bf16[128,1152]{1,0:T(8,128)(2,1)}) custom-call(s32[3]{0:T(128)S(1)} %pad_add_fusion.ids_ref, s32[8,16]{1,0:T(8,128)S(1)} %copy-done.1, bf16[512,512]{1,0:T(8,128)(2,1)S(1)} %copy-done), custom_call_target="tpu_custom_call" | custom-call | tf_op jit(solution)/shard_map/pack/pallas_call | solution.py:201
  4.6 5.8 %collective-permute-start = (bf16[512,128]{1,0:T(8,128)(2,1)S(1)}, bf16[512,128]{1,0:T(8,128)(2,1)S(1)}, u32[]{:S(2)}, u32[]{:S(2)}) collective-permute-start(bf16[512,128]{1,0:T(8,128)(2,1)S(1)} %get-tuple-element.9.strip_ref), channel_id=1, source_target_pairs={{0,0},{4,64},{8,128},{12,192},{16,256},{20,320},{24,384},{28,448},... | collective-permute-start | bytes 393224 | tf_op jit(solution)/shard_map/ppermute | solution.py:216
  10.3 4.9 %collective-permute-start.1 = (bf16[512,128]{1,0:T(8,128)(2,1)S(1)}, bf16[512,128]{1,0:T(8,128)(2,1)S(1)}, u32[]{:S(2)}, u32[]{:S(2)}) collective-permute-start(bf16[512,128]{1,0:T(8,128)(2,1)S(1)} %get-tuple-element.9.strip_ref), channel_id=1, source_target_pairs={{0,512},{64,576},{128,640},{192,704},{256,768},{320,832},{384,896}... | collective-permute-start | bytes 393224 | tf_op jit(solution)/shard_map/ppermute | solution.py:129
  15.2 7.8 %all-to-all-start = ((bf16[16,8,1152]{2,1,0:T(8,128)(2,1)}), bf16[16,8,1152]{2,1,0:T(8,128)(2,1)S(1)}, u32[]{:S(2)}, u32[]{:S(2)}) async-start(bf16[16,8,1152]{2,1,0:T(8,128)(2,1)} %bitcast.3), calls=%async_computation | async-start | bytes 589824 | tf_op jit(solution)/shard_map/all_to_all | solution.py:218
  23.1 0.0 collective-permute-done.trans_ref
  23.1 0.0 copy-start.3
  23.1 0.6 copy-done.3
  23.7 0.8 diagonal.1.terms_ref
  24.5 0.0 collective-permute-done.1
  24.5 11.7 %all-to-all-done.parts_ref = bf16[16,8,1152]{2,1,0:T(8,128)(2,1)S(1)} async-done(((bf16[16,8,1152]{2,1,0:T(8,128)(2,1)}), bf16[16,8,1152]{2,1,0:T(8,128)(2,1)S(1)}, u32[]{:S(2)}, u32[]{:S(2)}) %all-to-all-start) | async-done | bytes 294944 | tf_op jit(solution)/shard_map/all_to_all | solution.py:218
  36.3 1.1 %share.1 = bf16[64,8,1152]{2,1,0:T(8,128)(2,1)} custom-call(f32[8,128]{1,0:T(8,128)S(1)} %diagonal.1.terms_ref, bf16[16,8,1152]{2,1,0:T(8,128)(2,1)S(1)} %all-to-all-done.parts_ref), custom_call_target="tpu_custom_call" | custom-call | tf_op jit(solution)/shard_map/share/pallas_call | solution.py:230
  37.4 20.9 %all-to-all-start.1 = ((bf16[64,8,1152]{2,1,0:T(8,128)(2,1)}), bf16[64,8,1152]{2,1,0:T(8,128)(2,1)S(1)}, u32[]{:S(2)}, u32[]{:S(2)}) async-start(bf16[64,8,1152]{2,1,0:T(8,128)(2,1)} %share.1), calls=%async_computation.1 | async-start | bytes 2359296 | tf_op jit(solution)/shard_map/all_to_all | solution.py:238
  58.3 0.0 copy-start.2
  58.3 0.0 copy-start.4
  58.3 0.0 copy-start.5
  58.3 2.1 %collective-permute-start.2 = (bf16[512,128]{1,0:T(8,128)(2,1)S(1)}, bf16[512,128]{1,0:T(8,128)(2,1)S(1)}, u32[]{:S(2)}, u32[]{:S(2)}) collective-permute-start(bf16[512,128]{1,0:T(8,128)(2,1)S(1)} %get-tuple-element.9.strip_ref), channel_id=1, source_target_pairs={{0,768},{64,832},{128,896},{192,960},{256,0},{320,64},{384,128},{4... | collective-permute-start | bytes 393224 | tf_op jit(solution)/shard_map/ppermute | solution.py:129
  60.5 1.9 %collective-permute-start.4 = (bf16[1024,128]{1,0:T(8,128)(2,1)S(1)}, bf16[1024,128]{1,0:T(8,128)(2,1)S(1)}, u32[]{:S(2)}, u32[]{:S(2)}) collective-permute-start(bf16[1024,128]{1,0:T(8,128)(2,1)S(1)} %get-tuple-element.16), channel_id=1, source_target_pairs={{0,896},{64,960},{128,0},{192,64},{256,128},{320,192},{384,256},{4... | collective-permute-start | bytes 786440 | tf_op jit(solution)/shard_map/ppermute | solution.py:129
  62.4 6.0 %collective-permute-start.3 = (bf16[512,128]{1,0:T(8,128)(2,1)S(1)}, bf16[512,128]{1,0:T(8,128)(2,1)S(1)}, u32[]{:S(2)}, u32[]{:S(2)}) collective-permute-start(bf16[512,128]{1,0:T(8,128)(2,1)S(1)} %get-tuple-element.9.strip_ref), channel_id=1, source_target_pairs={{0,256},{64,320},{128,384},{192,448},{256,512},{320,576},{384,640}... | collective-permute-start | bytes 393224 | tf_op jit(solution)/shard_map/ppermute | solution.py:129
  68.4 3.9 %collective-permute-start.5 = (bf16[1024,128]{1,0:T(8,128)(2,1)S(1)}, bf16[1024,128]{1,0:T(8,128)(2,1)S(1)}, u32[]{:S(2)}, u32[]{:S(2)}) collective-permute-start(bf16[1024,128]{1,0:T(8,128)(2,1)S(1)} %get-tuple-element.16), channel_id=1, source_target_pairs={{0,128},{64,192},{128,256},{192,320},{256,384},{320,448},{384,512}... | collective-permute-start | bytes 786440 | tf_op jit(solution)/shard_map/ppermute | solution.py:129
  72.4 0.0 collective-permute-done.2
  72.4 0.9 collective-permute-done.3
  73.3 0.4 collective-permute-done.4
  73.8 6.4 %collective-permute-done.5 = bf16[1024,128]{1,0:T(8,128)(2,1)S(1)} collective-permute-done((bf16[1024,128]{1,0:T(8,128)(2,1)S(1)}, bf16[1024,128]{1,0:T(8,128)(2,1)S(1)}, u32[]{:S(2)}, u32[]{:S(2)}) %collective-permute-start.5) | collective-permute-done | bytes 262176 | tf_op jit(solution)/shard_map/ppermute | solution.py:129
  80.3 1.9 %collective-permute-start.6 = (bf16[4096,128]{1,0:T(8,128)(2,1)S(1)}, bf16[4096,128]{1,0:T(8,128)(2,1)S(1)}, u32[]{:S(2)}, u32[]{:S(2)}) collective-permute-start(bf16[4096,128]{1,0:T(8,128)(2,1)S(1)} %constant_dynamic-update-slice_fusion.2.even_ref), channel_id=1, source_target_pairs={{0,64},{64,0},{128,192},{192,128},{256,320},{320,256},{384,448},{4... | collective-permute-start | bytes 3145736 | tf_op jit(solution)/shard_map/ppermute | solution.py:138
  82.2 2.6 %collective-permute-done.6.odd_ref = bf16[4096,128]{1,0:T(8,128)(2,1)S(1)} collective-permute-done((bf16[4096,128]{1,0:T(8,128)(2,1)S(1)}, bf16[4096,128]{1,0:T(8,128)(2,1)S(1)}, u32[]{:S(2)}, u32[]{:S(2)}) %collective-permute-start.6) | collective-permute-done | bytes 1048608 | tf_op jit(solution)/shard_map/ppermute | solution.py:138
  84.8 6.1 %all-to-all-done.1 = bf16[64,8,1152]{2,1,0:T(8,128)(2,1)S(1)} async-done(((bf16[64,8,1152]{2,1,0:T(8,128)(2,1)}), bf16[64,8,1152]{2,1,0:T(8,128)(2,1)S(1)}, u32[]{:S(2)}, u32[]{:S(2)}) %all-to-all-start.1) | async-done | bytes 1179680 | tf_op jit(solution)/shard_map/all_to_all | solution.py:238
  90.9 0.0 copy-done.2
  90.9 0.0 copy-done.4
  90.9 3.7 %product.1 = (bf16[512,128]{1,0:T(8,128)(2,1)}, f32[1,128]{1,0:T(1,128)}) custom-call(s32[3]{0:T(128)S(1)} %pad_add_fusion.ids_ref, s32[8,16]{1,0:T(8,128)S(1)} %copy-done.2, s32[8]{0:T(128)S(1)} %copy-done.4, s32[1,128]{1,0:T(1,128)S(1)} %copy-done.5, bf16[512,128]{1,0:T(8,128)(2,1)S(1)} %get-tuple-element.9.strip_ref, bf16[512,1152]{1,0:T(8,128)(2,1)S(1)} %bitcast.6, ...), custom_call_target="tpu_custom_call" | custom-call | tf_op jit(solution)/shard_map/product/pallas_call | solution.py:239
  (9 shorter events, 0.2 us)
Async XLA Ops:
  0.7 1.0 %copy-start = (bf16[512,512]{1,0:T(8,128)(2,1)S(1)}, bf16[512,512]{1,0:T(8,128)(2,1)}, u32[]{:S(2)}) copy-start(bf16[512,512]{1,0:T(8,128)(2,1)} %dens_ref.1) | copy-start | bytes 1572868
  1.8 0.7 copy-start.1
  4.6 18.5 %collective-permute-start = (bf16[512,128]{1,0:T(8,128)(2,1)S(1)}, bf16[512,128]{1,0:T(8,128)(2,1)S(1)}, u32[]{:S(2)}, u32[]{:S(2)}) collective-permute-start(bf16[512,128]{1,0:T(8,128)(2,1)S(1)} %get-tuple-element.9.strip_ref), channel_id=1, source_target_pairs={{0,0},{4,64},{8,128},{12,192},{16,256},{20,320},{24,384},{28,448},... | collective-permute-start | bytes 393224 | tf_op jit(solution)/shard_map/ppermute | solution.py:216
  10.3 14.2 %collective-permute-start.1 = (bf16[512,128]{1,0:T(8,128)(2,1)S(1)}, bf16[512,128]{1,0:T(8,128)(2,1)S(1)}, u32[]{:S(2)}, u32[]{:S(2)}) collective-permute-start(bf16[512,128]{1,0:T(8,128)(2,1)S(1)} %get-tuple-element.9.strip_ref), channel_id=1, source_target_pairs={{0,512},{64,576},{128,640},{192,704},{256,768},{320,832},{384,896}... | collective-permute-start | bytes 393224 | tf_op jit(solution)/shard_map/ppermute | solution.py:129
  15.2 21.0 %all-to-all-start = ((bf16[16,8,1152]{2,1,0:T(8,128)(2,1)}), bf16[16,8,1152]{2,1,0:T(8,128)(2,1)S(1)}, u32[]{:S(2)}, u32[]{:S(2)}) async-start(bf16[16,8,1152]{2,1,0:T(8,128)(2,1)} %bitcast.3), calls=%async_computation | async-start | bytes 589824 | tf_op jit(solution)/shard_map/all_to_all | solution.py:218
  23.1 0.7 copy-start.3
  37.4 53.4 %all-to-all-start.1 = ((bf16[64,8,1152]{2,1,0:T(8,128)(2,1)}), bf16[64,8,1152]{2,1,0:T(8,128)(2,1)S(1)}, u32[]{:S(2)}, u32[]{:S(2)}) async-start(bf16[64,8,1152]{2,1,0:T(8,128)(2,1)} %share.1), calls=%async_computation.1 | async-start | bytes 2359296 | tf_op jit(solution)/shard_map/all_to_all | solution.py:238
  58.3 32.6 %copy-start.2 = (s32[8,16]{1,0:T(8,128)S(1)}, s32[8,16]{1,0:T(8,128)}, u32[]{:S(2)}) copy-start(s32[8,16]{1,0:T(8,128)} %pat_ref.3) | copy-start | bytes 1540
  58.3 32.6 %copy-start.4 = (s32[8]{0:T(128)S(1)}, s32[8]{0:T(128)}, u32[]{:S(2)}) copy-start(s32[8]{0:T(128)} %flag_ref.3) | copy-start | bytes 100
  58.3 32.6 %copy-start.5 = (s32[1,128]{1,0:T(1,128)S(1)}, s32[1,128]{1,0:T(1,128)}, u32[]{:S(2)}) copy-start(s32[1,128]{1,0:T(1,128)} %count_ref.1) | copy-start | bytes 1540
  58.3 14.0 %collective-permute-start.2 = (bf16[512,128]{1,0:T(8,128)(2,1)S(1)}, bf16[512,128]{1,0:T(8,128)(2,1)S(1)}, u32[]{:S(2)}, u32[]{:S(2)}) collective-permute-start(bf16[512,128]{1,0:T(8,128)(2,1)S(1)} %get-tuple-element.9.strip_ref), channel_id=1, source_target_pairs={{0,768},{64,832},{128,896},{192,960},{256,0},{320,64},{384,128},{4... | collective-permute-start | bytes 393224 | tf_op jit(solution)/shard_map/ppermute | solution.py:129
  60.5 13.3 %collective-permute-start.4 = (bf16[1024,128]{1,0:T(8,128)(2,1)S(1)}, bf16[1024,128]{1,0:T(8,128)(2,1)S(1)}, u32[]{:S(2)}, u32[]{:S(2)}) collective-permute-start(bf16[1024,128]{1,0:T(8,128)(2,1)S(1)} %get-tuple-element.16), channel_id=1, source_target_pairs={{0,896},{64,960},{128,0},{192,64},{256,128},{320,192},{384,256},{4... | collective-permute-start | bytes 786440 | tf_op jit(solution)/shard_map/ppermute | solution.py:129
  62.4 10.9 %collective-permute-start.3 = (bf16[512,128]{1,0:T(8,128)(2,1)S(1)}, bf16[512,128]{1,0:T(8,128)(2,1)S(1)}, u32[]{:S(2)}, u32[]{:S(2)}) collective-permute-start(bf16[512,128]{1,0:T(8,128)(2,1)S(1)} %get-tuple-element.9.strip_ref), channel_id=1, source_target_pairs={{0,256},{64,320},{128,384},{192,448},{256,512},{320,576},{384,640}... | collective-permute-start | bytes 393224 | tf_op jit(solution)/shard_map/ppermute | solution.py:129
  68.4 11.8 %collective-permute-start.5 = (bf16[1024,128]{1,0:T(8,128)(2,1)S(1)}, bf16[1024,128]{1,0:T(8,128)(2,1)S(1)}, u32[]{:S(2)}, u32[]{:S(2)}) collective-permute-start(bf16[1024,128]{1,0:T(8,128)(2,1)S(1)} %get-tuple-element.16), channel_id=1, source_target_pairs={{0,128},{64,192},{128,256},{192,320},{256,384},{320,448},{384,512}... | collective-permute-start | bytes 786440 | tf_op jit(solution)/shard_map/ppermute | solution.py:129
  80.3 4.6 %collective-permute-start.6 = (bf16[4096,128]{1,0:T(8,128)(2,1)S(1)}, bf16[4096,128]{1,0:T(8,128)(2,1)S(1)}, u32[]{:S(2)}, u32[]{:S(2)}) collective-permute-start(bf16[4096,128]{1,0:T(8,128)(2,1)S(1)} %constant_dynamic-update-slice_fusion.2.even_ref), channel_id=1, source_target_pairs={{0,64},{64,0},{128,192},{192,128},{256,320},{320,256},{384,448},{4... | collective-permute-start | bytes 3145736 | tf_op jit(solution)/shard_map/ppermute | solution.py:138

commit v6 on v5

--- a/solution.py
+++ b/solution.py
@@ -10,6 +10,7 @@
 BLOCK = 64
 VMEM = pl.BlockSpec(memory_space=pltpu.VMEM)
 SMEM = pl.BlockSpec(memory_space=pltpu.SMEM)
+HBM = pl.BlockSpec(memory_space=pltpu.HBM)
 F32 = jnp.float32
 BF16 = jnp.bfloat16
 PLACES = 0x63517240
@@ -30,8 +31,12 @@
     return bits
 
 
-def pack_kernel(ids_ref, pat_ref, dens_ref, strip_ref, rows_ref, slots_ref, blocks):
-    row, col, depth = ids_ref[0], ids_ref[1], ids_ref[2]
+def pack_kernel(pat_hbm, dens_hbm, strip_ref, rows_ref, slots_ref, pat_ref, dens_ref, blocks, done):
+    pat_copy = pltpu.make_async_copy(pat_hbm, pat_ref, done.at[0])
+    dens_copy = pltpu.make_async_copy(dens_hbm, dens_ref, done.at[1])
+    pat_copy.start()
+    dens_copy.start()
+    row, col, depth = (lax.axis_index(name) for name in ("row", "col", "depth"))
     n_rows, names = pat_ref.shape
     tile = dens_ref.shape[1]
     n_cols = tile // BLOCK
@@ -40,8 +45,10 @@
     first_col = col * n_cols
     start = pl.multiple_of(depth * width, width)
     which = lanes(BLOCK, width) // BLOCK
-    for i in range(n_rows):
-        bits = block_bits(pat_ref, i, row * n_rows + i, first_col, n_cols)
+    pat_copy.wait()
+    kept = [block_bits(pat_ref, i, row * n_rows + i, first_col, n_cols) for i in range(n_rows)]
+    dens_copy.wait()
+    for i, bits in enumerate(kept):
         keep = (lax.shift_right_logical(bits, depth * (width // BLOCK)) >> which) & 1
         here = pl.ds(i * BLOCK, BLOCK)
         value = dens_ref[here, pl.ds(start, width)].astype(F32)
@@ -83,25 +90,21 @@
             slots_ref[here, pair * 2 * BLOCK : (pair + 1) * 2 * BLOCK] = value.astype(BF16)
 
 
-def diagonal_kernel(ids_ref, flag_ref, rows_ref, trans_ref, terms_ref):
-    row, col, depth = ids_ref[0], ids_ref[1], ids_ref[2]
+def diagonal_kernel(rows_ref, trans_ref, terms_ref):
+    row, col, depth = (lax.axis_index(name) for name in ("row", "col", "depth"))
     part = rows_ref.shape[0]
     product = jnp.dot(rows_ref[...], trans_ref[...], preferred_element_type=F32)
     eye = lax.broadcasted_iota(jnp.int32, (part, part), 0) == lanes(part, part)
     share = jnp.sum(jnp.where(eye, product, 0.0), axis=0, keepdims=True)
     own = rows_ref[:, pl.ds(pl.multiple_of(depth * part, part), part)].astype(F32)
-    own = jnp.sum(jnp.where(eye, own, 0.0), axis=0, keepdims=True)
-    twice = jnp.where(row == col, 2.0, 0.0) * own
-    first = depth * (part // BLOCK)
-    flags = jnp.where(lanes(1, part) < BLOCK, flag_ref[first], flag_ref[first + 1])
-    share = jnp.where(flags == 1, share, twice - share)
+    own = jnp.where(row == col, 1.0, 0.0) * jnp.sum(jnp.where(eye, own, 0.0), axis=0, keepdims=True)
     rows8 = lax.broadcasted_iota(jnp.int32, (8, part), 0)
-    full = jnp.broadcast_to(share, (8, part))
+    full = jnp.where(rows8 < 6, jnp.broadcast_to(share, (8, part)), jnp.broadcast_to(own, (8, part)))
     base = jnp.where(rows8 % 2 == 0, pltpu.roll(full, BLOCK, 1), full)
     high = base.astype(BF16).astype(F32)
     middle = (base - high).astype(BF16).astype(F32)
     low = (base - high - middle).astype(BF16).astype(F32)
-    terms_ref[...] = jnp.where(rows8 < 2, high, jnp.where(rows8 < 4, middle, jnp.where(rows8 < 6, low, 0.0)))
+    terms_ref[...] = jnp.where(rows8 < 2, high, jnp.where(rows8 < 4, middle, jnp.where(rows8 < 6, low, base)))
 
 
 def share_kernel(terms_ref, parts_ref, out_ref):
@@ -139,17 +142,47 @@
 
 
 def product_kernel(
-    ids_ref, pat_ref, flag_ref, count_ref, strip_ref, slots_ref, even_ref, odd_ref, out_ref, pop_ref, full, chosen
+    pat_ref, flag_ref, count_ref, strip_ref, slots_ref, even_ref, odd_ref, out_ref, pop_ref, full, chosen, done
 ):
-    row, col, depth = ids_ref[0], ids_ref[1], ids_ref[2]
+    row, col, depth = (lax.axis_index(name) for name in ("row", "col", "depth"))
     n_rows, names = pat_ref.shape
     width = strip_ref.shape[1]
     first_col = col * n_rows
     which = lanes(BLOCK, width) // BLOCK
     used = (names + 1) * BLOCK
     half = even_ref.shape[0]
-    full[0:half, :] = even_ref[...]
-    full[half : 2 * half, :] = odd_ref[...]
+    even_copy = pltpu.make_async_copy(even_ref, full.at[pl.ds(0, half), :], done.at[0])
+    odd_copy = pltpu.make_async_copy(odd_ref, full.at[pl.ds(half, half), :], done.at[1])
+    even_copy.start()
+    odd_copy.start()
+    atoms = count_ref.shape[1]
+    span = 2 * BLOCK
+    wide = slots_ref.shape[1]
+    low = lax.broadcasted_iota(jnp.int32, (atoms, atoms), 0)
+    counts = jnp.broadcast_to(count_ref[...].astype(F32), (atoms, atoms))
+    ends = jnp.sum(jnp.where(lanes(atoms, atoms) <= low, counts, 0.0), axis=1, keepdims=True)
+    starts = jnp.sum(jnp.where(lanes(atoms, atoms) < low, counts, 0.0), axis=1, keepdims=True)
+    at = lanes(atoms, span)
+    total = jnp.zeros((atoms, span), F32)
+    per_depth = 2 * BLOCK
+    for d in range(n_rows // 2):
+        terms = slots_ref[d * per_depth : (d + 1) * per_depth, wide - span :].astype(F32)
+        terms = jnp.sum(terms.reshape(per_depth // 8, 8, span), axis=0)
+        for u in range(2):
+            squared = terms[u : u + 1] + terms[u + 2 : u + 3] + terms[u + 4 : u + 5]
+            flag = jnp.broadcast_to(flag_ref[2 * d + u], squared.shape)
+            diag = jnp.where(flag == 1, squared, 2.0 * terms[u + 6 : u + 7] - squared)
+            diag = diag.astype(BF16).astype(F32)
+            place = (at + ((2 * d + u) * BLOCK - BLOCK)).astype(F32)
+            inside = (place >= starts) & (place < ends) & (at >= BLOCK)
+            total = total + jnp.where(inside, jnp.broadcast_to(diag, (atoms, span)), 0.0)
+    ones = jnp.ones((8, span), F32)
+    sums = lax.dot_general(
+        ones, total, (((1,), (1,)), ((), ())), precision=lax.Precision.HIGHEST, preferred_element_type=F32
+    )
+    pop_ref[...] = sums[0:1]
+    even_copy.wait()
+    odd_copy.wait()
     for i in range(n_rows):
         bits = block_bits(pat_ref, i, row * n_rows + i, first_col, n_rows)
         keep = (lax.shift_right_logical(bits, depth * (width // BLOCK)) >> which) & 1
@@ -164,30 +197,6 @@
         flag = jnp.broadcast_to(flag_ref[i], squared.shape)
         value = jnp.where(flag == 1, squared, 2.0 * own - squared)
         out_ref[here, :] = jnp.where(keep == 1, value, 0.0).astype(BF16)
-    atoms = count_ref.shape[1]
-    span = 2 * BLOCK
-    wide = slots_ref.shape[1]
-    low = lax.broadcasted_iota(jnp.int32, (atoms, atoms), 0)
-    counts = jnp.broadcast_to(count_ref[...].astype(F32), (atoms, atoms))
-    ends = jnp.sum(jnp.where(lanes(atoms, atoms) <= low, counts, 0.0), axis=1, keepdims=True)
-    starts = jnp.sum(jnp.where(lanes(atoms, atoms) < low, counts, 0.0), axis=1, keepdims=True)
-    at = lanes(atoms, span)
-    total = jnp.zeros((atoms, span), F32)
-    per_depth = 2 * BLOCK
-    for d in range(n_rows // 2):
-        terms = slots_ref[d * per_depth : (d + 1) * per_depth, wide - span :].astype(F32)
-        terms = jnp.sum(terms.reshape(per_depth // 8, 8, span), axis=0)
-        diag = terms[0:2] + terms[2:4] + terms[4:6]
-        diag = diag.astype(BF16).astype(F32)
-        for u in range(2):
-            place = (at + ((2 * d + u) * BLOCK - BLOCK)).astype(F32)
-            inside = (place >= starts) & (place < ends) & (at >= BLOCK)
-            total = total + jnp.where(inside, jnp.broadcast_to(diag[u : u + 1], (atoms, span)), 0.0)
-    ones = jnp.ones((8, span), F32)
-    sums = lax.dot_general(
-        ones, total, (((1,), (1,)), ((), ())), precision=lax.Precision.HIGHEST, preferred_element_type=F32
-    )
-    pop_ref[...] = sums[0:1]
 
 
 def per_device(density, pattern, orbital_counts, branch_flag):
@@ -196,7 +205,6 @@
     width = tile // n_depth
     n_rows, names = pattern.shape
     slots_wide = (names + 2) * BLOCK
-    ids = jnp.stack([lax.axis_index("row"), lax.axis_index("col"), lax.axis_index("depth")]).astype(jnp.int32)
     limit = pltpu.CompilerParams(vmem_limit_bytes=24 << 20)
     strip, rows, slots = pl.pallas_call(
         pack_kernel,
@@ -205,28 +213,31 @@
             jax.ShapeDtypeStruct((width, tile), BF16),
             jax.ShapeDtypeStruct((width, slots_wide), BF16),
         ),
-        in_specs=[SMEM, SMEM, VMEM],
+        in_specs=[HBM, HBM],
         out_specs=(VMEM, VMEM, VMEM),
-        scratch_shapes=[pltpu.VMEM((tile // BLOCK + 1, width, 2 * BLOCK), F32)],
-        compiler_params=limit,
+        scratch_shapes=[
+            pltpu.SMEM(pattern.shape, jnp.int32),
+            pltpu.VMEM(density.shape, BF16),
+            pltpu.VMEM((tile // BLOCK + 1, width, 2 * BLOCK), F32),
+            pltpu.SemaphoreType.DMA((2,)),
+        ],
+        compiler_params=pltpu.CompilerParams(vmem_limit_bytes=60 << 20),
         name="pack",
-    )(ids, pattern, density)
+    )(pattern, density)
     across = from_chip(4, strip)
     swap = [(r * n_col + c, c * n_col + r) for r in range(n_row) for c in range(n_col)]
     trans = lax.ppermute(strip, ("row", "col"), swap)
     chunk = width // n_col
     parts = lax.all_to_all(slots.reshape(n_col, chunk, slots_wide), "col", 0, 0)
-    parts, across = lax.optimization_barrier((parts, across))
-    held, other = gather_strip(strip, across)
     terms = pl.pallas_call(
         diagonal_kernel,
         out_shape=jax.ShapeDtypeStruct((8, width), F32),
-        in_specs=[SMEM, SMEM, VMEM, VMEM],
+        in_specs=[VMEM, VMEM],
         out_specs=VMEM,
         compiler_params=limit,
         cost_estimate=pl.CostEstimate(flops=COST, bytes_accessed=1 << 20, transcendentals=0),
         name="diagonal",
-    )(ids, branch_flag, rows, trans)
+    )(rows, trans)
     send = pl.pallas_call(
         share_kernel,
         out_shape=jax.ShapeDtypeStruct((n_depth * n_col, chunk, slots_wide), BF16),
@@ -235,6 +246,7 @@
         compiler_params=limit,
         name="share",
     )(terms, parts)
+    held, other = gather_strip(strip, across)
     stripe = lax.all_to_all(send, ("depth", "col"), 0, 0).reshape(tile, slots_wide)
     updated, populations = pl.pallas_call(
         product_kernel,
@@ -242,15 +254,16 @@
             jax.ShapeDtypeStruct((tile, width), BF16),
             jax.ShapeDtypeStruct((1, orbital_counts.shape[1]), F32),
         ),
-        in_specs=[SMEM, SMEM, SMEM, VMEM, VMEM, VMEM, VMEM, VMEM],
+        in_specs=[SMEM, SMEM, VMEM, VMEM, VMEM, VMEM, VMEM],
         out_specs=(VMEM, VMEM),
         scratch_shapes=[
             pltpu.VMEM((n_row * tile, width), BF16),
             pltpu.VMEM((n_rows, slots_wide, width), BF16),
+            pltpu.SemaphoreType.DMA((2,)),
         ],
         compiler_params=limit,
         name="product",
-    )(ids, pattern, branch_flag, orbital_counts, strip, stripe, held, other)
+    )(pattern, branch_flag, orbital_counts, strip, stripe, held, other)
     return (updated, populations.reshape(-1))
 
 

time: 95.1 us -> 95.7 us (level)
  the two profiles are of different devices: /device:TPU:6 before, /device:TPU:1 now
where the time goes in v6:
time: 95.7 us; the launch traced here: 95.1 us
  starting transfers between devices  63.6 us (66%)
  waiting for transfers between devices  21.8 us (23%)
  Pallas kernels  7.77 us (8%)
  local copies, waits for them, and re-layouts  1.09 us (1%)
    ppermute x5, starting transfers between devices, from_chip(): lax.ppermute(value, 'row', [(s, (s - 2 * distance) % n_row) for s in rang...  22.5 us
    all_to_all x1, starting transfers between devices, per_device(): lax.all_to_all(send, ('depth', 'col'), 0, 0).reshape(tile, slots_wide)  20.5 us
    all_to_all x1, starting transfers between devices, per_device(): parts = lax.all_to_all(slots.reshape(n_col, chunk, slots_wide), 'col', 0, 0)  11.4 us
    ppermute x5, waiting for transfers between devices, from_chip(): lax.ppermute(value, 'row', [(s, (s - 2 * distance) % n_row) for s in rang...  10.2 us
    all_to_all x1, waiting for transfers between devices, per_device(): parts = lax.all_to_all(slots.reshape(n_col, chunk, slots_wide), 'col', 0, 0)  9.34 us
    ppermute x1, starting transfers between devices, per_device(): trans = lax.ppermute(strip, ('row', 'col'), swap)  6.3 us
    pallas_call x1, Pallas kernels, per_device(): pl.pallas_call(product_kernel, out_shape=(jax.ShapeDtypeStruct((tile, wid...  4.16 us
    ppermute x1, starting transfers between devices, gather_strip(): return (held, lax.ppermute(held, 'row', [(s, s ^ 1) for s in range(n_row)]))  2.92 us
  transfers between devices with their start and end apart: 9, of which 5 were waited for; matrix products, arithmetic and copies ran while one was open for 0% of the time, Pallas kernels for 0%

profile of v6, /device:TPU:1, one launch (start us, length us, event | category | flops | bytes accessed | tf_op | source)
XLA Modules:
  0.0 95.1 jit_solution(16283959730556150228)
XLA Ops:
  0.6 2.2 %pack.1 = (bf16[512,128]{1,0:T(8,128)(2,1)}, bf16[128,512]{1,0:T(8,128)(2,1)}, bf16[128,1152]{1,0:T(8,128)(2,1)}) custom-call(s32[8,16]{1,0:T(8,128)} %pat_ref.1, bf16[512,512]{1,0:T(8,128)(2,1)} %dens_hbm.1), custom_call_target="tpu_custom_call" | custom-call | tf_op jit(solution)/shard_map/pack/pallas_call | solution.py:209
  2.8 6.3 %collective-permute-start = (bf16[512,128]{1,0:T(8,128)(2,1)}, bf16[512,128]{1,0:T(8,128)(2,1)S(1)}, u32[]{:S(2)}, u32[]{:S(2)}) collective-permute-start(bf16[512,128]{1,0:T(8,128)(2,1)} %get-tuple-element.7.strip_ref), channel_id=1, source_target_pairs={{0,0},{4,64},{8,128},{12,192},{16,256},{20,320},{24,384},{28,448},... | collective-permute-start | bytes 393224 | tf_op jit(solution)/shard_map/ppermute | solution.py:229
  9.1 11.4 %all-to-all-start = ((bf16[16,8,1152]{2,1,0:T(8,128)(2,1)}), bf16[16,8,1152]{2,1,0:T(8,128)(2,1)S(1)}, u32[]{:S(2)}, u32[]{:S(2)}) async-start(bf16[16,8,1152]{2,1,0:T(8,128)(2,1)} %bitcast.4), calls=%async_computation | async-start | bytes 589824 | tf_op jit(solution)/shard_map/all_to_all | solution.py:231
  20.5 0.0 collective-permute-done.trans_ref
  20.6 0.0 copy-start.4
  20.6 0.9 copy-done.4
  21.5 0.3 diagonal.1.terms_ref
  21.7 9.3 %all-to-all-done.parts_ref = bf16[16,8,1152]{2,1,0:T(8,128)(2,1)S(1)} async-done(((bf16[16,8,1152]{2,1,0:T(8,128)(2,1)}), bf16[16,8,1152]{2,1,0:T(8,128)(2,1)S(1)}, u32[]{:S(2)}, u32[]{:S(2)}) %all-to-all-start) | async-done | bytes 294944 | tf_op jit(solution)/shard_map/all_to_all | solution.py:231
  31.1 1.2 %share.1 = bf16[64,8,1152]{2,1,0:T(8,128)(2,1)} custom-call(f32[8,128]{1,0:T(8,128)S(1)} %diagonal.1.terms_ref, bf16[16,8,1152]{2,1,0:T(8,128)(2,1)S(1)} %all-to-all-done.parts_ref), custom_call_target="tpu_custom_call" | custom-call | tf_op jit(solution)/shard_map/share/pallas_call | solution.py:241
  32.2 0.0 copy-start
  32.2 20.5 %all-to-all-start.1 = ((bf16[64,8,1152]{2,1,0:T(8,128)(2,1)}), bf16[64,8,1152]{2,1,0:T(8,128)(2,1)S(1)}, u32[]{:S(2)}, u32[]{:S(2)}) async-start(bf16[64,8,1152]{2,1,0:T(8,128)(2,1)} %share.1), calls=%async_computation.1 | async-start | bytes 2359296 | tf_op jit(solution)/shard_map/all_to_all | solution.py:250
  52.8 0.0 copy-done
  52.8 0.0 copy-start.1
  52.8 0.0 copy-start.2
  52.8 0.0 copy-start.3
  52.8 6.4 %collective-permute-start.1 = (bf16[512,128]{1,0:T(8,128)(2,1)S(1)}, bf16[512,128]{1,0:T(8,128)(2,1)S(1)}, u32[]{:S(2)}, u32[]{:S(2)}) collective-permute-start(bf16[512,128]{1,0:T(8,128)(2,1)S(1)} %copy-done), channel_id=1, source_target_pairs={{0,512},{64,576},{128,640},{192,704},{256,768},{320,832},{384,896}... | collective-permute-start | bytes 393224 | tf_op jit(solution)/shard_map/ppermute | solution.py:132
  59.2 3.2 %collective-permute-start.2 = (bf16[512,128]{1,0:T(8,128)(2,1)S(1)}, bf16[512,128]{1,0:T(8,128)(2,1)S(1)}, u32[]{:S(2)}, u32[]{:S(2)}) collective-permute-start(bf16[512,128]{1,0:T(8,128)(2,1)S(1)} %copy-done), channel_id=1, source_target_pairs={{0,768},{64,832},{128,896},{192,960},{256,0},{320,64},{384,128},{4... | collective-permute-start | bytes 393224 | tf_op jit(solution)/shard_map/ppermute | solution.py:132
  62.4 0.9 collective-permute-done.1
  63.4 6.6 %collective-permute-start.4 = (bf16[1024,128]{1,0:T(8,128)(2,1)S(1)}, bf16[1024,128]{1,0:T(8,128)(2,1)S(1)}, u32[]{:S(2)}, u32[]{:S(2)}) collective-permute-start(bf16[1024,128]{1,0:T(8,128)(2,1)S(1)} %get-tuple-element.12), channel_id=1, source_target_pairs={{0,896},{64,960},{128,0},{192,64},{256,128},{320,192},{384,256},{4... | collective-permute-start | bytes 786440 | tf_op jit(solution)/shard_map/ppermute | solution.py:132
  70.0 3.0 %collective-permute-start.3 = (bf16[512,128]{1,0:T(8,128)(2,1)S(1)}, bf16[512,128]{1,0:T(8,128)(2,1)S(1)}, u32[]{:S(2)}, u32[]{:S(2)}) collective-permute-start(bf16[512,128]{1,0:T(8,128)(2,1)S(1)} %copy-done), channel_id=1, source_target_pairs={{0,256},{64,320},{128,384},{192,448},{256,512},{320,576},{384,640}... | collective-permute-start | bytes 393224 | tf_op jit(solution)/shard_map/ppermute | solution.py:132
  72.9 3.4 %collective-permute-start.5 = (bf16[1024,128]{1,0:T(8,128)(2,1)S(1)}, bf16[1024,128]{1,0:T(8,128)(2,1)S(1)}, u32[]{:S(2)}, u32[]{:S(2)}) collective-permute-start(bf16[1024,128]{1,0:T(8,128)(2,1)S(1)} %get-tuple-element.12), channel_id=1, source_target_pairs={{0,128},{64,192},{128,256},{192,320},{256,384},{320,448},{384,512}... | collective-permute-start | bytes 786440 | tf_op jit(solution)/shard_map/ppermute | solution.py:132
  76.3 0.0 collective-permute-done.2
  76.3 1.8 %collective-permute-done.3 = bf16[512,128]{1,0:T(8,128)(2,1)S(1)} collective-permute-done((bf16[512,128]{1,0:T(8,128)(2,1)S(1)}, bf16[512,128]{1,0:T(8,128)(2,1)S(1)}, u32[]{:S(2)}, u32[]{:S(2)}) %collective-permute-start.3) | collective-permute-done | bytes 131104 | tf_op jit(solution)/shard_map/ppermute | solution.py:132
  78.2 0.0 collective-permute-done.4
  78.2 7.5 %collective-permute-done.5 = bf16[1024,128]{1,0:T(8,128)(2,1)S(1)} collective-permute-done((bf16[1024,128]{1,0:T(8,128)(2,1)S(1)}, bf16[1024,128]{1,0:T(8,128)(2,1)S(1)}, u32[]{:S(2)}, u32[]{:S(2)}) %collective-permute-start.5) | collective-permute-done | bytes 262176 | tf_op jit(solution)/shard_map/ppermute | solution.py:132
  85.8 2.9 %collective-permute-start.6 = (bf16[4096,128]{1,0:T(8,128)(2,1)S(1)}, bf16[4096,128]{1,0:T(8,128)(2,1)S(1)}, u32[]{:S(2)}, u32[]{:S(2)}) collective-permute-start(bf16[4096,128]{1,0:T(8,128)(2,1)S(1)} %constant_dynamic-update-slice_fusion.2.even_ref), channel_id=1, source_target_pairs={{0,64},{64,0},{128,192},{192,128},{256,320},{320,256},{384,448},{4... | collective-permute-start | bytes 3145736 | tf_op jit(solution)/shard_map/ppermute | solution.py:141
  88.7 2.3 %collective-permute-done.6.odd_ref = bf16[4096,128]{1,0:T(8,128)(2,1)S(1)} collective-permute-done((bf16[4096,128]{1,0:T(8,128)(2,1)S(1)}, bf16[4096,128]{1,0:T(8,128)(2,1)S(1)}, u32[]{:S(2)}, u32[]{:S(2)}) %collective-permute-start.6) | collective-permute-done | bytes 1048608 | tf_op jit(solution)/shard_map/ppermute | solution.py:141
  90.9 0.0 all-to-all-done.1
  91.0 0.0 copy-done.1
  91.0 0.0 copy-done.2
  91.0 0.0 copy-done.3
  91.0 4.2 %product.1 = (bf16[512,128]{1,0:T(8,128)(2,1)}, f32[1,128]{1,0:T(1,128)}) custom-call(s32[8,16]{1,0:T(8,128)S(1)} %copy-done.1, s32[8]{0:T(128)S(1)} %copy-done.2, s32[1,128]{1,0:T(1,128)S(1)} %copy-done.3, bf16[512,128]{1,0:T(8,128)(2,1)S(1)} %copy-done, bf16[512,1152]{1,0:T(8,128)(2,1)S(1)} %bitcast.3, ...), custom_call_target="tpu_custom_call" | custom-call | tf_op jit(solution)/shard_map/product/pallas_call | solution.py:251
  (6 shorter events, 0.2 us)
Async XLA Ops:
  2.8 17.7 %collective-permute-start = (bf16[512,128]{1,0:T(8,128)(2,1)}, bf16[512,128]{1,0:T(8,128)(2,1)S(1)}, u32[]{:S(2)}, u32[]{:S(2)}) collective-permute-start(bf16[512,128]{1,0:T(8,128)(2,1)} %get-tuple-element.7.strip_ref), channel_id=1, source_target_pairs={{0,0},{4,64},{8,128},{12,192},{16,256},{20,320},{24,384},{28,448},... | collective-permute-start | bytes 393224 | tf_op jit(solution)/shard_map/ppermute | solution.py:229
  9.1 21.9 %all-to-all-start = ((bf16[16,8,1152]{2,1,0:T(8,128)(2,1)}), bf16[16,8,1152]{2,1,0:T(8,128)(2,1)S(1)}, u32[]{:S(2)}, u32[]{:S(2)}) async-start(bf16[16,8,1152]{2,1,0:T(8,128)(2,1)} %bitcast.4), calls=%async_computation | async-start | bytes 589824 | tf_op jit(solution)/shard_map/all_to_all | solution.py:231
  20.6 0.9 copy-start.4
  32.2 20.5 %copy-start = (bf16[512,128]{1,0:T(8,128)(2,1)S(1)}, bf16[512,128]{1,0:T(8,128)(2,1)}, u32[]{:S(2)}) copy-start(bf16[512,128]{1,0:T(8,128)(2,1)} %get-tuple-element.7.strip_ref) | copy-start | bytes 393220
  32.2 58.7 %all-to-all-start.1 = ((bf16[64,8,1152]{2,1,0:T(8,128)(2,1)}), bf16[64,8,1152]{2,1,0:T(8,128)(2,1)S(1)}, u32[]{:S(2)}, u32[]{:S(2)}) async-start(bf16[64,8,1152]{2,1,0:T(8,128)(2,1)} %share.1), calls=%async_computation.1 | async-start | bytes 2359296 | tf_op jit(solution)/shard_map/all_to_all | solution.py:250
  52.8 38.2 %copy-start.1 = (s32[8,16]{1,0:T(8,128)S(1)}, s32[8,16]{1,0:T(8,128)}, u32[]{:S(2)}) copy-start(s32[8,16]{1,0:T(8,128)} %pat_ref.1) | copy-start | bytes 1540
  52.8 38.2 %copy-start.2 = (s32[8]{0:T(128)S(1)}, s32[8]{0:T(128)}, u32[]{:S(2)}) copy-start(s32[8]{0:T(128)} %flag_ref.1) | copy-start | bytes 100
  52.8 38.2 %copy-start.3 = (s32[1,128]{1,0:T(1,128)S(1)}, s32[1,128]{1,0:T(1,128)}, u32[]{:S(2)}) copy-start(s32[1,128]{1,0:T(1,128)} %count_ref.1) | copy-start | bytes 1540
  52.8 10.5 %collective-permute-start.1 = (bf16[512,128]{1,0:T(8,128)(2,1)S(1)}, bf16[512,128]{1,0:T(8,128)(2,1)S(1)}, u32[]{:S(2)}, u32[]{:S(2)}) collective-permute-start(bf16[512,128]{1,0:T(8,128)(2,1)S(1)} %copy-done), channel_id=1, source_target_pairs={{0,512},{64,576},{128,640},{192,704},{256,768},{320,832},{384,896}... | collective-permute-start | bytes 393224 | tf_op jit(solution)/shard_map/ppermute | solution.py:132
  59.2 17.1 %collective-permute-start.2 = (bf16[512,128]{1,0:T(8,128)(2,1)S(1)}, bf16[512,128]{1,0:T(8,128)(2,1)S(1)}, u32[]{:S(2)}, u32[]{:S(2)}) collective-permute-start(bf16[512,128]{1,0:T(8,128)(2,1)S(1)} %copy-done), channel_id=1, source_target_pairs={{0,768},{64,832},{128,896},{192,960},{256,0},{320,64},{384,128},{4... | collective-permute-start | bytes 393224 | tf_op jit(solution)/shard_map/ppermute | solution.py:132
  63.4 14.8 %collective-permute-start.4 = (bf16[1024,128]{1,0:T(8,128)(2,1)S(1)}, bf16[1024,128]{1,0:T(8,128)(2,1)S(1)}, u32[]{:S(2)}, u32[]{:S(2)}) collective-permute-start(bf16[1024,128]{1,0:T(8,128)(2,1)S(1)} %get-tuple-element.12), channel_id=1, source_target_pairs={{0,896},{64,960},{128,0},{192,64},{256,128},{320,192},{384,256},{4... | collective-permute-start | bytes 786440 | tf_op jit(solution)/shard_map/ppermute | solution.py:132
  70.0 8.2 %collective-permute-start.3 = (bf16[512,128]{1,0:T(8,128)(2,1)S(1)}, bf16[512,128]{1,0:T(8,128)(2,1)S(1)}, u32[]{:S(2)}, u32[]{:S(2)}) collective-permute-start(bf16[512,128]{1,0:T(8,128)(2,1)S(1)} %copy-done), channel_id=1, source_target_pairs={{0,256},{64,320},{128,384},{192,448},{256,512},{320,576},{384,640}... | collective-permute-start | bytes 393224 | tf_op jit(solution)/shard_map/ppermute | solution.py:132
  72.9 12.8 %collective-permute-start.5 = (bf16[1024,128]{1,0:T(8,128)(2,1)S(1)}, bf16[1024,128]{1,0:T(8,128)(2,1)S(1)}, u32[]{:S(2)}, u32[]{:S(2)}) collective-permute-start(bf16[1024,128]{1,0:T(8,128)(2,1)S(1)} %get-tuple-element.12), channel_id=1, source_target_pairs={{0,128},{64,192},{128,256},{192,320},{256,384},{320,448},{384,512}... | collective-permute-start | bytes 786440 | tf_op jit(solution)/shard_map/ppermute | solution.py:132
  85.8 5.2 %collective-permute-start.6 = (bf16[4096,128]{1,0:T(8,128)(2,1)S(1)}, bf16[4096,128]{1,0:T(8,128)(2,1)S(1)}, u32[]{:S(2)}, u32[]{:S(2)}) collective-permute-start(bf16[4096,128]{1,0:T(8,128)(2,1)S(1)} %constant_dynamic-update-slice_fusion.2.even_ref), channel_id=1, source_target_pairs={{0,64},{64,0},{128,192},{192,128},{256,320},{320,256},{384,448},{4... | collective-permute-start | bytes 3145736 | tf_op jit(solution)/shard_map/ppermute | solution.py:141

commit v7 on v6

--- a/solution.py
+++ b/solution.py
@@ -14,7 +14,7 @@
 F32 = jnp.float32
 BF16 = jnp.bfloat16
 PLACES = 0x63517240
-COST = 1 << 36
+COST = int(5.3e9)
 
 
 def lanes(rows, count):
@@ -224,11 +224,11 @@
         compiler_params=pltpu.CompilerParams(vmem_limit_bytes=60 << 20),
         name="pack",
     )(pattern, density)
-    across = from_chip(4, strip)
     swap = [(r * n_col + c, c * n_col + r) for r in range(n_row) for c in range(n_col)]
     trans = lax.ppermute(strip, ("row", "col"), swap)
     chunk = width // n_col
     parts = lax.all_to_all(slots.reshape(n_col, chunk, slots_wide), "col", 0, 0)
+    across = from_chip(4, strip)
     terms = pl.pallas_call(
         diagonal_kernel,
         out_shape=jax.ShapeDtypeStruct((8, width), F32),
@@ -246,6 +246,7 @@
         compiler_params=limit,
         name="share",
     )(terms, parts)
+    send, across = lax.optimization_barrier((send, across))
     held, other = gather_strip(strip, across)
     stripe = lax.all_to_all(send, ("depth", "col"), 0, 0).reshape(tile, slots_wide)
     updated, populations = pl.pallas_call(

time: 95.7 us -> 91.1 us (0.952)
  the two profiles are of different devices: /device:TPU:1 before, /device:TPU:14 now
where the time goes in v7:
time: 91.1 us; the launch traced here: 90.5 us
  starting transfers between devices  56.5 us (62%)
  waiting for transfers between devices  24.4 us (27%)
  Pallas kernels  7.77 us (9%)
  local copies, waits for them, and re-layouts  1.09 us (1%)
    all_to_all x1, starting transfers between devices, per_device(): lax.all_to_all(send, ('depth', 'col'), 0, 0).reshape(tile, slots_wide)  23.1 us
    ppermute x5, starting transfers between devices, from_chip(): lax.ppermute(value, 'row', [(s, (s - 2 * distance) % n_row) for s in rang...  17.7 us
    all_to_all x1, waiting for transfers between devices, per_device(): parts = lax.all_to_all(slots.reshape(n_col, chunk, slots_wide), 'col', 0, 0)  7.93 us
    all_to_all x1, starting transfers between devices, per_device(): parts = lax.all_to_all(slots.reshape(n_col, chunk, slots_wide), 'col', 0, 0)  7.8 us
    all_to_all x1, waiting for transfers between devices, per_device(): lax.all_to_all(send, ('depth', 'col'), 0, 0).reshape(tile, slots_wide)  6.92 us
    ppermute x5, waiting for transfers between devices, from_chip(): lax.ppermute(value, 'row', [(s, (s - 2 * distance) % n_row) for s in rang...  6.9 us
    ppermute x1, starting transfers between devices, per_device(): trans = lax.ppermute(strip, ('row', 'col'), swap)  5.97 us
    pallas_call x1, Pallas kernels, per_device(): pl.pallas_call(product_kernel, out_shape=(jax.ShapeDtypeStruct((tile, wid...  4.16 us
  transfers between devices with their start and end apart: 9, of which 6 were waited for; matrix products, arithmetic and copies ran while one was open for 0% of the time, Pallas kernels for 2%

profile of v7, /device:TPU:14, one launch (start us, length us, event | category | flops | bytes accessed | tf_op | source)
XLA Modules:
  0.0 90.5 jit_solution(15779296093989838855)
XLA Ops:
  0.6 2.2 %pack.1 = (bf16[512,128]{1,0:T(8,128)(2,1)}, bf16[128,512]{1,0:T(8,128)(2,1)}, bf16[128,1152]{1,0:T(8,128)(2,1)}) custom-call(s32[8,16]{1,0:T(8,128)} %pat_ref.1, bf16[512,512]{1,0:T(8,128)(2,1)} %dens_hbm.1), custom_call_target="tpu_custom_call" | custom-call | tf_op jit(solution)/shard_map/pack/pallas_call | solution.py:209
  2.8 6.0 %collective-permute-start = (bf16[512,128]{1,0:T(8,128)(2,1)}, bf16[512,128]{1,0:T(8,128)(2,1)S(1)}, u32[]{:S(2)}, u32[]{:S(2)}) collective-permute-start(bf16[512,128]{1,0:T(8,128)(2,1)} %get-tuple-element.9.strip_ref), channel_id=1, source_target_pairs={{0,0},{4,64},{8,128},{12,192},{16,256},{20,320},{24,384},{28,448},... | collective-permute-start | bytes 393224 | tf_op jit(solution)/shard_map/ppermute | solution.py:228
  8.8 7.8 %all-to-all-start = ((bf16[16,8,1152]{2,1,0:T(8,128)(2,1)}), bf16[16,8,1152]{2,1,0:T(8,128)(2,1)S(1)}, u32[]{:S(2)}, u32[]{:S(2)}) async-start(bf16[16,8,1152]{2,1,0:T(8,128)(2,1)} %bitcast.4), calls=%async_computation | async-start | bytes 589824 | tf_op jit(solution)/shard_map/all_to_all | solution.py:230
  16.6 3.8 %collective-permute-start.1 = (bf16[512,128]{1,0:T(8,128)(2,1)}, bf16[512,128]{1,0:T(8,128)(2,1)S(1)}, u32[]{:S(2)}, u32[]{:S(2)}) collective-permute-start(bf16[512,128]{1,0:T(8,128)(2,1)} %get-tuple-element.9.strip_ref), channel_id=1, source_target_pairs={{0,512},{64,576},{128,640},{192,704},{256,768},{320,832},{384,896}... | collective-permute-start | bytes 393224 | tf_op jit(solution)/shard_map/ppermute | solution.py:132
  20.4 0.0 collective-permute-done.trans_ref
  20.4 0.0 copy-start.4
  20.4 0.9 copy-done.4
  21.3 0.3 diagonal.1.terms_ref
  21.6 7.9 %all-to-all-done.parts_ref = bf16[16,8,1152]{2,1,0:T(8,128)(2,1)S(1)} async-done(((bf16[16,8,1152]{2,1,0:T(8,128)(2,1)}), bf16[16,8,1152]{2,1,0:T(8,128)(2,1)S(1)}, u32[]{:S(2)}, u32[]{:S(2)}) %all-to-all-start) | async-done | bytes 294944 | tf_op jit(solution)/shard_map/all_to_all | solution.py:230
  29.5 1.2 %share.1 = bf16[64,8,1152]{2,1,0:T(8,128)(2,1)} custom-call(f32[8,128]{1,0:T(8,128)S(1)} %diagonal.1.terms_ref, bf16[16,8,1152]{2,1,0:T(8,128)(2,1)S(1)} %all-to-all-done.parts_ref), custom_call_target="tpu_custom_call" | custom-call | tf_op jit(solution)/shard_map/share/pallas_call | solution.py:241
  30.6 0.0 copy-start
  30.6 0.0 collective-permute-done.1
  30.7 23.1 %all-to-all-start.1 = ((bf16[64,8,1152]{2,1,0:T(8,128)(2,1)}), bf16[64,8,1152]{2,1,0:T(8,128)(2,1)S(1)}, u32[]{:S(2)}, u32[]{:S(2)}) async-start(bf16[64,8,1152]{2,1,0:T(8,128)(2,1)} %share.1), calls=%async_computation.1 | async-start | bytes 2359296 | tf_op jit(solution)/shard_map/all_to_all | solution.py:251
  53.8 0.0 copy-done
  53.8 0.0 copy-start.1
  53.8 0.0 copy-start.2
  53.8 0.0 copy-start.3
  53.8 2.1 %collective-permute-start.2 = (bf16[512,128]{1,0:T(8,128)(2,1)S(1)}, bf16[512,128]{1,0:T(8,128)(2,1)S(1)}, u32[]{:S(2)}, u32[]{:S(2)}) collective-permute-start(bf16[512,128]{1,0:T(8,128)(2,1)S(1)} %copy-done), channel_id=1, source_target_pairs={{0,768},{64,832},{128,896},{192,960},{256,0},{320,64},{384,128},{4... | collective-permute-start | bytes 393224 | tf_op jit(solution)/shard_map/ppermute | solution.py:132
  56.0 2.9 %collective-permute-start.4 = (bf16[1024,128]{1,0:T(8,128)(2,1)S(1)}, bf16[1024,128]{1,0:T(8,128)(2,1)S(1)}, u32[]{:S(2)}, u32[]{:S(2)}) collective-permute-start(bf16[1024,128]{1,0:T(8,128)(2,1)S(1)} %get-tuple-element.16), channel_id=1, source_target_pairs={{0,896},{64,960},{128,0},{192,64},{256,128},{320,192},{384,256},{4... | collective-permute-start | bytes 786440 | tf_op jit(solution)/shard_map/ppermute | solution.py:132
  58.9 5.4 %collective-permute-start.3 = (bf16[512,128]{1,0:T(8,128)(2,1)S(1)}, bf16[512,128]{1,0:T(8,128)(2,1)S(1)}, u32[]{:S(2)}, u32[]{:S(2)}) collective-permute-start(bf16[512,128]{1,0:T(8,128)(2,1)S(1)} %copy-done), channel_id=1, source_target_pairs={{0,256},{64,320},{128,384},{192,448},{256,512},{320,576},{384,640}... | collective-permute-start | bytes 393224 | tf_op jit(solution)/shard_map/ppermute | solution.py:132
  64.3 3.6 %collective-permute-start.5 = (bf16[1024,128]{1,0:T(8,128)(2,1)S(1)}, bf16[1024,128]{1,0:T(8,128)(2,1)S(1)}, u32[]{:S(2)}, u32[]{:S(2)}) collective-permute-start(bf16[1024,128]{1,0:T(8,128)(2,1)S(1)} %get-tuple-element.16), channel_id=1, source_target_pairs={{0,128},{64,192},{128,256},{192,320},{256,384},{320,448},{384,512}... | collective-permute-start | bytes 786440 | tf_op jit(solution)/shard_map/ppermute | solution.py:132
  67.9 0.0 collective-permute-done.2
  67.9 1.7 %collective-permute-done.3 = bf16[512,128]{1,0:T(8,128)(2,1)S(1)} collective-permute-done((bf16[512,128]{1,0:T(8,128)(2,1)S(1)}, bf16[512,128]{1,0:T(8,128)(2,1)S(1)}, u32[]{:S(2)}, u32[]{:S(2)}) %collective-permute-start.3) | collective-permute-done | bytes 131104 | tf_op jit(solution)/shard_map/ppermute | solution.py:132
  69.6 0.9 %collective-permute-done.4 = bf16[1024,128]{1,0:T(8,128)(2,1)S(1)} collective-permute-done((bf16[1024,128]{1,0:T(8,128)(2,1)S(1)}, bf16[1024,128]{1,0:T(8,128)(2,1)S(1)}, u32[]{:S(2)}, u32[]{:S(2)}) %collective-permute-start.4) | collective-permute-done | bytes 262176 | tf_op jit(solution)/shard_map/ppermute | solution.py:132
  70.5 4.3 %collective-permute-done.5 = bf16[1024,128]{1,0:T(8,128)(2,1)S(1)} collective-permute-done((bf16[1024,128]{1,0:T(8,128)(2,1)S(1)}, bf16[1024,128]{1,0:T(8,128)(2,1)S(1)}, u32[]{:S(2)}, u32[]{:S(2)}) %collective-permute-start.5) | collective-permute-done | bytes 262176 | tf_op jit(solution)/shard_map/ppermute | solution.py:132
  74.9 1.9 %collective-permute-start.6 = (bf16[4096,128]{1,0:T(8,128)(2,1)S(1)}, bf16[4096,128]{1,0:T(8,128)(2,1)S(1)}, u32[]{:S(2)}, u32[]{:S(2)}) collective-permute-start(bf16[4096,128]{1,0:T(8,128)(2,1)S(1)} %constant_dynamic-update-slice_fusion.2.even_ref), channel_id=1, source_target_pairs={{0,64},{64,0},{128,192},{192,128},{256,320},{320,256},{384,448},{4... | collective-permute-start | bytes 3145736 | tf_op jit(solution)/shard_map/ppermute | solution.py:141
  76.8 2.6 %collective-permute-done.6.odd_ref = bf16[4096,128]{1,0:T(8,128)(2,1)S(1)} collective-permute-done((bf16[4096,128]{1,0:T(8,128)(2,1)S(1)}, bf16[4096,128]{1,0:T(8,128)(2,1)S(1)}, u32[]{:S(2)}, u32[]{:S(2)}) %collective-permute-start.6) | collective-permute-done | bytes 1048608 | tf_op jit(solution)/shard_map/ppermute | solution.py:141
  79.5 6.9 %all-to-all-done.1 = bf16[64,8,1152]{2,1,0:T(8,128)(2,1)S(1)} async-done(((bf16[64,8,1152]{2,1,0:T(8,128)(2,1)}), bf16[64,8,1152]{2,1,0:T(8,128)(2,1)S(1)}, u32[]{:S(2)}, u32[]{:S(2)}) %all-to-all-start.1) | async-done | bytes 1179680 | tf_op jit(solution)/shard_map/all_to_all | solution.py:251
  86.4 0.0 copy-done.1
  86.4 0.0 copy-done.2
  86.4 0.0 copy-done.3
  86.4 4.2 %product.1 = (bf16[512,128]{1,0:T(8,128)(2,1)}, f32[1,128]{1,0:T(1,128)}) custom-call(s32[8,16]{1,0:T(8,128)S(1)} %copy-done.1, s32[8]{0:T(128)S(1)} %copy-done.2, s32[1,128]{1,0:T(1,128)S(1)} %copy-done.3, bf16[512,128]{1,0:T(8,128)(2,1)S(1)} %copy-done, bf16[512,1152]{1,0:T(8,128)(2,1)S(1)} %bitcast.3, ...), custom_call_target="tpu_custom_call" | custom-call | tf_op jit(solution)/shard_map/product/pallas_call | solution.py:252
  (6 shorter events, 0.2 us)
Async XLA Ops:
  2.8 17.6 %collective-permute-start = (bf16[512,128]{1,0:T(8,128)(2,1)}, bf16[512,128]{1,0:T(8,128)(2,1)S(1)}, u32[]{:S(2)}, u32[]{:S(2)}) collective-permute-start(bf16[512,128]{1,0:T(8,128)(2,1)} %get-tuple-element.9.strip_ref), channel_id=1, source_target_pairs={{0,0},{4,64},{8,128},{12,192},{16,256},{20,320},{24,384},{28,448},... | collective-permute-start | bytes 393224 | tf_op jit(solution)/shard_map/ppermute | solution.py:228
  8.8 20.7 %all-to-all-start = ((bf16[16,8,1152]{2,1,0:T(8,128)(2,1)}), bf16[16,8,1152]{2,1,0:T(8,128)(2,1)S(1)}, u32[]{:S(2)}, u32[]{:S(2)}) async-start(bf16[16,8,1152]{2,1,0:T(8,128)(2,1)} %bitcast.4), calls=%async_computation | async-start | bytes 589824 | tf_op jit(solution)/shard_map/all_to_all | solution.py:230
  16.6 14.0 %collective-permute-start.1 = (bf16[512,128]{1,0:T(8,128)(2,1)}, bf16[512,128]{1,0:T(8,128)(2,1)S(1)}, u32[]{:S(2)}, u32[]{:S(2)}) collective-permute-start(bf16[512,128]{1,0:T(8,128)(2,1)} %get-tuple-element.9.strip_ref), channel_id=1, source_target_pairs={{0,512},{64,576},{128,640},{192,704},{256,768},{320,832},{384,896}... | collective-permute-start | bytes 393224 | tf_op jit(solution)/shard_map/ppermute | solution.py:132
  20.4 0.9 copy-start.4
  30.6 23.1 %copy-start = (bf16[512,128]{1,0:T(8,128)(2,1)S(1)}, bf16[512,128]{1,0:T(8,128)(2,1)}, u32[]{:S(2)}) copy-start(bf16[512,128]{1,0:T(8,128)(2,1)} %get-tuple-element.9.strip_ref) | copy-start | bytes 393220
  30.7 55.7 %all-to-all-start.1 = ((bf16[64,8,1152]{2,1,0:T(8,128)(2,1)}), bf16[64,8,1152]{2,1,0:T(8,128)(2,1)S(1)}, u32[]{:S(2)}, u32[]{:S(2)}) async-start(bf16[64,8,1152]{2,1,0:T(8,128)(2,1)} %share.1), calls=%async_computation.1 | async-start | bytes 2359296 | tf_op jit(solution)/shard_map/all_to_all | solution.py:251
  53.8 32.6 %copy-start.1 = (s32[8,16]{1,0:T(8,128)S(1)}, s32[8,16]{1,0:T(8,128)}, u32[]{:S(2)}) copy-start(s32[8,16]{1,0:T(8,128)} %pat_ref.1) | copy-start | bytes 1540
  53.8 32.6 %copy-start.2 = (s32[8]{0:T(128)S(1)}, s32[8]{0:T(128)}, u32[]{:S(2)}) copy-start(s32[8]{0:T(128)} %flag_ref.1) | copy-start | bytes 100
  53.8 32.6 %copy-start.3 = (s32[1,128]{1,0:T(1,128)S(1)}, s32[1,128]{1,0:T(1,128)}, u32[]{:S(2)}) copy-start(s32[1,128]{1,0:T(1,128)} %count_ref.1) | copy-start | bytes 1540
  53.8 14.0 %collective-permute-start.2 = (bf16[512,128]{1,0:T(8,128)(2,1)S(1)}, bf16[512,128]{1,0:T(8,128)(2,1)S(1)}, u32[]{:S(2)}, u32[]{:S(2)}) collective-permute-start(bf16[512,128]{1,0:T(8,128)(2,1)S(1)} %copy-done), channel_id=1, source_target_pairs={{0,768},{64,832},{128,896},{192,960},{256,0},{320,64},{384,128},{4... | collective-permute-start | bytes 393224 | tf_op jit(solution)/shard_map/ppermute | solution.py:132
  56.0 14.5 %collective-permute-start.4 = (bf16[1024,128]{1,0:T(8,128)(2,1)S(1)}, bf16[1024,128]{1,0:T(8,128)(2,1)S(1)}, u32[]{:S(2)}, u32[]{:S(2)}) collective-permute-start(bf16[1024,128]{1,0:T(8,128)(2,1)S(1)} %get-tuple-element.16), channel_id=1, source_target_pairs={{0,896},{64,960},{128,0},{192,64},{256,128},{320,192},{384,256},{4... | collective-permute-start | bytes 786440 | tf_op jit(solution)/shard_map/ppermute | solution.py:132
  58.9 10.7 %collective-permute-start.3 = (bf16[512,128]{1,0:T(8,128)(2,1)S(1)}, bf16[512,128]{1,0:T(8,128)(2,1)S(1)}, u32[]{:S(2)}, u32[]{:S(2)}) collective-permute-start(bf16[512,128]{1,0:T(8,128)(2,1)S(1)} %copy-done), channel_id=1, source_target_pairs={{0,256},{64,320},{128,384},{192,448},{256,512},{320,576},{384,640}... | collective-permute-start | bytes 393224 | tf_op jit(solution)/shard_map/ppermute | solution.py:132
  64.3 10.6 %collective-permute-start.5 = (bf16[1024,128]{1,0:T(8,128)(2,1)S(1)}, bf16[1024,128]{1,0:T(8,128)(2,1)S(1)}, u32[]{:S(2)}, u32[]{:S(2)}) collective-permute-start(bf16[1024,128]{1,0:T(8,128)(2,1)S(1)} %get-tuple-element.16), channel_id=1, source_target_pairs={{0,128},{64,192},{128,256},{192,320},{256,384},{320,448},{384,512}... | collective-permute-start | bytes 786440 | tf_op jit(solution)/shard_map/ppermute | solution.py:132
  74.9 4.6 %collective-permute-start.6 = (bf16[4096,128]{1,0:T(8,128)(2,1)S(1)}, bf16[4096,128]{1,0:T(8,128)(2,1)S(1)}, u32[]{:S(2)}, u32[]{:S(2)}) collective-permute-start(bf16[4096,128]{1,0:T(8,128)(2,1)S(1)} %constant_dynamic-update-slice_fusion.2.even_ref), channel_id=1, source_target_pairs={{0,64},{64,0},{128,192},{192,128},{256,320},{320,256},{384,448},{4... | collective-permute-start | bytes 3145736 | tf_op jit(solution)/shard_map/ppermute | solution.py:141

commit v8 on v7

--- a/solution.py
+++ b/solution.py
@@ -13,6 +13,7 @@
 HBM = pl.BlockSpec(memory_space=pltpu.HBM)
 F32 = jnp.float32
 BF16 = jnp.bfloat16
+GROUP = 4
 PLACES = 0x63517240
 COST = int(5.3e9)
 
@@ -141,20 +142,27 @@
     return held, lax.ppermute(held, "row", [(s, s ^ 1) for s in range(n_row)])
 
 
-def product_kernel(
-    pat_ref, flag_ref, count_ref, strip_ref, slots_ref, even_ref, odd_ref, out_ref, pop_ref, full, chosen, done
-):
+def plan_kernel(pat_ref, _, plan_ref):
     row, col, depth = (lax.axis_index(name) for name in ("row", "col", "depth"))
     n_rows, names = pat_ref.shape
+    blocks = n_rows // lax.axis_size("depth")
+    for i in range(n_rows):
+        own_block = row * n_rows + i
+        for slot in range(names + 1):
+            listed = own_block if slot == names else pat_ref[i, slot]
+            plan_ref[i, slot] = held_at(listed, row, n_rows) * BLOCK
+        plan_ref[i, names + 1] = block_bits(pat_ref, i, own_block, col * n_rows + depth * blocks, blocks)
+
+
+def product_kernel(
+    plan_ref, flag_ref, count_ref, strip_ref, slots_ref, even_ref, odd_ref, out_ref, pop_ref, full
+):
+    n_rows, slots = plan_ref.shape[0], plan_ref.shape[1] - 1
     width = strip_ref.shape[1]
-    first_col = col * n_rows
     which = lanes(BLOCK, width) // BLOCK
-    used = (names + 1) * BLOCK
     half = even_ref.shape[0]
-    even_copy = pltpu.make_async_copy(even_ref, full.at[pl.ds(0, half), :], done.at[0])
-    odd_copy = pltpu.make_async_copy(odd_ref, full.at[pl.ds(half, half), :], done.at[1])
-    even_copy.start()
-    odd_copy.start()
+    full[0:half, :] = even_ref[...]
+    full[half : 2 * half, :] = odd_ref[...]
     atoms = count_ref.shape[1]
     span = 2 * BLOCK
     wide = slots_ref.shape[1]
@@ -181,18 +189,16 @@
         ones, total, (((1,), (1,)), ((), ())), precision=lax.Precision.HIGHEST, preferred_element_type=F32
     )
     pop_ref[...] = sums[0:1]
-    even_copy.wait()
-    odd_copy.wait()
     for i in range(n_rows):
-        bits = block_bits(pat_ref, i, row * n_rows + i, first_col, n_rows)
-        keep = (lax.shift_right_logical(bits, depth * (width // BLOCK)) >> which) & 1
-        chosen[i, used:, :] = jnp.zeros_like(chosen[i, used:, :])
-        for slot in range(names + 1):
-            listed = row * n_rows + i if slot == names else pat_ref[i, slot]
-            source = pl.ds(pl.multiple_of(held_at(listed, row, n_rows) * BLOCK, BLOCK), BLOCK)
-            chosen[i, slot * BLOCK : (slot + 1) * BLOCK, :] = full[source, :]
         here = pl.ds(i * BLOCK, BLOCK)
-        squared = jnp.dot(slots_ref[here, :], chosen[i], preferred_element_type=F32)
+        squared = jnp.zeros((BLOCK, width), F32)
+        for first in range(0, slots, GROUP):
+            last = min(first + GROUP, slots)
+            starts = [pl.multiple_of(plan_ref[i, slot], BLOCK) for slot in range(first, last)]
+            chosen = jnp.concatenate([full[pl.ds(start, BLOCK), :] for start in starts], axis=0)
+            values = slots_ref[here, first * BLOCK : last * BLOCK]
+            squared = squared + jnp.dot(values, chosen, preferred_element_type=F32)
+        keep = (plan_ref[i, slots] >> which) & 1
         own = strip_ref[here, :].astype(F32)
         flag = jnp.broadcast_to(flag_ref[i], squared.shape)
         value = jnp.where(flag == 1, squared, 2.0 * own - squared)
@@ -249,6 +255,15 @@
     send, across = lax.optimization_barrier((send, across))
     held, other = gather_strip(strip, across)
     stripe = lax.all_to_all(send, ("depth", "col"), 0, 0).reshape(tile, slots_wide)
+    plan = pl.pallas_call(
+        plan_kernel,
+        out_shape=jax.ShapeDtypeStruct((n_rows, names + 2), jnp.int32),
+        in_specs=[SMEM, pl.BlockSpec(memory_space=pl.ANY)],
+        out_specs=SMEM,
+        compiler_params=limit,
+        cost_estimate=pl.CostEstimate(flops=1 << 31, bytes_accessed=1 << 12, transcendentals=0),
+        name="plan",
+    )(pattern, across)
     updated, populations = pl.pallas_call(
         product_kernel,
         out_shape=(
@@ -257,14 +272,10 @@
         ),
         in_specs=[SMEM, SMEM, VMEM, VMEM, VMEM, VMEM, VMEM],
         out_specs=(VMEM, VMEM),
-        scratch_shapes=[
-            pltpu.VMEM((n_row * tile, width), BF16),
-            pltpu.VMEM((n_rows, slots_wide, width), BF16),
-            pltpu.SemaphoreType.DMA((2,)),
-        ],
+        scratch_shapes=[pltpu.VMEM((n_row * tile, width), BF16)],
         compiler_params=limit,
         name="product",
-    )(pattern, branch_flag, orbital_counts, strip, stripe, held, other)
+    )(plan, branch_flag, orbital_counts, strip, stripe, held, other)
     return (updated, populations.reshape(-1))
 
 

time: 91.1 us -> 89.1 us (0.978)
  waiting for transfers between devices: 24.4 us -> 21 us
  Pallas kernels: 7.77 us -> 9.2 us
    pallas_call x0 -> x1, Pallas kernels: none -> 3.46 us  [per_device(): pl.pallas_call(plan_kernel, out_shape=jax.ShapeDtypeStruct((n_rows, names...]
    ppermute x1, waiting for transfers between devices: 2.63 us -> 0.01 us  [gather_strip(): return (held, lax.ppermute(held, 'row', [(s, s ^ 1) for s in range(n_row)]))]
    pallas_call x1, Pallas kernels: 4.16 us -> 2.14 us  [per_device(): pl.pallas_call(product_kernel, out_shape=(jax.ShapeDtypeStruct((tile, wid...]
  transfers between devices with their start and end apart: 9 -> 9, of which waited for: 6 -> 5; matrix products, arithmetic and copies ran while one was open for 0% -> 0% of each run, Pallas kernels for 2% -> 6%
where the time goes in v8:
time: 89.1 us; the launch traced here: 88.5 us
  starting transfers between devices  56.4 us (63%)
  waiting for transfers between devices  21 us (24%)
  Pallas kernels  9.2 us (10%)
  local copies, waits for them, and re-layouts  1.09 us (1%)
    all_to_all x1, starting transfers between devices, per_device(): lax.all_to_all(send, ('depth', 'col'), 0, 0).reshape(tile, slots_wide)  23.1 us
    ppermute x5, starting transfers between devices, from_chip(): lax.ppermute(value, 'row', [(s, (s - 2 * distance) % n_row) for s in rang...  17.6 us
    all_to_all x1, waiting for transfers between devices, per_device(): parts = lax.all_to_all(slots.reshape(n_col, chunk, slots_wide), 'col', 0, 0)  7.93 us
    all_to_all x1, starting transfers between devices, per_device(): parts = lax.all_to_all(slots.reshape(n_col, chunk, slots_wide), 'col', 0, 0)  7.8 us
    ppermute x5, waiting for transfers between devices, from_chip(): lax.ppermute(value, 'row', [(s, (s - 2 * distance) % n_row) for s in rang...  6.9 us
    all_to_all x1, waiting for transfers between devices, per_device(): lax.all_to_all(send, ('depth', 'col'), 0, 0).reshape(tile, slots_wide)  6.19 us
    ppermute x1, starting transfers between devices, per_device(): trans = lax.ppermute(strip, ('row', 'col'), swap)  5.97 us
    pallas_call x1, Pallas kernels, per_device(): pl.pallas_call(plan_kernel, out_shape=jax.ShapeDtypeStruct((n_rows, names...  3.46 us
  transfers between devices with their start and end apart: 9, of which 5 were waited for; matrix products, arithmetic and copies ran while one was open for 0% of the time, Pallas kernels for 6%

profile of v8, /device:TPU:14, one launch (start us, length us, event | category | flops | bytes accessed | tf_op | source)
XLA Modules:
  0.0 88.5 jit_solution(1816449333535764300)
XLA Ops:
  0.6 2.2 %pack.1 = (bf16[512,128]{1,0:T(8,128)(2,1)}, bf16[128,512]{1,0:T(8,128)(2,1)}, bf16[128,1152]{1,0:T(8,128)(2,1)}) custom-call(s32[8,16]{1,0:T(8,128)} %pat_ref.1, bf16[512,512]{1,0:T(8,128)(2,1)} %dens_hbm.1), custom_call_target="tpu_custom_call" | custom-call | tf_op jit(solution)/shard_map/pack/pallas_call | solution.py:215
  2.8 6.0 %collective-permute-start = (bf16[512,128]{1,0:T(8,128)(2,1)}, bf16[512,128]{1,0:T(8,128)(2,1)S(1)}, u32[]{:S(2)}, u32[]{:S(2)}) collective-permute-start(bf16[512,128]{1,0:T(8,128)(2,1)} %get-tuple-element.10.strip_ref), channel_id=1, source_target_pairs={{0,0},{4,64},{8,128},{12,192},{16,256},{20,320},{24,384},{28,448},... | collective-permute-start | bytes 393224 | tf_op jit(solution)/shard_map/ppermute | solution.py:234
  8.8 7.8 %all-to-all-start = ((bf16[16,8,1152]{2,1,0:T(8,128)(2,1)}), bf16[16,8,1152]{2,1,0:T(8,128)(2,1)S(1)}, u32[]{:S(2)}, u32[]{:S(2)}) async-start(bf16[16,8,1152]{2,1,0:T(8,128)(2,1)} %bitcast.4), calls=%async_computation | async-start | bytes 589824 | tf_op jit(solution)/shard_map/all_to_all | solution.py:236
  16.6 3.8 %collective-permute-start.1 = (bf16[512,128]{1,0:T(8,128)(2,1)}, bf16[512,128]{1,0:T(8,128)(2,1)S(1)}, u32[]{:S(2)}, u32[]{:S(2)}) collective-permute-start(bf16[512,128]{1,0:T(8,128)(2,1)} %get-tuple-element.10.strip_ref), channel_id=1, source_target_pairs={{0,512},{64,576},{128,640},{192,704},{256,768},{320,832},{384,896}... | collective-permute-start | bytes 393224 | tf_op jit(solution)/shard_map/ppermute | solution.py:133
  20.4 0.0 collective-permute-done.trans_ref
  20.4 0.0 copy-start.4
  20.4 0.9 %copy-done.4 = bf16[128,512]{1,0:T(8,128)(2,1)S(1)} copy-done((bf16[128,512]{1,0:T(8,128)(2,1)S(1)}, bf16[128,512]{1,0:T(8,128)(2,1)}, u32[]{:S(2)}) %copy-start.4) | copy-done | bytes 131096
  21.3 0.3 diagonal.1.terms_ref
  21.6 7.9 %all-to-all-done.parts_ref = bf16[16,8,1152]{2,1,0:T(8,128)(2,1)S(1)} async-done(((bf16[16,8,1152]{2,1,0:T(8,128)(2,1)}), bf16[16,8,1152]{2,1,0:T(8,128)(2,1)S(1)}, u32[]{:S(2)}, u32[]{:S(2)}) %all-to-all-start) | async-done | bytes 294944 | tf_op jit(solution)/shard_map/all_to_all | solution.py:236
  29.5 1.2 %share.1 = bf16[64,8,1152]{2,1,0:T(8,128)(2,1)} custom-call(f32[8,128]{1,0:T(8,128)S(1)} %diagonal.1.terms_ref, bf16[16,8,1152]{2,1,0:T(8,128)(2,1)S(1)} %all-to-all-done.parts_ref), custom_call_target="tpu_custom_call" | custom-call | tf_op jit(solution)/shard_map/share/pallas_call | solution.py:247
  30.6 0.0 collective-permute-done.1._
  30.7 23.1 %all-to-all-start.1 = ((bf16[64,8,1152]{2,1,0:T(8,128)(2,1)}), bf16[64,8,1152]{2,1,0:T(8,128)(2,1)S(1)}, u32[]{:S(2)}, u32[]{:S(2)}) async-start(bf16[64,8,1152]{2,1,0:T(8,128)(2,1)} %share.1), calls=%async_computation.1 | async-start | bytes 2359296 | tf_op jit(solution)/shard_map/all_to_all | solution.py:257
  53.8 0.0 copy-done
  53.8 0.0 copy-start.1
  53.8 1.9 %collective-permute-start.2 = (bf16[512,128]{1,0:T(8,128)(2,1)S(1)}, bf16[512,128]{1,0:T(8,128)(2,1)S(1)}, u32[]{:S(2)}, u32[]{:S(2)}) collective-permute-start(bf16[512,128]{1,0:T(8,128)(2,1)S(1)} %copy-done), channel_id=1, source_target_pairs={{0,768},{64,832},{128,896},{192,960},{256,0},{320,64},{384,128},{4... | collective-permute-start | bytes 393224 | tf_op jit(solution)/shard_map/ppermute | solution.py:133
  55.8 2.9 %collective-permute-start.4 = (bf16[1024,128]{1,0:T(8,128)(2,1)S(1)}, bf16[1024,128]{1,0:T(8,128)(2,1)S(1)}, u32[]{:S(2)}, u32[]{:S(2)}) collective-permute-start(bf16[1024,128]{1,0:T(8,128)(2,1)S(1)} %get-tuple-element.16), channel_id=1, source_target_pairs={{0,896},{64,960},{128,0},{192,64},{256,128},{320,192},{384,256},{4... | collective-permute-start | bytes 786440 | tf_op jit(solution)/shard_map/ppermute | solution.py:133
  58.7 5.4 %collective-permute-start.3 = (bf16[512,128]{1,0:T(8,128)(2,1)S(1)}, bf16[512,128]{1,0:T(8,128)(2,1)S(1)}, u32[]{:S(2)}, u32[]{:S(2)}) collective-permute-start(bf16[512,128]{1,0:T(8,128)(2,1)S(1)} %copy-done), channel_id=1, source_target_pairs={{0,256},{64,320},{128,384},{192,448},{256,512},{320,576},{384,640}... | collective-permute-start | bytes 393224 | tf_op jit(solution)/shard_map/ppermute | solution.py:133
  64.1 3.6 %collective-permute-start.5 = (bf16[1024,128]{1,0:T(8,128)(2,1)S(1)}, bf16[1024,128]{1,0:T(8,128)(2,1)S(1)}, u32[]{:S(2)}, u32[]{:S(2)}) collective-permute-start(bf16[1024,128]{1,0:T(8,128)(2,1)S(1)} %get-tuple-element.16), channel_id=1, source_target_pairs={{0,128},{64,192},{128,256},{192,320},{256,384},{320,448},{384,512}... | collective-permute-start | bytes 786440 | tf_op jit(solution)/shard_map/ppermute | solution.py:133
  67.7 0.0 collective-permute-done.2
  67.7 1.7 %collective-permute-done.3 = bf16[512,128]{1,0:T(8,128)(2,1)S(1)} collective-permute-done((bf16[512,128]{1,0:T(8,128)(2,1)S(1)}, bf16[512,128]{1,0:T(8,128)(2,1)S(1)}, u32[]{:S(2)}, u32[]{:S(2)}) %collective-permute-start.3) | collective-permute-done | bytes 131104 | tf_op jit(solution)/shard_map/ppermute | solution.py:133
  69.4 0.9 %collective-permute-done.4 = bf16[1024,128]{1,0:T(8,128)(2,1)S(1)} collective-permute-done((bf16[1024,128]{1,0:T(8,128)(2,1)S(1)}, bf16[1024,128]{1,0:T(8,128)(2,1)S(1)}, u32[]{:S(2)}, u32[]{:S(2)}) %collective-permute-start.4) | collective-permute-done | bytes 262176 | tf_op jit(solution)/shard_map/ppermute | solution.py:133
  70.4 4.3 %collective-permute-done.5 = bf16[1024,128]{1,0:T(8,128)(2,1)S(1)} collective-permute-done((bf16[1024,128]{1,0:T(8,128)(2,1)S(1)}, bf16[1024,128]{1,0:T(8,128)(2,1)S(1)}, u32[]{:S(2)}, u32[]{:S(2)}) %collective-permute-start.5) | collective-permute-done | bytes 262176 | tf_op jit(solution)/shard_map/ppermute | solution.py:133
  74.7 0.0 copy-start.2
  74.8 0.0 copy-start.3
  74.8 1.9 %collective-permute-start.6 = (bf16[4096,128]{1,0:T(8,128)(2,1)S(1)}, bf16[4096,128]{1,0:T(8,128)(2,1)S(1)}, u32[]{:S(2)}, u32[]{:S(2)}) collective-permute-start(bf16[4096,128]{1,0:T(8,128)(2,1)S(1)} %constant_dynamic-update-slice_fusion.2.even_ref), channel_id=1, source_target_pairs={{0,64},{64,0},{128,192},{192,128},{256,320},{320,256},{384,448},{4... | collective-permute-start | bytes 3145736 | tf_op jit(solution)/shard_map/ppermute | solution.py:142
  76.7 0.0 copy-done.1
  76.7 3.5 %plan.1.plan_ref = s32[8,18]{1,0:T(8,128)S(1)} custom-call(s32[8,16]{1,0:T(8,128)S(1)} %copy-done.1, bf16[512,128]{1,0:T(8,128)(2,1)S(1)} %collective-permute-done.1._), custom_call_target="tpu_custom_call" | custom-call | flops 2147483648 | bytes 4096 | tf_op jit(solution)/shard_map/plan/pallas_call | solution.py:258
  80.2 0.0 collective-permute-done.6.odd_ref
  80.2 6.2 %all-to-all-done.1 = bf16[64,8,1152]{2,1,0:T(8,128)(2,1)S(1)} async-done(((bf16[64,8,1152]{2,1,0:T(8,128)(2,1)}), bf16[64,8,1152]{2,1,0:T(8,128)(2,1)S(1)}, u32[]{:S(2)}, u32[]{:S(2)}) %all-to-all-start.1) | async-done | bytes 1179680 | tf_op jit(solution)/shard_map/all_to_all | solution.py:257
  86.4 0.0 copy-done.2
  86.4 0.0 copy-done.3
  86.4 2.1 %product.1 = (bf16[512,128]{1,0:T(8,128)(2,1)}, f32[1,128]{1,0:T(1,128)}) custom-call(s32[8,18]{1,0:T(8,128)S(1)} %plan.1.plan_ref, s32[8]{0:T(128)S(1)} %copy-done.2, s32[1,128]{1,0:T(1,128)S(1)} %copy-done.3, bf16[512,128]{1,0:T(8,128)(2,1)S(1)} %copy-done, bf16[512,1152]{1,0:T(8,128)(2,1)S(1)} %bitcast.3, ...), custom_call_target="tpu_custom_call" | custom-call | tf_op jit(solution)/shard_map/product/pallas_call | solution.py:267
  (7 shorter events, 0.2 us)
Async XLA Ops:
  2.8 17.6 %collective-permute-start = (bf16[512,128]{1,0:T(8,128)(2,1)}, bf16[512,128]{1,0:T(8,128)(2,1)S(1)}, u32[]{:S(2)}, u32[]{:S(2)}) collective-permute-start(bf16[512,128]{1,0:T(8,128)(2,1)} %get-tuple-element.10.strip_ref), channel_id=1, source_target_pairs={{0,0},{4,64},{8,128},{12,192},{16,256},{20,320},{24,384},{28,448},... | collective-permute-start | bytes 393224 | tf_op jit(solution)/shard_map/ppermute | solution.py:234
  8.8 20.7 %all-to-all-start = ((bf16[16,8,1152]{2,1,0:T(8,128)(2,1)}), bf16[16,8,1152]{2,1,0:T(8,128)(2,1)S(1)}, u32[]{:S(2)}, u32[]{:S(2)}) async-start(bf16[16,8,1152]{2,1,0:T(8,128)(2,1)} %bitcast.4), calls=%async_computation | async-start | bytes 589824 | tf_op jit(solution)/shard_map/all_to_all | solution.py:236
  16.6 14.0 %collective-permute-start.1 = (bf16[512,128]{1,0:T(8,128)(2,1)}, bf16[512,128]{1,0:T(8,128)(2,1)S(1)}, u32[]{:S(2)}, u32[]{:S(2)}) collective-permute-start(bf16[512,128]{1,0:T(8,128)(2,1)} %get-tuple-element.10.strip_ref), channel_id=1, source_target_pairs={{0,512},{64,576},{128,640},{192,704},{256,768},{320,832},{384,896}... | collective-permute-start | bytes 393224 | tf_op jit(solution)/shard_map/ppermute | solution.py:133
  20.4 0.9 %copy-start.4 = (bf16[128,512]{1,0:T(8,128)(2,1)S(1)}, bf16[128,512]{1,0:T(8,128)(2,1)}, u32[]{:S(2)}) copy-start(bf16[128,512]{1,0:T(8,128)(2,1)} %get-tuple-element.9.rows_ref) | copy-start | bytes 393220
  30.6 23.1 %copy-start = (bf16[512,128]{1,0:T(8,128)(2,1)S(1)}, bf16[512,128]{1,0:T(8,128)(2,1)}, u32[]{:S(2)}) copy-start(bf16[512,128]{1,0:T(8,128)(2,1)} %get-tuple-element.10.strip_ref) | copy-start | bytes 393220
  30.7 55.7 %all-to-all-start.1 = ((bf16[64,8,1152]{2,1,0:T(8,128)(2,1)}), bf16[64,8,1152]{2,1,0:T(8,128)(2,1)S(1)}, u32[]{:S(2)}, u32[]{:S(2)}) async-start(bf16[64,8,1152]{2,1,0:T(8,128)(2,1)} %share.1), calls=%async_computation.1 | async-start | bytes 2359296 | tf_op jit(solution)/shard_map/all_to_all | solution.py:257
  53.8 22.9 %copy-start.1 = (s32[8,16]{1,0:T(8,128)S(1)}, s32[8,16]{1,0:T(8,128)}, u32[]{:S(2)}) copy-start(s32[8,16]{1,0:T(8,128)} %pat_ref.1) | copy-start | bytes 1540
  53.8 13.9 %collective-permute-start.2 = (bf16[512,128]{1,0:T(8,128)(2,1)S(1)}, bf16[512,128]{1,0:T(8,128)(2,1)S(1)}, u32[]{:S(2)}, u32[]{:S(2)}) collective-permute-start(bf16[512,128]{1,0:T(8,128)(2,1)S(1)} %copy-done), channel_id=1, source_target_pairs={{0,768},{64,832},{128,896},{192,960},{256,0},{320,64},{384,128},{4... | collective-permute-start | bytes 393224 | tf_op jit(solution)/shard_map/ppermute | solution.py:133
  55.8 14.5 %collective-permute-start.4 = (bf16[1024,128]{1,0:T(8,128)(2,1)S(1)}, bf16[1024,128]{1,0:T(8,128)(2,1)S(1)}, u32[]{:S(2)}, u32[]{:S(2)}) collective-permute-start(bf16[1024,128]{1,0:T(8,128)(2,1)S(1)} %get-tuple-element.16), channel_id=1, source_target_pairs={{0,896},{64,960},{128,0},{192,64},{256,128},{320,192},{384,256},{4... | collective-permute-start | bytes 786440 | tf_op jit(solution)/shard_map/ppermute | solution.py:133
  58.7 10.7 %collective-permute-start.3 = (bf16[512,128]{1,0:T(8,128)(2,1)S(1)}, bf16[512,128]{1,0:T(8,128)(2,1)S(1)}, u32[]{:S(2)}, u32[]{:S(2)}) collective-permute-start(bf16[512,128]{1,0:T(8,128)(2,1)S(1)} %copy-done), channel_id=1, source_target_pairs={{0,256},{64,320},{128,384},{192,448},{256,512},{320,576},{384,640}... | collective-permute-start | bytes 393224 | tf_op jit(solution)/shard_map/ppermute | solution.py:133
  64.1 10.6 %collective-permute-start.5 = (bf16[1024,128]{1,0:T(8,128)(2,1)S(1)}, bf16[1024,128]{1,0:T(8,128)(2,1)S(1)}, u32[]{:S(2)}, u32[]{:S(2)}) collective-permute-start(bf16[1024,128]{1,0:T(8,128)(2,1)S(1)} %get-tuple-element.16), channel_id=1, source_target_pairs={{0,128},{64,192},{128,256},{192,320},{256,384},{320,448},{384,512}... | collective-permute-start | bytes 786440 | tf_op jit(solution)/shard_map/ppermute | solution.py:133
  74.7 11.6 %copy-start.2 = (s32[8]{0:T(128)S(1)}, s32[8]{0:T(128)}, u32[]{:S(2)}) copy-start(s32[8]{0:T(128)} %flag_ref.1) | copy-start | bytes 100
  74.8 11.6 %copy-start.3 = (s32[1,128]{1,0:T(1,128)S(1)}, s32[1,128]{1,0:T(1,128)}, u32[]{:S(2)}) copy-start(s32[1,128]{1,0:T(1,128)} %count_ref.1) | copy-start | bytes 1540
  74.8 5.4 %collective-permute-start.6 = (bf16[4096,128]{1,0:T(8,128)(2,1)S(1)}, bf16[4096,128]{1,0:T(8,128)(2,1)S(1)}, u32[]{:S(2)}, u32[]{:S(2)}) collective-permute-start(bf16[4096,128]{1,0:T(8,128)(2,1)S(1)} %constant_dynamic-update-slice_fusion.2.even_ref), channel_id=1, source_target_pairs={{0,64},{64,0},{128,192},{192,128},{256,320},{320,256},{384,448},{4... | collective-permute-start | bytes 3145736 | tf_op jit(solution)/shard_map/ppermute | solution.py:142

commit v9 on v8

--- a/solution.py
+++ b/solution.py
@@ -16,6 +16,7 @@
 GROUP = 4
 PLACES = 0x63517240
 COST = int(5.3e9)
+PAIR_COST = 1 << 33
 
 
 def lanes(rows, count):
@@ -133,9 +134,24 @@
     return lax.ppermute(value, "row", [(s, (s - 2 * distance) % n_row) for s in range(n_row)])
 
 
+def pair_kernel(own_ref, other_ref, pair_ref):
+    rows = own_ref.shape[0]
+    pair_ref[0:rows, :] = own_ref[...]
+    pair_ref[rows : 2 * rows, :] = other_ref[...]
+
+
 def gather_strip(strip, across):
     n_row = lax.axis_size("row")
-    pair = jnp.concatenate([strip, across], axis=0)
+    rows, width = strip.shape
+    pair = pl.pallas_call(
+        pair_kernel,
+        out_shape=jax.ShapeDtypeStruct((2 * rows, width), strip.dtype),
+        in_specs=[VMEM, VMEM],
+        out_specs=VMEM,
+        compiler_params=pltpu.CompilerParams(vmem_limit_bytes=24 << 20),
+        cost_estimate=pl.CostEstimate(flops=PAIR_COST, bytes_accessed=1 << 19, transcendentals=0),
+        name="pair",
+    )(strip, across)
     above, below = from_chip(1, pair), from_chip(-1, pair)
     second, sixth = from_chip(2, strip), from_chip(-2, strip)
     held = jnp.concatenate([pair, second, sixth, above, below], axis=0)
@@ -146,12 +162,16 @@
     row, col, depth = (lax.axis_index(name) for name in ("row", "col", "depth"))
     n_rows, names = pat_ref.shape
     blocks = n_rows // lax.axis_size("depth")
-    for i in range(n_rows):
-        own_block = row * n_rows + i
-        for slot in range(names + 1):
-            listed = own_block if slot == names else pat_ref[i, slot]
-            plan_ref[i, slot] = held_at(listed, row, n_rows) * BLOCK
-        plan_ref[i, names + 1] = block_bits(pat_ref, i, own_block, col * n_rows + depth * blocks, blocks)
+    listed = pat_ref[...]
+    own = row * n_rows + lax.broadcasted_iota(jnp.int32, (n_rows, 1), 0)
+    bits = jnp.zeros((n_rows, 1), jnp.int32)
+    for j in range(blocks):
+        block = col * n_rows + depth * blocks + j
+        hits = jnp.max(jnp.where(listed == block, 1, 0), axis=1, keepdims=True)
+        bits = bits + jnp.where((hits == 1) | (own == block), 1 << j, 0)
+    plan_ref[:, 0:names] = held_at(listed, row, n_rows) * BLOCK
+    plan_ref[:, names : names + 1] = held_at(own, row, n_rows) * BLOCK
+    plan_ref[:, names + 1 : names + 2] = bits
 
 
 def product_kernel(
@@ -252,14 +272,13 @@
         compiler_params=limit,
         name="share",
     )(terms, parts)
-    send, across = lax.optimization_barrier((send, across))
     held, other = gather_strip(strip, across)
     stripe = lax.all_to_all(send, ("depth", "col"), 0, 0).reshape(tile, slots_wide)
     plan = pl.pallas_call(
         plan_kernel,
         out_shape=jax.ShapeDtypeStruct((n_rows, names + 2), jnp.int32),
-        in_specs=[SMEM, pl.BlockSpec(memory_space=pl.ANY)],
-        out_specs=SMEM,
+        in_specs=[VMEM, pl.BlockSpec(memory_space=pl.ANY)],
+        out_specs=VMEM,
         compiler_params=limit,
         cost_estimate=pl.CostEstimate(flops=1 << 31, bytes_accessed=1 << 12, transcendentals=0),
         name="plan",

time: 89.1 us -> 89.4 us (level)
  the two profiles are of different devices: /device:TPU:14 before, /device:TPU:6 now
where the time goes in v9:
time: 89.4 us; the launch traced here: 88.9 us
  starting transfers between devices  57.6 us (64%)
  waiting for transfers between devices  23.5 us (26%)
  Pallas kernels  5.93 us (7%)
  local copies, waits for them, and re-layouts  1.05 us (1%)
    all_to_all x1, starting transfers between devices, per_device(): lax.all_to_all(send, ('depth', 'col'), 0, 0).reshape(tile, slots_wide)  22.2 us
    ppermute x5, starting transfers between devices, from_chip(): lax.ppermute(value, 'row', [(s, (s - 2 * distance) % n_row) for s in rang...  21 us
    all_to_all x1, waiting for transfers between devices, per_device(): lax.all_to_all(send, ('depth', 'col'), 0, 0).reshape(tile, slots_wide)  15.8 us
    all_to_all x1, starting transfers between devices, per_device(): parts = lax.all_to_all(slots.reshape(n_col, chunk, slots_wide), 'col', 0, 0)  6.71 us
    ppermute x1, starting transfers between devices, per_device(): trans = lax.ppermute(strip, ('row', 'col'), swap)  5.77 us
    ppermute x5, waiting for transfers between devices, from_chip(): lax.ppermute(value, 'row', [(s, (s - 2 * distance) % n_row) for s in rang...  5.24 us
    ppermute x1, waiting for transfers between devices, gather_strip(): return (held, lax.ppermute(held, 'row', [(s, s ^ 1) for s in range(n_row)]))  2.44 us
    pallas_call x1, Pallas kernels, per_device(): pl.pallas_call(pack_kernel, out_shape=(jax.ShapeDtypeStruct((tile, width)...  2.19 us
  transfers between devices with their start and end apart: 9, of which 4 were waited for; matrix products, arithmetic and copies ran while one was open for 0% of the time, Pallas kernels for 2%

profile of v9, /device:TPU:6, one launch (start us, length us, event | category | flops | bytes accessed | tf_op | source)
XLA Modules:
  0.0 88.9 jit_solution(15570531559794024496)
XLA Ops:
  0.6 2.2 %pack.1 = (bf16[512,128]{1,0:T(8,128)(2,1)}, bf16[128,512]{1,0:T(8,128)(2,1)}, bf16[128,1152]{1,0:T(8,128)(2,1)}) custom-call(s32[8,16]{1,0:T(8,128)} %pat_ref.1, bf16[512,512]{1,0:T(8,128)(2,1)} %dens_hbm.1), custom_call_target="tpu_custom_call" | custom-call | tf_op jit(solution)/shard_map/pack/pallas_call | solution.py:235
  2.8 5.8 %collective-permute-start.1 = (bf16[512,128]{1,0:T(8,128)(2,1)}, bf16[512,128]{1,0:T(8,128)(2,1)S(1)}, u32[]{:S(2)}, u32[]{:S(2)}) collective-permute-start(bf16[512,128]{1,0:T(8,128)(2,1)} %get-tuple-element.7.own_ref.strip_ref), channel_id=1, source_target_pairs={{0,0},{4,64},{8,128},{12,192},{16,256},{20,320},{24,384},{28,448},... | collective-permute-start | bytes 393224 | tf_op jit(solution)/shard_map/ppermute | solution.py:254
  8.6 6.7 %all-to-all-start = ((bf16[16,8,1152]{2,1,0:T(8,128)(2,1)}), bf16[16,8,1152]{2,1,0:T(8,128)(2,1)S(1)}, u32[]{:S(2)}, u32[]{:S(2)}) async-start(bf16[16,8,1152]{2,1,0:T(8,128)(2,1)} %bitcast.4), calls=%async_computation | async-start | bytes 589824 | tf_op jit(solution)/shard_map/all_to_all | solution.py:256
  15.3 6.0 %collective-permute-start = (bf16[512,128]{1,0:T(8,128)(2,1)}, bf16[512,128]{1,0:T(8,128)(2,1)S(1)}, u32[]{:S(2)}, u32[]{:S(2)}) collective-permute-start(bf16[512,128]{1,0:T(8,128)(2,1)} %get-tuple-element.7.own_ref.strip_ref), channel_id=1, source_target_pairs={{0,512},{64,576},{128,640},{192,704},{256,768},{320,832},{384,896}... | collective-permute-start | bytes 393224 | tf_op jit(solution)/shard_map/ppermute | solution.py:134
  21.3 2.7 %collective-permute-start.2 = (bf16[512,128]{1,0:T(8,128)(2,1)}, bf16[512,128]{1,0:T(8,128)(2,1)S(1)}, u32[]{:S(2)}, u32[]{:S(2)}) collective-permute-start(bf16[512,128]{1,0:T(8,128)(2,1)} %get-tuple-element.7.own_ref.strip_ref), channel_id=1, source_target_pairs={{0,768},{64,832},{128,896},{192,960},{256,0},{320,64},{384,128},{4... | collective-permute-start | bytes 393224 | tf_op jit(solution)/shard_map/ppermute | solution.py:134
  24.1 5.2 %collective-permute-start.3 = (bf16[512,128]{1,0:T(8,128)(2,1)}, bf16[512,128]{1,0:T(8,128)(2,1)S(1)}, u32[]{:S(2)}, u32[]{:S(2)}) collective-permute-start(bf16[512,128]{1,0:T(8,128)(2,1)} %get-tuple-element.7.own_ref.strip_ref), channel_id=1, source_target_pairs={{0,256},{64,320},{128,384},{192,448},{256,512},{320,576},{384,640}... | collective-permute-start | bytes 393224 | tf_op jit(solution)/shard_map/ppermute | solution.py:134
  29.3 0.0 collective-permute-done.1.trans_ref
  29.3 0.0 copy-start.4
  29.3 0.9 %copy-done.4 = bf16[128,512]{1,0:T(8,128)(2,1)S(1)} copy-done((bf16[128,512]{1,0:T(8,128)(2,1)S(1)}, bf16[128,512]{1,0:T(8,128)(2,1)}, u32[]{:S(2)}) %copy-start.4) | copy-done | bytes 131096
  30.2 0.3 diagonal.1.terms_ref
  30.5 0.0 all-to-all-done.parts_ref
  30.5 1.1 %share.1 = bf16[64,8,1152]{2,1,0:T(8,128)(2,1)} custom-call(f32[8,128]{1,0:T(8,128)S(1)} %diagonal.1.terms_ref, bf16[16,8,1152]{2,1,0:T(8,128)(2,1)S(1)} %all-to-all-done.parts_ref), custom_call_target="tpu_custom_call" | custom-call | tf_op jit(solution)/shard_map/share/pallas_call | solution.py:267
  31.6 22.2 %all-to-all-start.1 = ((bf16[64,8,1152]{2,1,0:T(8,128)(2,1)}), bf16[64,8,1152]{2,1,0:T(8,128)(2,1)S(1)}, u32[]{:S(2)}, u32[]{:S(2)}) async-start(bf16[64,8,1152]{2,1,0:T(8,128)(2,1)} %share.1), calls=%async_computation.1 | async-start | bytes 2359296 | tf_op jit(solution)/shard_map/all_to_all | solution.py:276
  53.8 0.0 collective-permute-done._.other_ref
  53.8 0.0 copy-done
  53.8 0.0 copy-start.1
  53.9 2.2 %collective-permute-start.4 = (bf16[1024,128]{1,0:T(8,128)(2,1)S(1)}, bf16[1024,128]{1,0:T(8,128)(2,1)S(1)}, u32[]{:S(2)}, u32[]{:S(2)}) collective-permute-start(bf16[1024,128]{1,0:T(8,128)(2,1)S(1)} %pair.1), channel_id=1, source_target_pairs={{0,896},{64,960},{128,0},{192,64},{256,128},{320,192},{384,256},{4... | collective-permute-start | bytes 786440 | tf_op jit(solution)/shard_map/ppermute | solution.py:134
  56.1 4.8 %collective-permute-start.5 = (bf16[1024,128]{1,0:T(8,128)(2,1)S(1)}, bf16[1024,128]{1,0:T(8,128)(2,1)S(1)}, u32[]{:S(2)}, u32[]{:S(2)}) collective-permute-start(bf16[1024,128]{1,0:T(8,128)(2,1)S(1)} %pair.1), channel_id=1, source_target_pairs={{0,128},{64,192},{128,256},{192,320},{256,384},{320,448},{384,512}... | collective-permute-start | bytes 786440 | tf_op jit(solution)/shard_map/ppermute | solution.py:134
  61.0 0.0 collective-permute-done.2
  61.0 0.0 collective-permute-done.3
  61.0 4.1 %collective-permute-done.4 = bf16[1024,128]{1,0:T(8,128)(2,1)S(1)} collective-permute-done((bf16[1024,128]{1,0:T(8,128)(2,1)S(1)}, bf16[1024,128]{1,0:T(8,128)(2,1)S(1)}, u32[]{:S(2)}, u32[]{:S(2)}) %collective-permute-start.4) | collective-permute-done | bytes 262176 | tf_op jit(solution)/shard_map/ppermute | solution.py:134
  65.1 1.2 %collective-permute-done.5 = bf16[1024,128]{1,0:T(8,128)(2,1)S(1)} collective-permute-done((bf16[1024,128]{1,0:T(8,128)(2,1)S(1)}, bf16[1024,128]{1,0:T(8,128)(2,1)S(1)}, u32[]{:S(2)}, u32[]{:S(2)}) %collective-permute-start.5) | collective-permute-done | bytes 262176 | tf_op jit(solution)/shard_map/ppermute | solution.py:134
  66.3 0.0 copy-start.2
  66.3 0.0 copy-start.3
  66.4 1.9 %collective-permute-start.6 = (bf16[4096,128]{1,0:T(8,128)(2,1)S(1)}, bf16[4096,128]{1,0:T(8,128)(2,1)S(1)}, u32[]{:S(2)}, u32[]{:S(2)}) collective-permute-start(bf16[4096,128]{1,0:T(8,128)(2,1)S(1)} %constant_dynamic-update-slice_fusion.even_ref), channel_id=1, source_target_pairs={{0,64},{64,0},{128,192},{192,128},{256,320},{320,256},{384,448},{4... | collective-permute-start | bytes 3145736 | tf_op jit(solution)/shard_map/ppermute | solution.py:158
  68.3 0.0 copy-done.1
  68.3 0.2 plan.1.plan_ref
  68.5 2.4 %collective-permute-done.6.odd_ref = bf16[4096,128]{1,0:T(8,128)(2,1)S(1)} collective-permute-done((bf16[4096,128]{1,0:T(8,128)(2,1)S(1)}, bf16[4096,128]{1,0:T(8,128)(2,1)S(1)}, u32[]{:S(2)}, u32[]{:S(2)}) %collective-permute-start.6) | collective-permute-done | bytes 1048608 | tf_op jit(solution)/shard_map/ppermute | solution.py:158
  70.9 15.8 %all-to-all-done.1 = bf16[64,8,1152]{2,1,0:T(8,128)(2,1)S(1)} async-done(((bf16[64,8,1152]{2,1,0:T(8,128)(2,1)}), bf16[64,8,1152]{2,1,0:T(8,128)(2,1)S(1)}, u32[]{:S(2)}, u32[]{:S(2)}) %all-to-all-start.1) | async-done | bytes 1179680 | tf_op jit(solution)/shard_map/all_to_all | solution.py:276
  86.7 0.0 copy-done.2
  86.7 0.0 copy-done.3
  86.7 2.1 %product.1 = (bf16[512,128]{1,0:T(8,128)(2,1)}, f32[1,128]{1,0:T(1,128)}) custom-call(s32[8,18]{1,0:T(8,128)S(1)} %plan.1.plan_ref, s32[8]{0:T(128)S(1)} %copy-done.2, s32[1,128]{1,0:T(1,128)S(1)} %copy-done.3, bf16[512,128]{1,0:T(8,128)(2,1)S(1)} %copy-done, bf16[512,1152]{1,0:T(8,128)(2,1)S(1)} %bitcast.3, ...), custom_call_target="tpu_custom_call" | custom-call | tf_op jit(solution)/shard_map/product/pallas_call | solution.py:286
  (7 shorter events, 0.1 us)
Async XLA Ops:
  2.8 26.5 %collective-permute-start.1 = (bf16[512,128]{1,0:T(8,128)(2,1)}, bf16[512,128]{1,0:T(8,128)(2,1)S(1)}, u32[]{:S(2)}, u32[]{:S(2)}) collective-permute-start(bf16[512,128]{1,0:T(8,128)(2,1)} %get-tuple-element.7.own_ref.strip_ref), channel_id=1, source_target_pairs={{0,0},{4,64},{8,128},{12,192},{16,256},{20,320},{24,384},{28,448},... | collective-permute-start | bytes 393224 | tf_op jit(solution)/shard_map/ppermute | solution.py:254
  8.6 21.9 %all-to-all-start = ((bf16[16,8,1152]{2,1,0:T(8,128)(2,1)}), bf16[16,8,1152]{2,1,0:T(8,128)(2,1)S(1)}, u32[]{:S(2)}, u32[]{:S(2)}) async-start(bf16[16,8,1152]{2,1,0:T(8,128)(2,1)} %bitcast.4), calls=%async_computation | async-start | bytes 589824 | tf_op jit(solution)/shard_map/all_to_all | solution.py:256
  15.3 38.5 %collective-permute-start = (bf16[512,128]{1,0:T(8,128)(2,1)}, bf16[512,128]{1,0:T(8,128)(2,1)S(1)}, u32[]{:S(2)}, u32[]{:S(2)}) collective-permute-start(bf16[512,128]{1,0:T(8,128)(2,1)} %get-tuple-element.7.own_ref.strip_ref), channel_id=1, source_target_pairs={{0,512},{64,576},{128,640},{192,704},{256,768},{320,832},{384,896}... | collective-permute-start | bytes 393224 | tf_op jit(solution)/shard_map/ppermute | solution.py:134
  21.3 39.6 %collective-permute-start.2 = (bf16[512,128]{1,0:T(8,128)(2,1)}, bf16[512,128]{1,0:T(8,128)(2,1)S(1)}, u32[]{:S(2)}, u32[]{:S(2)}) collective-permute-start(bf16[512,128]{1,0:T(8,128)(2,1)} %get-tuple-element.7.own_ref.strip_ref), channel_id=1, source_target_pairs={{0,768},{64,832},{128,896},{192,960},{256,0},{320,64},{384,128},{4... | collective-permute-start | bytes 393224 | tf_op jit(solution)/shard_map/ppermute | solution.py:134
  24.1 36.9 %collective-permute-start.3 = (bf16[512,128]{1,0:T(8,128)(2,1)}, bf16[512,128]{1,0:T(8,128)(2,1)S(1)}, u32[]{:S(2)}, u32[]{:S(2)}) collective-permute-start(bf16[512,128]{1,0:T(8,128)(2,1)} %get-tuple-element.7.own_ref.strip_ref), channel_id=1, source_target_pairs={{0,256},{64,320},{128,384},{192,448},{256,512},{320,576},{384,640}... | collective-permute-start | bytes 393224 | tf_op jit(solution)/shard_map/ppermute | solution.py:134
  29.3 0.9 %copy-start.4 = (bf16[128,512]{1,0:T(8,128)(2,1)S(1)}, bf16[128,512]{1,0:T(8,128)(2,1)}, u32[]{:S(2)}) copy-start(bf16[128,512]{1,0:T(8,128)(2,1)} %get-tuple-element.8.rows_ref) | copy-start | bytes 393220
  31.6 22.2 %copy-start = (bf16[512,128]{1,0:T(8,128)(2,1)S(1)}, bf16[512,128]{1,0:T(8,128)(2,1)}, u32[]{:S(2)}) copy-start(bf16[512,128]{1,0:T(8,128)(2,1)} %get-tuple-element.7.own_ref.strip_ref) | copy-start | bytes 393220
  31.6 55.1 %all-to-all-start.1 = ((bf16[64,8,1152]{2,1,0:T(8,128)(2,1)}), bf16[64,8,1152]{2,1,0:T(8,128)(2,1)S(1)}, u32[]{:S(2)}, u32[]{:S(2)}) async-start(bf16[64,8,1152]{2,1,0:T(8,128)(2,1)} %share.1), calls=%async_computation.1 | async-start | bytes 2359296 | tf_op jit(solution)/shard_map/all_to_all | solution.py:276
  53.8 14.4 %copy-start.1 = (s32[8,16]{1,0:T(8,128)S(1)}, s32[8,16]{1,0:T(8,128)}, u32[]{:S(2)}) copy-start(s32[8,16]{1,0:T(8,128)} %pat_ref.1) | copy-start | bytes 1540
  53.9 11.2 %collective-permute-start.4 = (bf16[1024,128]{1,0:T(8,128)(2,1)S(1)}, bf16[1024,128]{1,0:T(8,128)(2,1)S(1)}, u32[]{:S(2)}, u32[]{:S(2)}) collective-permute-start(bf16[1024,128]{1,0:T(8,128)(2,1)S(1)} %pair.1), channel_id=1, source_target_pairs={{0,896},{64,960},{128,0},{192,64},{256,128},{320,192},{384,256},{4... | collective-permute-start | bytes 786440 | tf_op jit(solution)/shard_map/ppermute | solution.py:134
  56.1 10.2 %collective-permute-start.5 = (bf16[1024,128]{1,0:T(8,128)(2,1)S(1)}, bf16[1024,128]{1,0:T(8,128)(2,1)S(1)}, u32[]{:S(2)}, u32[]{:S(2)}) collective-permute-start(bf16[1024,128]{1,0:T(8,128)(2,1)S(1)} %pair.1), channel_id=1, source_target_pairs={{0,128},{64,192},{128,256},{192,320},{256,384},{320,448},{384,512}... | collective-permute-start | bytes 786440 | tf_op jit(solution)/shard_map/ppermute | solution.py:134
  66.3 20.4 %copy-start.2 = (s32[8]{0:T(128)S(1)}, s32[8]{0:T(128)}, u32[]{:S(2)}) copy-start(s32[8]{0:T(128)} %flag_ref.1) | copy-start | bytes 100
  66.3 20.4 %copy-start.3 = (s32[1,128]{1,0:T(1,128)S(1)}, s32[1,128]{1,0:T(1,128)}, u32[]{:S(2)}) copy-start(s32[1,128]{1,0:T(1,128)} %count_ref.1) | copy-start | bytes 1540
  66.4 4.6 %collective-permute-start.6 = (bf16[4096,128]{1,0:T(8,128)(2,1)S(1)}, bf16[4096,128]{1,0:T(8,128)(2,1)S(1)}, u32[]{:S(2)}, u32[]{:S(2)}) collective-permute-start(bf16[4096,128]{1,0:T(8,128)(2,1)S(1)} %constant_dynamic-update-slice_fusion.even_ref), channel_id=1, source_target_pairs={{0,64},{64,0},{128,192},{192,128},{256,320},{320,256},{384,448},{4... | collective-permute-start | bytes 3145736 | tf_op jit(solution)/shard_map/ppermute | solution.py:158

commit v10 on v9

--- a/solution.py
+++ b/solution.py
@@ -152,6 +152,7 @@
         cost_estimate=pl.CostEstimate(flops=PAIR_COST, bytes_accessed=1 << 19, transcendentals=0),
         name="pair",
     )(strip, across)
+    strip, pair = lax.optimization_barrier((strip, pair))
     above, below = from_chip(1, pair), from_chip(-1, pair)
     second, sixth = from_chip(2, strip), from_chip(-2, strip)
     held = jnp.concatenate([pair, second, sixth, above, below], axis=0)
@@ -260,7 +261,7 @@
         out_shape=jax.ShapeDtypeStruct((8, width), F32),
         in_specs=[VMEM, VMEM],
         out_specs=VMEM,
-        compiler_params=limit,
+        compiler_params=pltpu.CompilerParams(vmem_limit_bytes=60 << 20),
         cost_estimate=pl.CostEstimate(flops=COST, bytes_accessed=1 << 20, transcendentals=0),
         name="diagonal",
     )(rows, trans)

time: 89.4 us -> 88.6 us (level)
  waiting for transfers between devices: 23.5 us -> 21.1 us
  Pallas kernels: 5.93 us -> 7.51 us
    all_to_all x1, waiting for transfers between devices: 15.8 us -> 8.14 us  [per_device(): lax.all_to_all(send, ('depth', 'col'), 0, 0).reshape(tile, slots_wide)]
    all_to_all x1, waiting for transfers between devices: 0.01 us -> 5.94 us  [per_device(): parts = lax.all_to_all(slots.reshape(n_col, chunk, slots_wide), 'col', 0, 0)]
    pallas_call x1, Pallas kernels: 0.26 us -> 1.82 us  [per_device(): pl.pallas_call(diagonal_kernel, out_shape=jax.ShapeDtypeStruct((8, width)...]
  transfers between devices with their start and end apart: 9 -> 9, of which waited for: 4 -> 5; matrix products, arithmetic and copies ran while one was open for 0% -> 0% of each run, Pallas kernels for 2% -> 4%
where the time goes in v10:
time: 88.6 us; the launch traced here: 88 us
  starting transfers between devices  57.1 us (64%)
  waiting for transfers between devices  21.1 us (24%)
  Pallas kernels  7.51 us (8%)
  local copies, waits for them, and re-layouts  1.48 us (2%)
    all_to_all x1, starting transfers between devices, per_device(): lax.all_to_all(send, ('depth', 'col'), 0, 0).reshape(tile, slots_wide)  21.7 us
    ppermute x5, starting transfers between devices, from_chip(): lax.ppermute(value, 'row', [(s, (s - 2 * distance) % n_row) for s in rang...  21 us
    all_to_all x1, waiting for transfers between devices, per_device(): lax.all_to_all(send, ('depth', 'col'), 0, 0).reshape(tile, slots_wide)  8.14 us
    all_to_all x1, starting transfers between devices, per_device(): parts = lax.all_to_all(slots.reshape(n_col, chunk, slots_wide), 'col', 0, 0)  6.71 us
    all_to_all x1, waiting for transfers between devices, per_device(): parts = lax.all_to_all(slots.reshape(n_col, chunk, slots_wide), 'col', 0, 0)  5.94 us
    ppermute x1, starting transfers between devices, per_device(): trans = lax.ppermute(strip, ('row', 'col'), swap)  5.77 us
    ppermute x5, waiting for transfers between devices, from_chip(): lax.ppermute(value, 'row', [(s, (s - 2 * distance) % n_row) for s in rang...  4.6 us
    ppermute x1, waiting for transfers between devices, gather_strip(): return (held, lax.ppermute(held, 'row', [(s, s ^ 1) for s in range(n_row)]))  2.44 us
  transfers between devices with their start and end apart: 9, of which 5 were waited for; matrix products, arithmetic and copies ran while one was open for 0% of the time, Pallas kernels for 4%

profile of v10, /device:TPU:6, one launch (start us, length us, event | category | flops | bytes accessed | tf_op | source)
XLA Modules:
  0.0 88.0 jit_solution(10501681862713454154)
XLA Ops:
  0.6 2.2 %pack.1 = (bf16[512,128]{1,0:T(8,128)(2,1)}, bf16[128,512]{1,0:T(8,128)(2,1)}, bf16[128,1152]{1,0:T(8,128)(2,1)}) custom-call(s32[8,16]{1,0:T(8,128)} %pat_ref.1, bf16[512,512]{1,0:T(8,128)(2,1)} %dens_hbm.1), custom_call_target="tpu_custom_call" | custom-call | tf_op jit(solution)/shard_map/pack/pallas_call | solution.py:236
  2.8 5.8 %collective-permute-start.1 = (bf16[512,128]{1,0:T(8,128)(2,1)}, bf16[512,128]{1,0:T(8,128)(2,1)S(1)}, u32[]{:S(2)}, u32[]{:S(2)}) collective-permute-start(bf16[512,128]{1,0:T(8,128)(2,1)} %get-tuple-element.13.own_ref.strip_ref), channel_id=1, source_target_pairs={{0,0},{4,64},{8,128},{12,192},{16,256},{20,320},{24,384},{28,448},... | collective-permute-start | bytes 393224 | tf_op jit(solution)/shard_map/ppermute | solution.py:255
  8.6 6.7 %all-to-all-start = ((bf16[16,8,1152]{2,1,0:T(8,128)(2,1)}), bf16[16,8,1152]{2,1,0:T(8,128)(2,1)S(1)}, u32[]{:S(2)}, u32[]{:S(2)}) async-start(bf16[16,8,1152]{2,1,0:T(8,128)(2,1)} %bitcast.4), calls=%async_computation | async-start | bytes 589824 | tf_op jit(solution)/shard_map/all_to_all | solution.py:257
  15.3 6.0 %collective-permute-start = (bf16[512,128]{1,0:T(8,128)(2,1)}, bf16[512,128]{1,0:T(8,128)(2,1)S(1)}, u32[]{:S(2)}, u32[]{:S(2)}) collective-permute-start(bf16[512,128]{1,0:T(8,128)(2,1)} %get-tuple-element.13.own_ref.strip_ref), channel_id=1, source_target_pairs={{0,512},{64,576},{128,640},{192,704},{256,768},{320,832},{384,896}... | collective-permute-start | bytes 393224 | tf_op jit(solution)/shard_map/ppermute | solution.py:134
  21.3 0.0 collective-permute-done.1.trans_ref
  21.3 0.0 copy-start.5
  21.3 0.6 copy-done.5
  22.0 1.8 %diagonal.1.terms_ref = f32[8,128]{1,0:T(8,128)} custom-call(bf16[128,512]{1,0:T(8,128)(2,1)} %get-tuple-element.10.rows_ref, bf16[512,128]{1,0:T(8,128)(2,1)} %copy-done.5), custom_call_target="tpu_custom_call" | custom-call | flops 5299999744 | bytes 1048576 | tf_op jit(solution)/shard_map/diagonal/pallas_call | solution.py:259
  23.8 5.9 %all-to-all-done.parts_ref = bf16[16,8,1152]{2,1,0:T(8,128)(2,1)S(1)} async-done(((bf16[16,8,1152]{2,1,0:T(8,128)(2,1)}), bf16[16,8,1152]{2,1,0:T(8,128)(2,1)S(1)}, u32[]{:S(2)}, u32[]{:S(2)}) %all-to-all-start) | async-done | bytes 294944 | tf_op jit(solution)/shard_map/all_to_all | solution.py:257
  29.8 0.7 copy-done.2
  30.4 1.2 %share.1 = bf16[64,8,1152]{2,1,0:T(8,128)(2,1)} custom-call(f32[8,128]{1,0:T(8,128)S(1)} %copy-done.2, bf16[16,8,1152]{2,1,0:T(8,128)(2,1)S(1)} %all-to-all-done.parts_ref), custom_call_target="tpu_custom_call" | custom-call | tf_op jit(solution)/shard_map/share/pallas_call | solution.py:268
  31.6 21.7 %all-to-all-start.1 = ((bf16[64,8,1152]{2,1,0:T(8,128)(2,1)}), bf16[64,8,1152]{2,1,0:T(8,128)(2,1)S(1)}, u32[]{:S(2)}, u32[]{:S(2)}) async-start(bf16[64,8,1152]{2,1,0:T(8,128)(2,1)} %share.1), calls=%async_computation.1 | async-start | bytes 2359296 | tf_op jit(solution)/shard_map/all_to_all | solution.py:277
  53.3 0.0 collective-permute-done._.other_ref
  53.3 0.0 copy-done
  53.3 0.0 copy-start.1
  53.3 1.9 %collective-permute-start.2 = (bf16[512,128]{1,0:T(8,128)(2,1)S(1)}, bf16[512,128]{1,0:T(8,128)(2,1)S(1)}, u32[]{:S(2)}, u32[]{:S(2)}) collective-permute-start(bf16[512,128]{1,0:T(8,128)(2,1)S(1)} %copy-done), channel_id=1, source_target_pairs={{0,768},{64,832},{128,896},{192,960},{256,0},{320,64},{384,128},{4... | collective-permute-start | bytes 393224 | tf_op jit(solution)/shard_map/ppermute | solution.py:134
  55.3 6.0 %collective-permute-start.3 = (bf16[512,128]{1,0:T(8,128)(2,1)S(1)}, bf16[512,128]{1,0:T(8,128)(2,1)S(1)}, u32[]{:S(2)}, u32[]{:S(2)}) collective-permute-start(bf16[512,128]{1,0:T(8,128)(2,1)S(1)} %copy-done), channel_id=1, source_target_pairs={{0,256},{64,320},{128,384},{192,448},{256,512},{320,576},{384,640}... | collective-permute-start | bytes 393224 | tf_op jit(solution)/shard_map/ppermute | solution.py:134
  61.3 2.0 %collective-permute-start.4 = (bf16[1024,128]{1,0:T(8,128)(2,1)S(1)}, bf16[1024,128]{1,0:T(8,128)(2,1)S(1)}, u32[]{:S(2)}, u32[]{:S(2)}) collective-permute-start(bf16[1024,128]{1,0:T(8,128)(2,1)S(1)} %pair.1), channel_id=1, source_target_pairs={{0,896},{64,960},{128,0},{192,64},{256,128},{320,192},{384,256},{4... | collective-permute-start | bytes 786440 | tf_op jit(solution)/shard_map/ppermute | solution.py:134
  63.3 5.1 %collective-permute-start.5 = (bf16[1024,128]{1,0:T(8,128)(2,1)S(1)}, bf16[1024,128]{1,0:T(8,128)(2,1)S(1)}, u32[]{:S(2)}, u32[]{:S(2)}) collective-permute-start(bf16[1024,128]{1,0:T(8,128)(2,1)S(1)} %pair.1), channel_id=1, source_target_pairs={{0,128},{64,192},{128,256},{192,320},{256,384},{320,448},{384,512}... | collective-permute-start | bytes 786440 | tf_op jit(solution)/shard_map/ppermute | solution.py:134
  68.4 0.0 collective-permute-done.2
  68.4 0.0 collective-permute-done.3
  68.5 3.4 %collective-permute-done.4 = bf16[1024,128]{1,0:T(8,128)(2,1)S(1)} collective-permute-done((bf16[1024,128]{1,0:T(8,128)(2,1)S(1)}, bf16[1024,128]{1,0:T(8,128)(2,1)S(1)}, u32[]{:S(2)}, u32[]{:S(2)}) %collective-permute-start.4) | collective-permute-done | bytes 262176 | tf_op jit(solution)/shard_map/ppermute | solution.py:134
  71.9 1.2 %collective-permute-done.5 = bf16[1024,128]{1,0:T(8,128)(2,1)S(1)} collective-permute-done((bf16[1024,128]{1,0:T(8,128)(2,1)S(1)}, bf16[1024,128]{1,0:T(8,128)(2,1)S(1)}, u32[]{:S(2)}, u32[]{:S(2)}) %collective-permute-start.5) | collective-permute-done | bytes 262176 | tf_op jit(solution)/shard_map/ppermute | solution.py:134
  73.1 0.0 copy-start.3
  73.2 0.0 copy-start.4
  73.2 1.9 %collective-permute-start.6 = (bf16[4096,128]{1,0:T(8,128)(2,1)S(1)}, bf16[4096,128]{1,0:T(8,128)(2,1)S(1)}, u32[]{:S(2)}, u32[]{:S(2)}) collective-permute-start(bf16[4096,128]{1,0:T(8,128)(2,1)S(1)} %constant_dynamic-update-slice_fusion.even_ref), channel_id=1, source_target_pairs={{0,64},{64,0},{128,192},{192,128},{256,320},{320,256},{384,448},{4... | collective-permute-start | bytes 3145736 | tf_op jit(solution)/shard_map/ppermute | solution.py:159
  75.1 0.0 copy-done.1
  75.1 0.2 plan.1.plan_ref
  75.3 2.4 %collective-permute-done.6.odd_ref = bf16[4096,128]{1,0:T(8,128)(2,1)S(1)} collective-permute-done((bf16[4096,128]{1,0:T(8,128)(2,1)S(1)}, bf16[4096,128]{1,0:T(8,128)(2,1)S(1)}, u32[]{:S(2)}, u32[]{:S(2)}) %collective-permute-start.6) | collective-permute-done | bytes 1048608 | tf_op jit(solution)/shard_map/ppermute | solution.py:159
  77.7 8.1 %all-to-all-done.1 = bf16[64,8,1152]{2,1,0:T(8,128)(2,1)S(1)} async-done(((bf16[64,8,1152]{2,1,0:T(8,128)(2,1)}), bf16[64,8,1152]{2,1,0:T(8,128)(2,1)S(1)}, u32[]{:S(2)}, u32[]{:S(2)}) %all-to-all-start.1) | async-done | bytes 1179680 | tf_op jit(solution)/shard_map/all_to_all | solution.py:277
  85.9 0.0 copy-done.3
  85.9 2.1 %product.1 = (bf16[512,128]{1,0:T(8,128)(2,1)}, f32[1,128]{1,0:T(1,128)}) custom-call(s32[8,18]{1,0:T(8,128)S(1)} %plan.1.plan_ref, s32[8]{0:T(128)S(1)} %copy-done.3, s32[1,128]{1,0:T(1,128)S(1)} %copy-done.4, bf16[512,128]{1,0:T(8,128)(2,1)S(1)} %copy-done, bf16[512,1152]{1,0:T(8,128)(2,1)S(1)} %bitcast.3, ...), custom_call_target="tpu_custom_call" | custom-call | tf_op jit(solution)/shard_map/product/pallas_call | solution.py:287
  (9 shorter events, 0.2 us)
Async XLA Ops:
  2.8 18.5 %collective-permute-start.1 = (bf16[512,128]{1,0:T(8,128)(2,1)}, bf16[512,128]{1,0:T(8,128)(2,1)S(1)}, u32[]{:S(2)}, u32[]{:S(2)}) collective-permute-start(bf16[512,128]{1,0:T(8,128)(2,1)} %get-tuple-element.13.own_ref.strip_ref), channel_id=1, source_target_pairs={{0,0},{4,64},{8,128},{12,192},{16,256},{20,320},{24,384},{28,448},... | collective-permute-start | bytes 393224 | tf_op jit(solution)/shard_map/ppermute | solution.py:255
  8.6 21.2 %all-to-all-start = ((bf16[16,8,1152]{2,1,0:T(8,128)(2,1)}), bf16[16,8,1152]{2,1,0:T(8,128)(2,1)S(1)}, u32[]{:S(2)}, u32[]{:S(2)}) async-start(bf16[16,8,1152]{2,1,0:T(8,128)(2,1)} %bitcast.4), calls=%async_computation | async-start | bytes 589824 | tf_op jit(solution)/shard_map/all_to_all | solution.py:257
  15.3 38.0 %collective-permute-start = (bf16[512,128]{1,0:T(8,128)(2,1)}, bf16[512,128]{1,0:T(8,128)(2,1)S(1)}, u32[]{:S(2)}, u32[]{:S(2)}) collective-permute-start(bf16[512,128]{1,0:T(8,128)(2,1)} %get-tuple-element.13.own_ref.strip_ref), channel_id=1, source_target_pairs={{0,512},{64,576},{128,640},{192,704},{256,768},{320,832},{384,896}... | collective-permute-start | bytes 393224 | tf_op jit(solution)/shard_map/ppermute | solution.py:134
  21.3 0.7 copy-start.5
  29.8 0.7 copy-start.2
  31.6 21.7 %copy-start = (bf16[512,128]{1,0:T(8,128)(2,1)S(1)}, bf16[512,128]{1,0:T(8,128)(2,1)}, u32[]{:S(2)}) copy-start(bf16[512,128]{1,0:T(8,128)(2,1)} %get-tuple-element.13.own_ref.strip_ref) | copy-start | bytes 393220
  31.6 54.3 %all-to-all-start.1 = ((bf16[64,8,1152]{2,1,0:T(8,128)(2,1)}), bf16[64,8,1152]{2,1,0:T(8,128)(2,1)S(1)}, u32[]{:S(2)}, u32[]{:S(2)}) async-start(bf16[64,8,1152]{2,1,0:T(8,128)(2,1)} %share.1), calls=%async_computation.1 | async-start | bytes 2359296 | tf_op jit(solution)/shard_map/all_to_all | solution.py:277
  53.3 21.8 %copy-start.1 = (s32[8,16]{1,0:T(8,128)S(1)}, s32[8,16]{1,0:T(8,128)}, u32[]{:S(2)}) copy-start(s32[8,16]{1,0:T(8,128)} %pat_ref.1) | copy-start | bytes 1540
  53.3 15.1 %collective-permute-start.2 = (bf16[512,128]{1,0:T(8,128)(2,1)S(1)}, bf16[512,128]{1,0:T(8,128)(2,1)S(1)}, u32[]{:S(2)}, u32[]{:S(2)}) collective-permute-start(bf16[512,128]{1,0:T(8,128)(2,1)S(1)} %copy-done), channel_id=1, source_target_pairs={{0,768},{64,832},{128,896},{192,960},{256,0},{320,64},{384,128},{4... | collective-permute-start | bytes 393224 | tf_op jit(solution)/shard_map/ppermute | solution.py:134
  55.3 13.2 %collective-permute-start.3 = (bf16[512,128]{1,0:T(8,128)(2,1)S(1)}, bf16[512,128]{1,0:T(8,128)(2,1)S(1)}, u32[]{:S(2)}, u32[]{:S(2)}) collective-permute-start(bf16[512,128]{1,0:T(8,128)(2,1)S(1)} %copy-done), channel_id=1, source_target_pairs={{0,256},{64,320},{128,384},{192,448},{256,512},{320,576},{384,640}... | collective-permute-start | bytes 393224 | tf_op jit(solution)/shard_map/ppermute | solution.py:134
  61.3 10.6 %collective-permute-start.4 = (bf16[1024,128]{1,0:T(8,128)(2,1)S(1)}, bf16[1024,128]{1,0:T(8,128)(2,1)S(1)}, u32[]{:S(2)}, u32[]{:S(2)}) collective-permute-start(bf16[1024,128]{1,0:T(8,128)(2,1)S(1)} %pair.1), channel_id=1, source_target_pairs={{0,896},{64,960},{128,0},{192,64},{256,128},{320,192},{384,256},{4... | collective-permute-start | bytes 786440 | tf_op jit(solution)/shard_map/ppermute | solution.py:134
  63.3 9.8 %collective-permute-start.5 = (bf16[1024,128]{1,0:T(8,128)(2,1)S(1)}, bf16[1024,128]{1,0:T(8,128)(2,1)S(1)}, u32[]{:S(2)}, u32[]{:S(2)}) collective-permute-start(bf16[1024,128]{1,0:T(8,128)(2,1)S(1)} %pair.1), channel_id=1, source_target_pairs={{0,128},{64,192},{128,256},{192,320},{256,384},{320,448},{384,512}... | collective-permute-start | bytes 786440 | tf_op jit(solution)/shard_map/ppermute | solution.py:134
  73.1 12.7 %copy-start.3 = (s32[8]{0:T(128)S(1)}, s32[8]{0:T(128)}, u32[]{:S(2)}) copy-start(s32[8]{0:T(128)} %flag_ref.1) | copy-start | bytes 100
  73.2 12.7 %copy-start.4 = (s32[1,128]{1,0:T(1,128)S(1)}, s32[1,128]{1,0:T(1,128)}, u32[]{:S(2)}) copy-start(s32[1,128]{1,0:T(1,128)} %count_ref.1) | copy-start | bytes 1540
  73.2 4.6 %collective-permute-start.6 = (bf16[4096,128]{1,0:T(8,128)(2,1)S(1)}, bf16[4096,128]{1,0:T(8,128)(2,1)S(1)}, u32[]{:S(2)}, u32[]{:S(2)}) collective-permute-start(bf16[4096,128]{1,0:T(8,128)(2,1)S(1)} %constant_dynamic-update-slice_fusion.even_ref), channel_id=1, source_target_pairs={{0,64},{64,0},{128,192},{192,128},{256,320},{320,256},{384,448},{4... | collective-permute-start | bytes 3145736 | tf_op jit(solution)/shard_map/ppermute | solution.py:159

commit v11 on v9

--- a/solution.py
+++ b/solution.py
@@ -152,6 +152,7 @@
         cost_estimate=pl.CostEstimate(flops=PAIR_COST, bytes_accessed=1 << 19, transcendentals=0),
         name="pair",
     )(strip, across)
+    strip, pair = lax.optimization_barrier((strip, pair))
     above, below = from_chip(1, pair), from_chip(-1, pair)
     second, sixth = from_chip(2, strip), from_chip(-2, strip)
     held = jnp.concatenate([pair, second, sixth, above, below], axis=0)

time: 89.4 us -> 87.9 us (0.983)
  waiting for transfers between devices: 23.5 us -> 22.4 us
    all_to_all x1, waiting for transfers between devices: 15.8 us -> 8.14 us  [per_device(): lax.all_to_all(send, ('depth', 'col'), 0, 0).reshape(tile, slots_wide)]
    all_to_all x1, waiting for transfers between devices: 0.01 us -> 7.26 us  [per_device(): parts = lax.all_to_all(slots.reshape(n_col, chunk, slots_wide), 'col', 0, 0)]
  transfers between devices with their start and end apart: 9 -> 9, of which waited for: 4 -> 5; matrix products, arithmetic and copies ran while one was open for 0% -> 0% of each run, Pallas kernels for 2% -> 2%
where the time goes in v11:
time: 87.9 us; the launch traced here: 87.3 us
  starting transfers between devices  57.1 us (65%)
  waiting for transfers between devices  22.4 us (25%)
  Pallas kernels  5.93 us (7%)
  local copies, waits for them, and re-layouts  1.05 us (1%)
    all_to_all x1, starting transfers between devices, per_device(): lax.all_to_all(send, ('depth', 'col'), 0, 0).reshape(tile, slots_wide)  21.7 us
    ppermute x5, starting transfers between devices, from_chip(): lax.ppermute(value, 'row', [(s, (s - 2 * distance) % n_row) for s in rang...  21 us
    all_to_all x1, waiting for transfers between devices, per_device(): lax.all_to_all(send, ('depth', 'col'), 0, 0).reshape(tile, slots_wide)  8.14 us
    all_to_all x1, waiting for transfers between devices, per_device(): parts = lax.all_to_all(slots.reshape(n_col, chunk, slots_wide), 'col', 0, 0)  7.26 us
    all_to_all x1, starting transfers between devices, per_device(): parts = lax.all_to_all(slots.reshape(n_col, chunk, slots_wide), 'col', 0, 0)  6.71 us
    ppermute x1, starting transfers between devices, per_device(): trans = lax.ppermute(strip, ('row', 'col'), swap)  5.77 us
    ppermute x5, waiting for transfers between devices, from_chip(): lax.ppermute(value, 'row', [(s, (s - 2 * distance) % n_row) for s in rang...  4.6 us
    ppermute x1, waiting for transfers between devices, gather_strip(): return (held, lax.ppermute(held, 'row', [(s, s ^ 1) for s in range(n_row)]))  2.44 us
  transfers between devices with their start and end apart: 9, of which 5 were waited for; matrix products, arithmetic and copies ran while one was open for 0% of the time, Pallas kernels for 2%

profile of v11, /device:TPU:6, one launch (start us, length us, event | category | flops | bytes accessed | tf_op | source)
XLA Modules:
  0.0 87.3 jit_solution(18311487012790533613)
XLA Ops:
  0.6 2.2 %pack.1 = (bf16[512,128]{1,0:T(8,128)(2,1)}, bf16[128,512]{1,0:T(8,128)(2,1)}, bf16[128,1152]{1,0:T(8,128)(2,1)}) custom-call(s32[8,16]{1,0:T(8,128)} %pat_ref.1, bf16[512,512]{1,0:T(8,128)(2,1)} %dens_hbm.1), custom_call_target="tpu_custom_call" | custom-call | tf_op jit(solution)/shard_map/pack/pallas_call | solution.py:236
  2.8 5.8 %collective-permute-start.1 = (bf16[512,128]{1,0:T(8,128)(2,1)}, bf16[512,128]{1,0:T(8,128)(2,1)S(1)}, u32[]{:S(2)}, u32[]{:S(2)}) collective-permute-start(bf16[512,128]{1,0:T(8,128)(2,1)} %get-tuple-element.13.own_ref.strip_ref), channel_id=1, source_target_pairs={{0,0},{4,64},{8,128},{12,192},{16,256},{20,320},{24,384},{28,448},... | collective-permute-start | bytes 393224 | tf_op jit(solution)/shard_map/ppermute | solution.py:255
  8.6 6.7 %all-to-all-start = ((bf16[16,8,1152]{2,1,0:T(8,128)(2,1)}), bf16[16,8,1152]{2,1,0:T(8,128)(2,1)S(1)}, u32[]{:S(2)}, u32[]{:S(2)}) async-start(bf16[16,8,1152]{2,1,0:T(8,128)(2,1)} %bitcast.4), calls=%async_computation | async-start | bytes 589824 | tf_op jit(solution)/shard_map/all_to_all | solution.py:257
  15.3 6.0 %collective-permute-start = (bf16[512,128]{1,0:T(8,128)(2,1)}, bf16[512,128]{1,0:T(8,128)(2,1)S(1)}, u32[]{:S(2)}, u32[]{:S(2)}) collective-permute-start(bf16[512,128]{1,0:T(8,128)(2,1)} %get-tuple-element.13.own_ref.strip_ref), channel_id=1, source_target_pairs={{0,512},{64,576},{128,640},{192,704},{256,768},{320,832},{384,896}... | collective-permute-start | bytes 393224 | tf_op jit(solution)/shard_map/ppermute | solution.py:134
  21.3 0.0 collective-permute-done.1.trans_ref
  21.3 0.0 copy-start.4
  21.3 0.9 %copy-done.4 = bf16[128,512]{1,0:T(8,128)(2,1)S(1)} copy-done((bf16[128,512]{1,0:T(8,128)(2,1)S(1)}, bf16[128,512]{1,0:T(8,128)(2,1)}, u32[]{:S(2)}) %copy-start.4) | copy-done | bytes 131096
  22.2 0.3 diagonal.1.terms_ref
  22.5 7.3 %all-to-all-done.parts_ref = bf16[16,8,1152]{2,1,0:T(8,128)(2,1)S(1)} async-done(((bf16[16,8,1152]{2,1,0:T(8,128)(2,1)}), bf16[16,8,1152]{2,1,0:T(8,128)(2,1)S(1)}, u32[]{:S(2)}, u32[]{:S(2)}) %all-to-all-start) | async-done | bytes 294944 | tf_op jit(solution)/shard_map/all_to_all | solution.py:257
  29.8 1.1 %share.1 = bf16[64,8,1152]{2,1,0:T(8,128)(2,1)} custom-call(f32[8,128]{1,0:T(8,128)S(1)} %diagonal.1.terms_ref, bf16[16,8,1152]{2,1,0:T(8,128)(2,1)S(1)} %all-to-all-done.parts_ref), custom_call_target="tpu_custom_call" | custom-call | tf_op jit(solution)/shard_map/share/pallas_call | solution.py:268
  30.9 21.7 %all-to-all-start.1 = ((bf16[64,8,1152]{2,1,0:T(8,128)(2,1)}), bf16[64,8,1152]{2,1,0:T(8,128)(2,1)S(1)}, u32[]{:S(2)}, u32[]{:S(2)}) async-start(bf16[64,8,1152]{2,1,0:T(8,128)(2,1)} %share.1), calls=%async_computation.1 | async-start | bytes 2359296 | tf_op jit(solution)/shard_map/all_to_all | solution.py:277
  52.6 0.0 collective-permute-done._.other_ref
  52.6 0.0 copy-done
  52.6 0.0 copy-start.1
  52.6 1.9 %collective-permute-start.2 = (bf16[512,128]{1,0:T(8,128)(2,1)S(1)}, bf16[512,128]{1,0:T(8,128)(2,1)S(1)}, u32[]{:S(2)}, u32[]{:S(2)}) collective-permute-start(bf16[512,128]{1,0:T(8,128)(2,1)S(1)} %copy-done), channel_id=1, source_target_pairs={{0,768},{64,832},{128,896},{192,960},{256,0},{320,64},{384,128},{4... | collective-permute-start | bytes 393224 | tf_op jit(solution)/shard_map/ppermute | solution.py:134
  54.6 6.0 %collective-permute-start.3 = (bf16[512,128]{1,0:T(8,128)(2,1)S(1)}, bf16[512,128]{1,0:T(8,128)(2,1)S(1)}, u32[]{:S(2)}, u32[]{:S(2)}) collective-permute-start(bf16[512,128]{1,0:T(8,128)(2,1)S(1)} %copy-done), channel_id=1, source_target_pairs={{0,256},{64,320},{128,384},{192,448},{256,512},{320,576},{384,640}... | collective-permute-start | bytes 393224 | tf_op jit(solution)/shard_map/ppermute | solution.py:134
  60.6 2.0 %collective-permute-start.4 = (bf16[1024,128]{1,0:T(8,128)(2,1)S(1)}, bf16[1024,128]{1,0:T(8,128)(2,1)S(1)}, u32[]{:S(2)}, u32[]{:S(2)}) collective-permute-start(bf16[1024,128]{1,0:T(8,128)(2,1)S(1)} %pair.1), channel_id=1, source_target_pairs={{0,896},{64,960},{128,0},{192,64},{256,128},{320,192},{384,256},{4... | collective-permute-start | bytes 786440 | tf_op jit(solution)/shard_map/ppermute | solution.py:134
  62.6 5.1 %collective-permute-start.5 = (bf16[1024,128]{1,0:T(8,128)(2,1)S(1)}, bf16[1024,128]{1,0:T(8,128)(2,1)S(1)}, u32[]{:S(2)}, u32[]{:S(2)}) collective-permute-start(bf16[1024,128]{1,0:T(8,128)(2,1)S(1)} %pair.1), channel_id=1, source_target_pairs={{0,128},{64,192},{128,256},{192,320},{256,384},{320,448},{384,512}... | collective-permute-start | bytes 786440 | tf_op jit(solution)/shard_map/ppermute | solution.py:134
  67.7 0.0 collective-permute-done.2
  67.7 0.0 collective-permute-done.3
  67.8 3.4 %collective-permute-done.4 = bf16[1024,128]{1,0:T(8,128)(2,1)S(1)} collective-permute-done((bf16[1024,128]{1,0:T(8,128)(2,1)S(1)}, bf16[1024,128]{1,0:T(8,128)(2,1)S(1)}, u32[]{:S(2)}, u32[]{:S(2)}) %collective-permute-start.4) | collective-permute-done | bytes 262176 | tf_op jit(solution)/shard_map/ppermute | solution.py:134
  71.2 1.2 %collective-permute-done.5 = bf16[1024,128]{1,0:T(8,128)(2,1)S(1)} collective-permute-done((bf16[1024,128]{1,0:T(8,128)(2,1)S(1)}, bf16[1024,128]{1,0:T(8,128)(2,1)S(1)}, u32[]{:S(2)}, u32[]{:S(2)}) %collective-permute-start.5) | collective-permute-done | bytes 262176 | tf_op jit(solution)/shard_map/ppermute | solution.py:134
  72.4 0.0 copy-start.2
  72.5 0.0 copy-start.3
  72.5 1.9 %collective-permute-start.6 = (bf16[4096,128]{1,0:T(8,128)(2,1)S(1)}, bf16[4096,128]{1,0:T(8,128)(2,1)S(1)}, u32[]{:S(2)}, u32[]{:S(2)}) collective-permute-start(bf16[4096,128]{1,0:T(8,128)(2,1)S(1)} %constant_dynamic-update-slice_fusion.even_ref), channel_id=1, source_target_pairs={{0,64},{64,0},{128,192},{192,128},{256,320},{320,256},{384,448},{4... | collective-permute-start | bytes 3145736 | tf_op jit(solution)/shard_map/ppermute | solution.py:159
  74.4 0.0 copy-done.1
  74.4 0.2 plan.1.plan_ref
  74.6 2.4 %collective-permute-done.6.odd_ref = bf16[4096,128]{1,0:T(8,128)(2,1)S(1)} collective-permute-done((bf16[4096,128]{1,0:T(8,128)(2,1)S(1)}, bf16[4096,128]{1,0:T(8,128)(2,1)S(1)}, u32[]{:S(2)}, u32[]{:S(2)}) %collective-permute-start.6) | collective-permute-done | bytes 1048608 | tf_op jit(solution)/shard_map/ppermute | solution.py:159
  77.0 8.1 %all-to-all-done.1 = bf16[64,8,1152]{2,1,0:T(8,128)(2,1)S(1)} async-done(((bf16[64,8,1152]{2,1,0:T(8,128)(2,1)}), bf16[64,8,1152]{2,1,0:T(8,128)(2,1)S(1)}, u32[]{:S(2)}, u32[]{:S(2)}) %all-to-all-start.1) | async-done | bytes 1179680 | tf_op jit(solution)/shard_map/all_to_all | solution.py:277
  85.2 0.0 copy-done.2
  85.2 0.0 copy-done.3
  85.2 2.1 %product.1 = (bf16[512,128]{1,0:T(8,128)(2,1)}, f32[1,128]{1,0:T(1,128)}) custom-call(s32[8,18]{1,0:T(8,128)S(1)} %plan.1.plan_ref, s32[8]{0:T(128)S(1)} %copy-done.2, s32[1,128]{1,0:T(1,128)S(1)} %copy-done.3, bf16[512,128]{1,0:T(8,128)(2,1)S(1)} %copy-done, bf16[512,1152]{1,0:T(8,128)(2,1)S(1)} %bitcast.3, ...), custom_call_target="tpu_custom_call" | custom-call | tf_op jit(solution)/shard_map/product/pallas_call | solution.py:287
  (7 shorter events, 0.2 us)
Async XLA Ops:
  2.8 18.5 %collective-permute-start.1 = (bf16[512,128]{1,0:T(8,128)(2,1)}, bf16[512,128]{1,0:T(8,128)(2,1)S(1)}, u32[]{:S(2)}, u32[]{:S(2)}) collective-permute-start(bf16[512,128]{1,0:T(8,128)(2,1)} %get-tuple-element.13.own_ref.strip_ref), channel_id=1, source_target_pairs={{0,0},{4,64},{8,128},{12,192},{16,256},{20,320},{24,384},{28,448},... | collective-permute-start | bytes 393224 | tf_op jit(solution)/shard_map/ppermute | solution.py:255
  8.6 21.2 %all-to-all-start = ((bf16[16,8,1152]{2,1,0:T(8,128)(2,1)}), bf16[16,8,1152]{2,1,0:T(8,128)(2,1)S(1)}, u32[]{:S(2)}, u32[]{:S(2)}) async-start(bf16[16,8,1152]{2,1,0:T(8,128)(2,1)} %bitcast.4), calls=%async_computation | async-start | bytes 589824 | tf_op jit(solution)/shard_map/all_to_all | solution.py:257
  15.3 37.3 %collective-permute-start = (bf16[512,128]{1,0:T(8,128)(2,1)}, bf16[512,128]{1,0:T(8,128)(2,1)S(1)}, u32[]{:S(2)}, u32[]{:S(2)}) collective-permute-start(bf16[512,128]{1,0:T(8,128)(2,1)} %get-tuple-element.13.own_ref.strip_ref), channel_id=1, source_target_pairs={{0,512},{64,576},{128,640},{192,704},{256,768},{320,832},{384,896}... | collective-permute-start | bytes 393224 | tf_op jit(solution)/shard_map/ppermute | solution.py:134
  21.3 0.9 %copy-start.4 = (bf16[128,512]{1,0:T(8,128)(2,1)S(1)}, bf16[128,512]{1,0:T(8,128)(2,1)}, u32[]{:S(2)}) copy-start(bf16[128,512]{1,0:T(8,128)(2,1)} %get-tuple-element.10.rows_ref) | copy-start | bytes 393220
  30.9 21.7 %copy-start = (bf16[512,128]{1,0:T(8,128)(2,1)S(1)}, bf16[512,128]{1,0:T(8,128)(2,1)}, u32[]{:S(2)}) copy-start(bf16[512,128]{1,0:T(8,128)(2,1)} %get-tuple-element.13.own_ref.strip_ref) | copy-start | bytes 393220
  30.9 54.3 %all-to-all-start.1 = ((bf16[64,8,1152]{2,1,0:T(8,128)(2,1)}), bf16[64,8,1152]{2,1,0:T(8,128)(2,1)S(1)}, u32[]{:S(2)}, u32[]{:S(2)}) async-start(bf16[64,8,1152]{2,1,0:T(8,128)(2,1)} %share.1), calls=%async_computation.1 | async-start | bytes 2359296 | tf_op jit(solution)/shard_map/all_to_all | solution.py:277
  52.6 21.8 %copy-start.1 = (s32[8,16]{1,0:T(8,128)S(1)}, s32[8,16]{1,0:T(8,128)}, u32[]{:S(2)}) copy-start(s32[8,16]{1,0:T(8,128)} %pat_ref.1) | copy-start | bytes 1540
  52.6 15.1 %collective-permute-start.2 = (bf16[512,128]{1,0:T(8,128)(2,1)S(1)}, bf16[512,128]{1,0:T(8,128)(2,1)S(1)}, u32[]{:S(2)}, u32[]{:S(2)}) collective-permute-start(bf16[512,128]{1,0:T(8,128)(2,1)S(1)} %copy-done), channel_id=1, source_target_pairs={{0,768},{64,832},{128,896},{192,960},{256,0},{320,64},{384,128},{4... | collective-permute-start | bytes 393224 | tf_op jit(solution)/shard_map/ppermute | solution.py:134
  54.6 13.2 %collective-permute-start.3 = (bf16[512,128]{1,0:T(8,128)(2,1)S(1)}, bf16[512,128]{1,0:T(8,128)(2,1)S(1)}, u32[]{:S(2)}, u32[]{:S(2)}) collective-permute-start(bf16[512,128]{1,0:T(8,128)(2,1)S(1)} %copy-done), channel_id=1, source_target_pairs={{0,256},{64,320},{128,384},{192,448},{256,512},{320,576},{384,640}... | collective-permute-start | bytes 393224 | tf_op jit(solution)/shard_map/ppermute | solution.py:134
  60.6 10.6 %collective-permute-start.4 = (bf16[1024,128]{1,0:T(8,128)(2,1)S(1)}, bf16[1024,128]{1,0:T(8,128)(2,1)S(1)}, u32[]{:S(2)}, u32[]{:S(2)}) collective-permute-start(bf16[1024,128]{1,0:T(8,128)(2,1)S(1)} %pair.1), channel_id=1, source_target_pairs={{0,896},{64,960},{128,0},{192,64},{256,128},{320,192},{384,256},{4... | collective-permute-start | bytes 786440 | tf_op jit(solution)/shard_map/ppermute | solution.py:134
  62.6 9.8 %collective-permute-start.5 = (bf16[1024,128]{1,0:T(8,128)(2,1)S(1)}, bf16[1024,128]{1,0:T(8,128)(2,1)S(1)}, u32[]{:S(2)}, u32[]{:S(2)}) collective-permute-start(bf16[1024,128]{1,0:T(8,128)(2,1)S(1)} %pair.1), channel_id=1, source_target_pairs={{0,128},{64,192},{128,256},{192,320},{256,384},{320,448},{384,512}... | collective-permute-start | bytes 786440 | tf_op jit(solution)/shard_map/ppermute | solution.py:134
  72.4 12.7 %copy-start.2 = (s32[8]{0:T(128)S(1)}, s32[8]{0:T(128)}, u32[]{:S(2)}) copy-start(s32[8]{0:T(128)} %flag_ref.1) | copy-start | bytes 100
  72.5 12.7 %copy-start.3 = (s32[1,128]{1,0:T(1,128)S(1)}, s32[1,128]{1,0:T(1,128)}, u32[]{:S(2)}) copy-start(s32[1,128]{1,0:T(1,128)} %count_ref.1) | copy-start | bytes 1540
  72.5 4.6 %collective-permute-start.6 = (bf16[4096,128]{1,0:T(8,128)(2,1)S(1)}, bf16[4096,128]{1,0:T(8,128)(2,1)S(1)}, u32[]{:S(2)}, u32[]{:S(2)}) collective-permute-start(bf16[4096,128]{1,0:T(8,128)(2,1)S(1)} %constant_dynamic-update-slice_fusion.even_ref), channel_id=1, source_target_pairs={{0,64},{64,0},{128,192},{192,128},{256,320},{320,256},{384,448},{4... | collective-permute-start | bytes 3145736 | tf_op jit(solution)/shard_map/ppermute | solution.py:159

commit v12 on v11

--- a/solution.py
+++ b/solution.py
@@ -33,10 +33,12 @@
     return bits
 
 
-def pack_kernel(pat_hbm, dens_hbm, strip_ref, rows_ref, slots_ref, pat_ref, dens_ref, blocks, done):
+def pack_kernel(pat_hbm, dens_hbm, strip_ref, rows_ref, slots_ref, pat_ref, pat_vec, dens_ref, blocks, done):
     pat_copy = pltpu.make_async_copy(pat_hbm, pat_ref, done.at[0])
     dens_copy = pltpu.make_async_copy(dens_hbm, dens_ref, done.at[1])
+    vec_copy = pltpu.make_async_copy(pat_hbm, pat_vec, done.at[2])
     pat_copy.start()
+    vec_copy.start()
     dens_copy.start()
     row, col, depth = (lax.axis_index(name) for name in ("row", "col", "depth"))
     n_rows, names = pat_ref.shape
@@ -47,33 +49,20 @@
     first_col = col * n_cols
     start = pl.multiple_of(depth * width, width)
     which = lanes(BLOCK, width) // BLOCK
+    vec_copy.wait()
+    own = row * n_rows + lax.broadcasted_iota(jnp.int32, (n_rows, 1), 0)
+    kept = jnp.zeros((n_rows, 1), jnp.int32)
+    for j in range(width // BLOCK):
+        block = first_col + depth * (width // BLOCK) + j
+        hits = jnp.max(jnp.where(pat_vec[...] == block, 1, 0), axis=1, keepdims=True)
+        kept = kept + jnp.where((hits == 1) | (own == block), 1 << j, 0)
     pat_copy.wait()
-    kept = [block_bits(pat_ref, i, row * n_rows + i, first_col, n_cols) for i in range(n_rows)]
-    dens_copy.wait()
-    for i, bits in enumerate(kept):
-        keep = (lax.shift_right_logical(bits, depth * (width // BLOCK)) >> which) & 1
-        here = pl.ds(i * BLOCK, BLOCK)
-        value = dens_ref[here, pl.ds(start, width)].astype(F32)
-        strip_ref[here, :] = jnp.where(keep == 1, value, 0.0).astype(BF16)
     first_row = depth * (part // BLOCK)
-    begin = pl.multiple_of(depth * part, part)
-    which = lanes(BLOCK, tile) // BLOCK
-    blocks[n_cols] = jnp.zeros_like(blocks[n_cols])
-    for u in range(part // BLOCK):
-        i = first_row + u
-        bits = block_bits(pat_ref, i, row * n_rows + i, first_col, n_cols)
-        value = dens_ref[pl.ds(pl.multiple_of(begin + u * BLOCK, BLOCK), BLOCK), :].astype(F32)
-        value = jnp.where(((bits >> which) & 1) == 1, value, 0.0)
-        here = pl.ds(u * BLOCK, BLOCK)
-        rows_ref[here, :] = value.astype(BF16)
-        for j in range(n_cols):
-            one = value[:, j * BLOCK : (j + 1) * BLOCK]
-            blocks[j, here, :] = jnp.concatenate([one, one], axis=1)
-    left = lanes(BLOCK, 2 * BLOCK) < BLOCK
+    row_bits, row_places = [], []
     for u in range(part // BLOCK):
         i = first_row + u
         own_block = row * n_rows + i
-        here = pl.ds(u * BLOCK, BLOCK)
+        row_bits.append(block_bits(pat_ref, i, own_block, first_col, n_cols))
         places = []
         repeated = jnp.int32(0)
         for slot in range(names):
@@ -85,6 +74,28 @@
         inside = (local >= 0) & (local < n_cols) & (repeated == 0)
         places.append(jnp.where(inside, local, n_cols))
         places.append(jnp.int32(n_cols))
+        row_places.append(places)
+    dens_copy.wait()
+    for i in range(n_rows):
+        keep = (jnp.broadcast_to(kept[i : i + 1, :], (BLOCK, width)) >> which) & 1
+        here = pl.ds(i * BLOCK, BLOCK)
+        value = dens_ref[here, pl.ds(start, width)].astype(F32)
+        strip_ref[here, :] = jnp.where(keep == 1, value, 0.0).astype(BF16)
+    begin = pl.multiple_of(depth * part, part)
+    which = lanes(BLOCK, tile) // BLOCK
+    blocks[n_cols] = jnp.zeros_like(blocks[n_cols])
+    for u in range(part // BLOCK):
+        bits = row_bits[u]
+        value = dens_ref[pl.ds(pl.multiple_of(begin + u * BLOCK, BLOCK), BLOCK), :].astype(F32)
+        value = jnp.where(((bits >> which) & 1) == 1, value, 0.0)
+        here = pl.ds(u * BLOCK, BLOCK)
+        rows_ref[here, :] = value.astype(BF16)
+        for j in range(n_cols):
+            one = value[:, j * BLOCK : (j + 1) * BLOCK]
+            blocks[j, here, :] = jnp.concatenate([one, one], axis=1)
+    left = lanes(BLOCK, 2 * BLOCK) < BLOCK
+    for u, places in enumerate(row_places):
+        here = pl.ds(u * BLOCK, BLOCK)
         for pair in range(len(places) // 2):
             value = jnp.where(
                 left, blocks[places[2 * pair], here, :], blocks[places[2 * pair + 1], here, :]
@@ -244,9 +255,10 @@
         out_specs=(VMEM, VMEM, VMEM),
         scratch_shapes=[
             pltpu.SMEM(pattern.shape, jnp.int32),
+            pltpu.VMEM(pattern.shape, jnp.int32),
             pltpu.VMEM(density.shape, BF16),
             pltpu.VMEM((tile // BLOCK + 1, width, 2 * BLOCK), F32),
-            pltpu.SemaphoreType.DMA((2,)),
+            pltpu.SemaphoreType.DMA((3,)),
         ],
         compiler_params=pltpu.CompilerParams(vmem_limit_bytes=60 << 20),
         name="pack",

time: 87.9 us -> 87.7 us (level)
  no operation moved by 1% of the time
where the time goes in v12:
time: 87.7 us; the launch traced here: 87.1 us
  starting transfers between devices  57.1 us (65%)
  waiting for transfers between devices  22.4 us (26%)
  Pallas kernels  5.74 us (7%)
  local copies, waits for them, and re-layouts  1.05 us (1%)
    all_to_all x1, starting transfers between devices, per_device(): lax.all_to_all(send, ('depth', 'col'), 0, 0).reshape(tile, slots_wide)  21.7 us
    ppermute x5, starting transfers between devices, from_chip(): lax.ppermute(value, 'row', [(s, (s - 2 * distance) % n_row) for s in rang...  21 us
    all_to_all x1, waiting for transfers between devices, per_device(): lax.all_to_all(send, ('depth', 'col'), 0, 0).reshape(tile, slots_wide)  8.14 us
    all_to_all x1, waiting for transfers between devices, per_device(): parts = lax.all_to_all(slots.reshape(n_col, chunk, slots_wide), 'col', 0, 0)  7.26 us
    all_to_all x1, starting transfers between devices, per_device(): parts = lax.all_to_all(slots.reshape(n_col, chunk, slots_wide), 'col', 0, 0)  6.71 us
    ppermute x1, starting transfers between devices, per_device(): trans = lax.ppermute(strip, ('row', 'col'), swap)  5.77 us
    ppermute x5, waiting for transfers between devices, from_chip(): lax.ppermute(value, 'row', [(s, (s - 2 * distance) % n_row) for s in rang...  4.6 us
    ppermute x1, waiting for transfers between devices, gather_strip(): return (held, lax.ppermute(held, 'row', [(s, s ^ 1) for s in range(n_row)]))  2.44 us
  transfers between devices with their start and end apart: 9, of which 5 were waited for; matrix products, arithmetic and copies ran while one was open for 0% of the time, Pallas kernels for 2%

profile of v12, /device:TPU:6, one launch (start us, length us, event | category | flops | bytes accessed | tf_op | source)
XLA Modules:
  0.0 87.1 jit_solution(7007761429962343636)
XLA Ops:
  0.6 2.0 %pack.1 = (bf16[512,128]{1,0:T(8,128)(2,1)}, bf16[128,512]{1,0:T(8,128)(2,1)}, bf16[128,1152]{1,0:T(8,128)(2,1)}) custom-call(s32[8,16]{1,0:T(8,128)} %pat_ref.1, bf16[512,512]{1,0:T(8,128)(2,1)} %dens_hbm.1), custom_call_target="tpu_custom_call" | custom-call | tf_op jit(solution)/shard_map/pack/pallas_call | solution.py:247
  2.6 5.8 %collective-permute-start.1 = (bf16[512,128]{1,0:T(8,128)(2,1)}, bf16[512,128]{1,0:T(8,128)(2,1)S(1)}, u32[]{:S(2)}, u32[]{:S(2)}) collective-permute-start(bf16[512,128]{1,0:T(8,128)(2,1)} %get-tuple-element.13.own_ref.strip_ref), channel_id=1, source_target_pairs={{0,0},{4,64},{8,128},{12,192},{16,256},{20,320},{24,384},{28,448},... | collective-permute-start | bytes 393224 | tf_op jit(solution)/shard_map/ppermute | solution.py:267
  8.4 6.7 %all-to-all-start = ((bf16[16,8,1152]{2,1,0:T(8,128)(2,1)}), bf16[16,8,1152]{2,1,0:T(8,128)(2,1)S(1)}, u32[]{:S(2)}, u32[]{:S(2)}) async-start(bf16[16,8,1152]{2,1,0:T(8,128)(2,1)} %bitcast.4), calls=%async_computation | async-start | bytes 589824 | tf_op jit(solution)/shard_map/all_to_all | solution.py:269
  15.1 6.0 %collective-permute-start = (bf16[512,128]{1,0:T(8,128)(2,1)}, bf16[512,128]{1,0:T(8,128)(2,1)S(1)}, u32[]{:S(2)}, u32[]{:S(2)}) collective-permute-start(bf16[512,128]{1,0:T(8,128)(2,1)} %get-tuple-element.13.own_ref.strip_ref), channel_id=1, source_target_pairs={{0,512},{64,576},{128,640},{192,704},{256,768},{320,832},{384,896}... | collective-permute-start | bytes 393224 | tf_op jit(solution)/shard_map/ppermute | solution.py:145
  21.1 0.0 collective-permute-done.1.trans_ref
  21.1 0.0 copy-start.4
  21.2 0.9 %copy-done.4 = bf16[128,512]{1,0:T(8,128)(2,1)S(1)} copy-done((bf16[128,512]{1,0:T(8,128)(2,1)S(1)}, bf16[128,512]{1,0:T(8,128)(2,1)}, u32[]{:S(2)}) %copy-start.4) | copy-done | bytes 131096
  22.1 0.3 diagonal.1.terms_ref
  22.3 7.3 %all-to-all-done.parts_ref = bf16[16,8,1152]{2,1,0:T(8,128)(2,1)S(1)} async-done(((bf16[16,8,1152]{2,1,0:T(8,128)(2,1)}), bf16[16,8,1152]{2,1,0:T(8,128)(2,1)S(1)}, u32[]{:S(2)}, u32[]{:S(2)}) %all-to-all-start) | async-done | bytes 294944 | tf_op jit(solution)/shard_map/all_to_all | solution.py:269
  29.6 1.1 %share.1 = bf16[64,8,1152]{2,1,0:T(8,128)(2,1)} custom-call(f32[8,128]{1,0:T(8,128)S(1)} %diagonal.1.terms_ref, bf16[16,8,1152]{2,1,0:T(8,128)(2,1)S(1)} %all-to-all-done.parts_ref), custom_call_target="tpu_custom_call" | custom-call | tf_op jit(solution)/shard_map/share/pallas_call | solution.py:280
  30.7 21.7 %all-to-all-start.1 = ((bf16[64,8,1152]{2,1,0:T(8,128)(2,1)}), bf16[64,8,1152]{2,1,0:T(8,128)(2,1)S(1)}, u32[]{:S(2)}, u32[]{:S(2)}) async-start(bf16[64,8,1152]{2,1,0:T(8,128)(2,1)} %share.1), calls=%async_computation.1 | async-start | bytes 2359296 | tf_op jit(solution)/shard_map/all_to_all | solution.py:289
  52.4 0.0 collective-permute-done._.other_ref
  52.4 0.0 copy-done
  52.4 0.0 copy-start.1
  52.5 1.9 %collective-permute-start.2 = (bf16[512,128]{1,0:T(8,128)(2,1)S(1)}, bf16[512,128]{1,0:T(8,128)(2,1)S(1)}, u32[]{:S(2)}, u32[]{:S(2)}) collective-permute-start(bf16[512,128]{1,0:T(8,128)(2,1)S(1)} %copy-done), channel_id=1, source_target_pairs={{0,768},{64,832},{128,896},{192,960},{256,0},{320,64},{384,128},{4... | collective-permute-start | bytes 393224 | tf_op jit(solution)/shard_map/ppermute | solution.py:145
  54.4 6.0 %collective-permute-start.3 = (bf16[512,128]{1,0:T(8,128)(2,1)S(1)}, bf16[512,128]{1,0:T(8,128)(2,1)S(1)}, u32[]{:S(2)}, u32[]{:S(2)}) collective-permute-start(bf16[512,128]{1,0:T(8,128)(2,1)S(1)} %copy-done), channel_id=1, source_target_pairs={{0,256},{64,320},{128,384},{192,448},{256,512},{320,576},{384,640}... | collective-permute-start | bytes 393224 | tf_op jit(solution)/shard_map/ppermute | solution.py:145
  60.4 2.0 %collective-permute-start.4 = (bf16[1024,128]{1,0:T(8,128)(2,1)S(1)}, bf16[1024,128]{1,0:T(8,128)(2,1)S(1)}, u32[]{:S(2)}, u32[]{:S(2)}) collective-permute-start(bf16[1024,128]{1,0:T(8,128)(2,1)S(1)} %pair.1), channel_id=1, source_target_pairs={{0,896},{64,960},{128,0},{192,64},{256,128},{320,192},{384,256},{4... | collective-permute-start | bytes 786440 | tf_op jit(solution)/shard_map/ppermute | solution.py:145
  62.4 5.1 %collective-permute-start.5 = (bf16[1024,128]{1,0:T(8,128)(2,1)S(1)}, bf16[1024,128]{1,0:T(8,128)(2,1)S(1)}, u32[]{:S(2)}, u32[]{:S(2)}) collective-permute-start(bf16[1024,128]{1,0:T(8,128)(2,1)S(1)} %pair.1), channel_id=1, source_target_pairs={{0,128},{64,192},{128,256},{192,320},{256,384},{320,448},{384,512}... | collective-permute-start | bytes 786440 | tf_op jit(solution)/shard_map/ppermute | solution.py:145
  67.5 0.0 collective-permute-done.2
  67.6 0.0 collective-permute-done.3
  67.6 3.4 %collective-permute-done.4 = bf16[1024,128]{1,0:T(8,128)(2,1)S(1)} collective-permute-done((bf16[1024,128]{1,0:T(8,128)(2,1)S(1)}, bf16[1024,128]{1,0:T(8,128)(2,1)S(1)}, u32[]{:S(2)}, u32[]{:S(2)}) %collective-permute-start.4) | collective-permute-done | bytes 262176 | tf_op jit(solution)/shard_map/ppermute | solution.py:145
  71.1 1.2 %collective-permute-done.5 = bf16[1024,128]{1,0:T(8,128)(2,1)S(1)} collective-permute-done((bf16[1024,128]{1,0:T(8,128)(2,1)S(1)}, bf16[1024,128]{1,0:T(8,128)(2,1)S(1)}, u32[]{:S(2)}, u32[]{:S(2)}) %collective-permute-start.5) | collective-permute-done | bytes 262176 | tf_op jit(solution)/shard_map/ppermute | solution.py:145
  72.3 0.0 copy-start.2
  72.3 0.0 copy-start.3
  72.3 1.9 %collective-permute-start.6 = (bf16[4096,128]{1,0:T(8,128)(2,1)S(1)}, bf16[4096,128]{1,0:T(8,128)(2,1)S(1)}, u32[]{:S(2)}, u32[]{:S(2)}) collective-permute-start(bf16[4096,128]{1,0:T(8,128)(2,1)S(1)} %constant_dynamic-update-slice_fusion.even_ref), channel_id=1, source_target_pairs={{0,64},{64,0},{128,192},{192,128},{256,320},{320,256},{384,448},{4... | collective-permute-start | bytes 3145736 | tf_op jit(solution)/shard_map/ppermute | solution.py:170
  74.2 0.0 copy-done.1
  74.2 0.2 plan.1.plan_ref
  74.4 2.4 %collective-permute-done.6.odd_ref = bf16[4096,128]{1,0:T(8,128)(2,1)S(1)} collective-permute-done((bf16[4096,128]{1,0:T(8,128)(2,1)S(1)}, bf16[4096,128]{1,0:T(8,128)(2,1)S(1)}, u32[]{:S(2)}, u32[]{:S(2)}) %collective-permute-start.6) | collective-permute-done | bytes 1048608 | tf_op jit(solution)/shard_map/ppermute | solution.py:170
  76.8 8.1 %all-to-all-done.1 = bf16[64,8,1152]{2,1,0:T(8,128)(2,1)S(1)} async-done(((bf16[64,8,1152]{2,1,0:T(8,128)(2,1)}), bf16[64,8,1152]{2,1,0:T(8,128)(2,1)S(1)}, u32[]{:S(2)}, u32[]{:S(2)}) %all-to-all-start.1) | async-done | bytes 1179680 | tf_op jit(solution)/shard_map/all_to_all | solution.py:289
  85.0 0.0 copy-done.2
  85.0 0.0 copy-done.3
  85.0 2.1 %product.1 = (bf16[512,128]{1,0:T(8,128)(2,1)}, f32[1,128]{1,0:T(1,128)}) custom-call(s32[8,18]{1,0:T(8,128)S(1)} %plan.1.plan_ref, s32[8]{0:T(128)S(1)} %copy-done.2, s32[1,128]{1,0:T(1,128)S(1)} %copy-done.3, bf16[512,128]{1,0:T(8,128)(2,1)S(1)} %copy-done, bf16[512,1152]{1,0:T(8,128)(2,1)S(1)} %bitcast.3, ...), custom_call_target="tpu_custom_call" | custom-call | tf_op jit(solution)/shard_map/product/pallas_call | solution.py:299
  (7 shorter events, 0.2 us)
Async XLA Ops:
  2.6 18.5 %collective-permute-start.1 = (bf16[512,128]{1,0:T(8,128)(2,1)}, bf16[512,128]{1,0:T(8,128)(2,1)S(1)}, u32[]{:S(2)}, u32[]{:S(2)}) collective-permute-start(bf16[512,128]{1,0:T(8,128)(2,1)} %get-tuple-element.13.own_ref.strip_ref), channel_id=1, source_target_pairs={{0,0},{4,64},{8,128},{12,192},{16,256},{20,320},{24,384},{28,448},... | collective-permute-start | bytes 393224 | tf_op jit(solution)/shard_map/ppermute | solution.py:267
  8.4 21.2 %all-to-all-start = ((bf16[16,8,1152]{2,1,0:T(8,128)(2,1)}), bf16[16,8,1152]{2,1,0:T(8,128)(2,1)S(1)}, u32[]{:S(2)}, u32[]{:S(2)}) async-start(bf16[16,8,1152]{2,1,0:T(8,128)(2,1)} %bitcast.4), calls=%async_computation | async-start | bytes 589824 | tf_op jit(solution)/shard_map/all_to_all | solution.py:269
  15.1 37.3 %collective-permute-start = (bf16[512,128]{1,0:T(8,128)(2,1)}, bf16[512,128]{1,0:T(8,128)(2,1)S(1)}, u32[]{:S(2)}, u32[]{:S(2)}) collective-permute-start(bf16[512,128]{1,0:T(8,128)(2,1)} %get-tuple-element.13.own_ref.strip_ref), channel_id=1, source_target_pairs={{0,512},{64,576},{128,640},{192,704},{256,768},{320,832},{384,896}... | collective-permute-start | bytes 393224 | tf_op jit(solution)/shard_map/ppermute | solution.py:145
  21.1 0.9 %copy-start.4 = (bf16[128,512]{1,0:T(8,128)(2,1)S(1)}, bf16[128,512]{1,0:T(8,128)(2,1)}, u32[]{:S(2)}) copy-start(bf16[128,512]{1,0:T(8,128)(2,1)} %get-tuple-element.10.rows_ref) | copy-start | bytes 393220
  30.7 21.7 %copy-start = (bf16[512,128]{1,0:T(8,128)(2,1)S(1)}, bf16[512,128]{1,0:T(8,128)(2,1)}, u32[]{:S(2)}) copy-start(bf16[512,128]{1,0:T(8,128)(2,1)} %get-tuple-element.13.own_ref.strip_ref) | copy-start | bytes 393220
  30.7 54.3 %all-to-all-start.1 = ((bf16[64,8,1152]{2,1,0:T(8,128)(2,1)}), bf16[64,8,1152]{2,1,0:T(8,128)(2,1)S(1)}, u32[]{:S(2)}, u32[]{:S(2)}) async-start(bf16[64,8,1152]{2,1,0:T(8,128)(2,1)} %share.1), calls=%async_computation.1 | async-start | bytes 2359296 | tf_op jit(solution)/shard_map/all_to_all | solution.py:289
  52.4 21.8 %copy-start.1 = (s32[8,16]{1,0:T(8,128)S(1)}, s32[8,16]{1,0:T(8,128)}, u32[]{:S(2)}) copy-start(s32[8,16]{1,0:T(8,128)} %pat_ref.1) | copy-start | bytes 1540
  52.5 15.1 %collective-permute-start.2 = (bf16[512,128]{1,0:T(8,128)(2,1)S(1)}, bf16[512,128]{1,0:T(8,128)(2,1)S(1)}, u32[]{:S(2)}, u32[]{:S(2)}) collective-permute-start(bf16[512,128]{1,0:T(8,128)(2,1)S(1)} %copy-done), channel_id=1, source_target_pairs={{0,768},{64,832},{128,896},{192,960},{256,0},{320,64},{384,128},{4... | collective-permute-start | bytes 393224 | tf_op jit(solution)/shard_map/ppermute | solution.py:145
  54.4 13.2 %collective-permute-start.3 = (bf16[512,128]{1,0:T(8,128)(2,1)S(1)}, bf16[512,128]{1,0:T(8,128)(2,1)S(1)}, u32[]{:S(2)}, u32[]{:S(2)}) collective-permute-start(bf16[512,128]{1,0:T(8,128)(2,1)S(1)} %copy-done), channel_id=1, source_target_pairs={{0,256},{64,320},{128,384},{192,448},{256,512},{320,576},{384,640}... | collective-permute-start | bytes 393224 | tf_op jit(solution)/shard_map/ppermute | solution.py:145
  60.4 10.6 %collective-permute-start.4 = (bf16[1024,128]{1,0:T(8,128)(2,1)S(1)}, bf16[1024,128]{1,0:T(8,128)(2,1)S(1)}, u32[]{:S(2)}, u32[]{:S(2)}) collective-permute-start(bf16[1024,128]{1,0:T(8,128)(2,1)S(1)} %pair.1), channel_id=1, source_target_pairs={{0,896},{64,960},{128,0},{192,64},{256,128},{320,192},{384,256},{4... | collective-permute-start | bytes 786440 | tf_op jit(solution)/shard_map/ppermute | solution.py:145
  62.4 9.8 %collective-permute-start.5 = (bf16[1024,128]{1,0:T(8,128)(2,1)S(1)}, bf16[1024,128]{1,0:T(8,128)(2,1)S(1)}, u32[]{:S(2)}, u32[]{:S(2)}) collective-permute-start(bf16[1024,128]{1,0:T(8,128)(2,1)S(1)} %pair.1), channel_id=1, source_target_pairs={{0,128},{64,192},{128,256},{192,320},{256,384},{320,448},{384,512}... | collective-permute-start | bytes 786440 | tf_op jit(solution)/shard_map/ppermute | solution.py:145
  72.3 12.7 %copy-start.2 = (s32[8]{0:T(128)S(1)}, s32[8]{0:T(128)}, u32[]{:S(2)}) copy-start(s32[8]{0:T(128)} %flag_ref.1) | copy-start | bytes 100
  72.3 12.7 %copy-start.3 = (s32[1,128]{1,0:T(1,128)S(1)}, s32[1,128]{1,0:T(1,128)}, u32[]{:S(2)}) copy-start(s32[1,128]{1,0:T(1,128)} %count_ref.1) | copy-start | bytes 1540
  72.3 4.6 %collective-permute-start.6 = (bf16[4096,128]{1,0:T(8,128)(2,1)S(1)}, bf16[4096,128]{1,0:T(8,128)(2,1)S(1)}, u32[]{:S(2)}, u32[]{:S(2)}) collective-permute-start(bf16[4096,128]{1,0:T(8,128)(2,1)S(1)} %constant_dynamic-update-slice_fusion.even_ref), channel_id=1, source_target_pairs={{0,64},{64,0},{128,192},{192,128},{256,320},{320,256},{384,448},{4... | collective-permute-start | bytes 3145736 | tf_op jit(solution)/shard_map/ppermute | solution.py:170
